TPU v7x, 32 devices: a whole 2x2x4 slice. The times are simulated.
32 devices in a mesh: fsdp: 8 (over y, x, core), seq: 4 (over z).
Axes of the slice: x: 2, y: 2, z: 4, core: 2. Of those that a mesh axis runs over, the one named last changes fastest.
Arguments:
- hidden: bfloat16 [4096, 5120], P(('fsdp', 'seq')), may hold values from -7 to 7
- destination: int32 [4096], P(('fsdp', 'seq')), may hold values from 0 to 4095, as said below
- segment_ids: int32 [8, 512], P('fsdp'), may hold values from 0 to 7, never falling along the last dimension, each value on 1 to 256 neighbouring positions
- cotangent: bfloat16 [4096, 5120], P('fsdp', 'seq'), may hold values from -6 to 6
- w_query: bfloat16 [5120, 5120], P('fsdp', 'seq'), may hold values from -0.078125 to 0.078125
- key_weight: bfloat16 [5120, 1024], P('fsdp', 'seq'), may hold values from -0.078125 to 0.078125
- value_weight: bfloat16 [5120, 1024], P('fsdp', 'seq'), may hold values from -0.078125 to 0.078125
Outputs:
- attn_out: bfloat16 [4096, 5120], P('fsdp', 'seq')
- grad_query: float32 [5120, 5120], P('fsdp', 'seq')
- grad_key: float32 [5120, 1024], P('fsdp', 'seq')
- grad_value: float32 [5120, 1024], P('fsdp', 'seq')
Inputs may be any that keep to these rules, and one draw needn't show every extreme that they name: destination is a permutation of the 4096 packed positions (pack * 512 + position in the pack); with packed rows laid 128 to a device in order, the 128 rows of one device go to exactly 16 devices, 8 rows to each.
All inputs are finite; a program needn't handle non-finite values.
Results may differ from a plain program's by a relative error of at most 0.025.
The roundings to bfloat16 on the way count: a program that leaves them out, or rounds other values in their place, can miss the bound.
Values may be sent and summed in bfloat16 or wider, within the bound.
No kernel may reach another device: no remote copies, remote signals or barrier semaphores. Data moves between devices by JAX's collectives and lax.ppermute only.
A program may use at most 128 MiB of HBM per device.

v0:
```python
import math

import jax
import jax.numpy as jnp
from jax import lax
from jax.sharding import PartitionSpec as P

HEAD_DIMENSION = 128


def attend_heads(query, keys, values, segments, cotangent, head_size):
    length = query.shape[0]
    heads = query.shape[1] // head_size
    groups = heads // (keys.shape[1] // head_size)
    scale = 1.0 / math.sqrt(head_size)
    order = jnp.arange(length, dtype=jnp.int32)
    allowed = (segments[:, None] == segments[None, :]) & (order[None, :] <= order[:, None])

    def one_head(index, carry):
        out_all, dq_all, dk_sum, dv_sum = carry
        start = index * head_size
        kv_start = index // groups * head_size
        q_h = lax.dynamic_slice_in_dim(query, start, head_size, 1)
        k_h = lax.dynamic_slice_in_dim(keys, kv_start, head_size, 1)
        v_h = lax.dynamic_slice_in_dim(values, kv_start, head_size, 1)
        d_h = lax.dynamic_slice_in_dim(cotangent, start, head_size, 1)
        scores = jnp.dot(q_h, k_h.T, preferred_element_type=jnp.float32) * scale
        scores = jnp.where(allowed, scores, -1e30)
        top = jnp.max(scores, axis=1, keepdims=True)
        weights = jnp.exp(scores - top)
        probs = weights / jnp.sum(weights, axis=1, keepdims=True)
        probs_b = probs.astype(jnp.bfloat16)
        out_h = jnp.dot(probs_b, v_h, preferred_element_type=jnp.float32).astype(jnp.bfloat16)
        delta = jnp.sum(d_h.astype(jnp.float32) * out_h.astype(jnp.float32), axis=1, keepdims=True)
        dv_h = jnp.dot(probs_b.T, d_h, preferred_element_type=jnp.float32)
        dprob = jnp.dot(d_h, v_h.T, preferred_element_type=jnp.float32)
        dscore = (probs * (dprob - delta)).astype(jnp.bfloat16)
        dq_h = (jnp.dot(dscore, k_h, preferred_element_type=jnp.float32) * scale).astype(
            jnp.bfloat16
        )
        dk_h = jnp.dot(dscore.T, q_h, preferred_element_type=jnp.float32)
        out_all = lax.dynamic_update_slice_in_dim(out_all, out_h, start, 1)
        dq_all = lax.dynamic_update_slice_in_dim(dq_all, dq_h, start, 1)
        dk_old = lax.dynamic_slice_in_dim(dk_sum, kv_start, head_size, 1)
        dk_sum = lax.dynamic_update_slice_in_dim(dk_sum, dk_old + dk_h, kv_start, 1)
        dv_old = lax.dynamic_slice_in_dim(dv_sum, kv_start, head_size, 1)
        dv_sum = lax.dynamic_update_slice_in_dim(dv_sum, dv_old + dv_h, kv_start, 1)
        return (out_all, dq_all, dk_sum, dv_sum)

    initial_carry = (
        jnp.zeros(query.shape, jnp.bfloat16),
        jnp.zeros(query.shape, jnp.bfloat16),
        jnp.zeros(keys.shape, jnp.float32),
        jnp.zeros(keys.shape, jnp.float32),
    )
    out_all, dq_all, dk_sum, dv_sum = lax.fori_loop(0, heads, one_head, initial_carry)
    return (out_all, dq_all, (dk_sum * scale).astype(jnp.bfloat16), dv_sum.astype(jnp.bfloat16))


def on_device(hidden, destination, segment_ids, cotangent, w_query, key_weight, value_weight):
    tok_rows, width = hidden.shape
    n_fsdp = lax.axis_size("fsdp")
    n_seq = lax.axis_size("seq")
    n_dev = n_fsdp * n_seq
    capacity = max(2, 2 * tok_rows // n_dev)
    target = destination // tok_rows
    slot = destination % tok_rows
    order = jnp.arange(tok_rows, dtype=jnp.int32)
    earlier = (target[:, None] == target[None, :]) & (order[None, :] < order[:, None])
    rank = jnp.sum(earlier.astype(jnp.int32), axis=1)
    where_to = target * capacity + rank
    outgoing = jnp.zeros((n_dev * capacity, width), hidden.dtype).at[where_to].set(hidden)
    slot_out = jnp.full((n_dev * capacity,), -1, jnp.int32).at[where_to].set(slot)
    arrived, arrived_slot = (
        lax.all_to_all(
            outgoing.reshape(n_dev, capacity, width),
            ("fsdp", "seq"),
            split_axis=0,
            concat_axis=0,
            tiled=True,
        ),
        lax.all_to_all(
            slot_out.reshape(n_dev, capacity),
            ("fsdp", "seq"),
            split_axis=0,
            concat_axis=0,
            tiled=True,
        ),
    )
    slot_in = arrived_slot.reshape(-1)
    slot_in = jnp.where(slot_in >= 0, slot_in, tok_rows)
    placed = (
        jnp.zeros((tok_rows, width), jnp.bfloat16)
        .at[slot_in]
        .set(arrived.reshape(-1, width), mode="drop")
    )
    cols_q = w_query.shape[1]
    cols_k = key_weight.shape[1]
    packed = lax.all_gather(placed, "seq", axis=0, tiled=True)
    part = packed
    query_sum = jnp.dot(
        part,
        lax.all_gather(w_query, "fsdp", axis=0, tiled=True),
        preferred_element_type=jnp.float32,
    )
    key_sum = jnp.dot(
        part,
        lax.all_gather(key_weight, "fsdp", axis=0, tiled=True),
        preferred_element_type=jnp.float32,
    )
    value_sum = jnp.dot(
        part,
        lax.all_gather(value_weight, "fsdp", axis=0, tiled=True),
        preferred_element_type=jnp.float32,
    )
    query = query_sum.astype(jnp.bfloat16)
    keys = key_sum.astype(jnp.bfloat16)
    values = value_sum.astype(jnp.bfloat16)
    attn_out, d_query, d_key, d_value = attend_heads(
        query, keys, values, segment_ids[0], cotangent, HEAD_DIMENSION
    )
    joined_grad = jnp.concatenate([d_query, d_key, d_value], axis=1)
    part = packed
    grads = lax.psum_scatter(
        lax.dot_general(
            part, joined_grad, (((0,), (0,)), ((), ())), preferred_element_type=jnp.float32
        ),
        "fsdp",
        scatter_dimension=0,
        tiled=True,
    )
    return (
        attn_out,
        grads[:, :cols_q],
        grads[:, cols_q : cols_q + cols_k],
        grads[:, cols_q + cols_k :],
    )


def solution(mesh):
    placed = (
        P(("fsdp", "seq"), None),
        P(("fsdp", "seq")),
        P("fsdp", None),
        P("fsdp", "seq"),
        P("fsdp", "seq"),
        P("fsdp", "seq"),
        P("fsdp", "seq"),
    )
    return jax.shard_map(
        on_device,
        mesh=mesh,
        in_specs=placed,
        out_specs=(P("fsdp", "seq"), P("fsdp", "seq"), P("fsdp", "seq"), P("fsdp", "seq")),
        check_vma=False,
    )
```

profile of v0, /device:TPU:0, one launch (start us, length us, event | category | flops | bytes accessed | tf_op | source)
XLA Modules:
  0.0 630.3 jit_solution(8425248926572323351)
XLA Ops:
  9.7 7.3 %all-to-all-start = ((s32[32,1,8]{2,1,0:T(1,128)}), s32[32,1,8]{2,1,0:T(1,128)S(1)}, u32[]{:S(2)}, u32[]{:S(2)}) async-start(s32[32,1,8]{2,1,0:T(1,128)} %bitcast), calls=%async_computation | async-start | bytes 32768 | tf_op jit(solution)/shard_map/all_to_all | solution.py:82
  17.0 5.0 scatter_custom_fusion.1
  22.0 2.1 all-to-all-done
  24.1 3.7 all-to-all-start.1
  29.9 56.8 %all-to-all-done.1 = bf16[32,8,5120]{2,1,0:T(8,128)(2,1)S(1)} async-done(((bf16[32,8,5120]{2,1,0:T(8,128)(2,1)}), bf16[32,8,5120]{2,1,0:T(8,128)(2,1)S(1)}, u32[]{:S(2)}, u32[]{:S(2)}) %all-to-all-start.1) | async-done | bytes 2621472 | tf_op jit(solution)/shard_map/all_to_all | solution.py:75
  86.8 5.1 scatter_custom_fusion.2
  93.3 96.7 %all-gather.5.cloned.1.call-done = bf16[512,5120]{1,0:T(8,128)(2,1)} async-done(((bf16[128,5120]{1,0:T(8,128)(2,1)}), bf16[512,5120]{1,0:T(8,128)(2,1)}) %all-gather.5.cloned.1.call-update) | async-done | bytes 5242896 | tf_op jit(solution)/shard_map/all_gather | solution.py:99
  190.0 4.8 convolution_convert_fusion.2
  194.8 25.6 %all-gather.9.cloned.1.call-done = bf16[5120,256]{1,0:T(8,128)(2,1)} async-done(((bf16[640,256]{1,0:T(8,128)(2,1)}), bf16[5120,256]{1,0:T(8,128)(2,1)}) %all-gather.9.cloned.1.call-update) | async-done | bytes 2621456 | tf_op jit(solution)/shard_map/all_gather | solution.py:108
  220.4 4.8 convolution_convert_fusion.3
  225.2 71.3 %all-gather.7.cloned.1.call-done = bf16[5120,1280]{1,0:T(8,128)(2,1)} async-done(((bf16[640,1280]{1,0:T(8,128)(2,1)}), bf16[5120,1280]{1,0:T(8,128)(2,1)}) %all-gather.7.cloned.1.call-update) | async-done | bytes 13107216 | tf_op jit(solution)/shard_map/all_gather | solution.py:103
  296.5 13.5 %convolution_convert_fusion.1 = bf16[512,1280]{1,0:T(8,128)(2,1)} fusion(bf16[512,5120]{1,0:T(8,128)(2,1)} %all-gather.5.cloned.1.call-done, bf16[5120,1280]{1,0:T(8,128)(2,1)} %all-gather.7.cloned.1.call-done), kind=kOutput, calls=%fused_computation.37 | convolution fusion | flops 6711541760 | bytes 19660800 | tf_op jit(solution)/shard_map/dot_general | solution.py:101
  312.4 66.2 %while.22 = (s32[]{:T(128)}, bf16[512,1280]{1,0:T(8,128)(2,1)}, bf16[512,1280]{1,0:T(8,128)(2,1)}, f32[512,256]{1,0:T(8,128)S(1)}, f32[512,256]{1,0:T(8,128)S(1)...) while((s32[]{:T(128)}, bf16[512,1280]{1,0:T(8,128)(2,1)}, ...), condition=%wide.region_8.9_spmd.clone, body=%wide.region_4.8_spmd.clone.sunk | while | flops 407435776 | bytes 10901883 | solution.py:56
  313.4 1.3 fusion.79
  316.1 1.2 fusion.84
  320.1 1.3 fusion.79
  322.7 1.2 fusion.84
  326.7 1.3 fusion.79
  329.4 1.2 fusion.84
  333.3 1.3 fusion.79
  336.0 1.2 fusion.84
  339.9 1.3 fusion.79
  342.6 1.2 fusion.84
  346.5 1.3 fusion.79
  353.2 1.3 fusion.79
  359.8 1.3 fusion.79
  366.4 1.3 fusion.79
  373.0 1.3 fusion.79
  378.7 18.8 %fusion.26 = f32[5120,1792]{1,0:T(8,128)} fusion(bf16[512,5120]{1,0:T(8,128)(2,1)} %all-gather.5.cloned.1.call-done, bf16[512,256]{1,0:T(8,128)(2,1)S(1)} %convert_element_type.83, bf16[512,256]{1,0:T(8,128)(2,1)S(1)} %multiply_convert_fusion, bf16[512,1280]{1,0:T(8,128)(2,1)} %get-tuple-element.251), kind=kOutput, calls=%fused_computation.40 | convolution fusion | flops 9400745984 | bytes 43778048 | tf_op jit(solution)/shard_map/dot_general | solution.py:125
  397.6 220.0 %reduce-scatter.2.cloned.1.call-done = f32[640,1792]{1,0:T(8,128)} async-done(((f32[5120,1792]{1,0:T(8,128)}), f32[640,1792]{1,0:T(8,128)}) %reduce-scatter.2.cloned.1.call-update) | async-done | bytes 4587536 | tf_op jit(solution)/shard_map/reduce_scatter | solution.py:124
  617.5 2.4 fusion.40
  620.0 3.8 slice.12
  (133 shorter events, 55.5 us)
Async XLA Ops:
  9.7 14.4 %all-to-all-start = ((s32[32,1,8]{2,1,0:T(1,128)}), s32[32,1,8]{2,1,0:T(1,128)S(1)}, u32[]{:S(2)}, u32[]{:S(2)}) async-start(s32[32,1,8]{2,1,0:T(1,128)} %bitcast), calls=%async_computation | async-start | bytes 32768 | tf_op jit(solution)/shard_map/all_to_all | solution.py:82
  24.1 62.7 %all-to-all-start.1 = ((bf16[32,8,5120]{2,1,0:T(8,128)(2,1)}), bf16[32,8,5120]{2,1,0:T(8,128)(2,1)S(1)}, u32[]{:S(2)}, u32[]{:S(2)}) async-start(bf16[32,8,5120]{2,1,0:T(8,128)(2,1)} %bitcast.2), calls=%async_computation.1 | async-start | bytes 5242880 | tf_op jit(solution)/shard_map/all_to_all | solution.py:75
  27.9 65.4 %all-gather.11.cloned.1.call-start = ((), (), s32[]{:S(2)}) async-start(), calls=%async_computation.6 | async-start | bytes 2949120 | tf_op jit(solution)/shard_map/all_gather | solution.py:113
  28.6 161.4 %all-gather.5.cloned.1.call-start = ((), (), s32[]{:S(2)}) async-start(), calls=%async_computation.3 | async-start | bytes 6553600 | tf_op jit(solution)/shard_map/all_gather | solution.py:99
  91.9 128.6 %all-gather.9.cloned.1.call-start = ((), (), s32[]{:S(2)}) async-start(), calls=%async_computation.5 | async-start | bytes 2949120 | tf_op jit(solution)/shard_map/all_gather | solution.py:108
  92.6 203.9 %all-gather.7.cloned.1.call-start = ((), (), s32[]{:S(2)}) async-start(), calls=%async_computation.4 | async-start | bytes 14745600 | tf_op jit(solution)/shard_map/all_gather | solution.py:103
  93.2 524.4 %reduce-scatter.2.cloned.1.call-start = ((), (), s32[]{:S(2)}) async-start(), calls=%async_computation.7 | async-start | bytes 41287680 | tf_op jit(solution)/shard_map/reduce_scatter | solution.py:124
  310.0 2.4 copy-start
Sparse Core Ops, SparseCore 0:
  30.6 44.7 all-gather.10
  92.0 97.9 all-gather.4
  191.9 28.4 all-gather.8
  222.2 74.3 all-gather.6
  397.7 219.7 reduce-scatter.1
where the time goes:
time: 631 us; the launch traced here: 630 us
  waiting for transfers between devices  474 us (75%)
  matrix products  86 us (14%)
  local copies, waits for them, and re-layouts  39.1 us (6%)
  between operations  13.9 us (2%)
  starting transfers between devices  11.2 us (2%)
    reduce_scatter x1, waiting for transfers between devices, on_device(): lax.psum_scatter(lax.dot_general(part, joined_grad, (((0,), (0,)), ((), (...  220 us
    all_gather x1, waiting for transfers between devices, on_device(): packed = lax.all_gather(placed, 'seq', axis=0, tiled=True)  96.7 us
    all_gather x1, waiting for transfers between devices, on_device(): lax.all_gather(w_query, 'fsdp', axis=0, tiled=True)  71.3 us
    all_to_all x1, waiting for transfers between devices, on_device(): lax.all_to_all(outgoing.reshape(n_dev, capacity, width), ('fsdp', 'seq'),...  56.8 us
    all_gather x1, waiting for transfers between devices, on_device(): lax.all_gather(key_weight, 'fsdp', axis=0, tiled=True)  25.6 us
    dot_general x1, matrix products, on_device(): lax.dot_general(part, joined_grad, (((0,), (0,)), ((), ())), preferred_el...  18.8 us
    dot_general x1, matrix products, on_device(): jnp.dot(part, lax.all_gather(w_query, 'fsdp', axis=0, tiled=True), prefer...  13.5 us
  transfers between devices with their start and end apart: 7, of which 6 were waited for; matrix products, arithmetic and copies ran while one was open for 3% of the time, Pallas kernels for 0%

commit v1 on v0

v1 whole, which is shorter than its diff:
```python
import functools
import math

import jax
import jax.numpy as jnp
from jax import lax
from jax.experimental import pallas as pl
from jax.experimental.pallas import tpu as pltpu
from jax.sharding import PartitionSpec as P

HEAD_DIMENSION = 128
VMEM_LIMIT = 56 * 1024 * 1024
ANY = pl.BlockSpec(memory_space=pl.ANY)
SMEM = pl.BlockSpec(memory_space=pltpu.SMEM)
VMEM = pl.BlockSpec(memory_space=pltpu.VMEM)


def swap(x, axis, bit):
    n = lax.axis_size(axis)
    return lax.ppermute(x, axis, [(i, i ^ bit) for i in range(n)])


def after(x, *others):
    return lax.optimization_barrier((x, *others))[0] if others else x


def together(*groups):
    flat = lax.optimization_barrier(tuple(x for group in groups for x in group))
    out, at = [], 0
    for group in groups:
        out.append(list(flat[at : at + len(group)]))
        at += len(group)
    return out


def spread(chunk, bits):
    have = {0: chunk}
    for bit in bits:
        for m in sorted(have):
            have[m ^ bit] = swap(have[m], "fsdp", bit)
    return [have[m] for m in range(len(have))]


def axis_bits(n):
    return [1 << i for i in range(1, n.bit_length() - 1)]


def gather_step(x, axis, bit):
    other = swap(x, axis, bit)
    mine_first = (lax.axis_index(axis) & bit) == 0
    return jnp.where(mine_first, jnp.concatenate([x, other]), jnp.concatenate([other, x]))


def line_step(up, down):
    n = lax.axis_size("seq")
    return (
        lax.ppermute(up, "seq", [(i, i + 1) for i in range(n - 1)]),
        lax.ppermute(down, "seq", [(i + 1, i) for i in range(n - 1)]),
    )


def line_gather(x):
    up, down = [x], [x]
    for _ in range(1, lax.axis_size("seq")):
        u, d = line_step(up[-1], down[-1])
        up.append(u)
        down.append(d)
    return up[1:], down[1:]


def gather_all(blocks, rows, short):
    n_fsdp, n_seq = lax.axis_size("fsdp"), lax.axis_size("seq")
    high = axis_bits(n_fsdp)
    short = short[None]
    if len(high) != 2 or n_seq != 4 or len(blocks) != 2:
        weights = [spread(block, high + [1]) for block in blocks]
        up, down = line_gather(rows)
        bit = 1
        while bit < n_seq:
            short = gather_step(short, "seq", bit)
            bit *= 2
        short = short[None]
        bit = 1
        while bit < n_fsdp:
            short = gather_step(short, "fsdp", bit)
            bit *= 2
        return weights, up, down, short, short[lax.axis_index("fsdp")]
    x, y = high
    p, q = blocks
    p_x, q_y = swap(p, "fsdp", x), swap(q, "fsdp", y)
    up1, down1 = line_step(rows, rows)
    short1 = gather_step(short, "seq", 1)
    (p, q, p_x, q_y, up1, down1, short1), = together((p, q, p_x, q_y, up1, down1, short1))
    p_y, q_x = swap(p, "fsdp", y), swap(q, "fsdp", x)
    up2, down2 = line_step(up1, down1)
    short2 = gather_step(short1, "seq", 2)
    p_c, q_c = swap(p, "fsdp", 1), swap(q, "fsdp", 1)
    p_xc, q_yc = swap(p_x, "fsdp", 1), swap(q_y, "fsdp", 1)
    (p_x, q_y, p_y, q_x, up2, down2, short2, p_c, q_c, p_xc, q_yc), = together(
        (p_x, q_y, p_y, q_x, up2, down2, short2, p_c, q_c, p_xc, q_yc)
    )
    p_xy, q_xy = swap(p_x, "fsdp", y), swap(q_y, "fsdp", x)
    up3, down3 = line_step(up2, down2)
    p_yc, q_xc = swap(p_y, "fsdp", 1), swap(q_x, "fsdp", 1)
    short3 = gather_step(short2[None], "fsdp", 1)
    (p_xy, q_xy, up3, down3, p_yc, q_xc, short3), = together(
        (p_xy, q_xy, up3, down3, p_yc, q_xc, short3)
    )
    p_xyc, q_xyc = swap(p_xy, "fsdp", 1), swap(q_xy, "fsdp", 1)
    short4 = gather_step(gather_step(short3, "fsdp", x), "fsdp", y)
    weights = [
        [p, p_c, p_x, p_xc, p_y, p_yc, p_xy, p_xyc],
        [q, q_c, q_x, q_xc, q_y, q_yc, q_xy, q_xyc],
    ]
    return weights, [up1, up2, up3], [down1, down2, down3], short4, short2


def gather_plane(block):
    n = lax.axis_size("fsdp")
    high = axis_bits(n)
    if len(high) != 2:
        return [[(0, part)] for part in spread(block, high + [1])]
    x, y = high
    half = block.shape[0] // 2
    from_x, from_y = swap(block, "fsdp", x), swap(block, "fsdp", y)
    top, bottom = swap(from_x[:half], "fsdp", y), swap(from_y[half:], "fsdp", x)
    whole = [(0, block)], [(0, from_x)], [(0, from_y)], [(0, top), (half, bottom)]
    out = []
    for parts in whole:
        out.append(parts)
        out.append([(at, swap(part, "fsdp", 1)) for at, part in parts])
    return out


def line_pick(x, up, down):
    n = lax.axis_size("seq")
    z = lax.axis_index("seq")
    return [x] + [jnp.where(z + k < n, down[k - 1], up[n - k - 1]) for k in range(1, n)]


def project_kernel(n_seq, n_fsdp, cap, me_ref, slot_ref, *refs):
    own = refs[0]
    up = refs[1:n_seq]
    down = refs[n_seq : 2 * n_seq - 1]
    chunks = refs[2 * n_seq - 1 : 2 * n_seq - 1 + n_fsdp]
    out_ref, a_v, w_v, acc, sem_a, sem_w = refs[2 * n_seq - 1 + n_fsdp :]
    me, z = me_ref[0], me_ref[1]
    tok = own.shape[0]
    depth = chunks[0].shape[0]
    in_w = []
    for m in range(n_fsdp):
        start = pl.multiple_of((me ^ m) * depth, depth)
        in_w.append(pltpu.make_async_copy(chunks[m], w_v.at[pl.ds(start, depth)], sem_w.at[m]))
    in_rows = [pltpu.make_async_copy(own, a_v.at[pl.ds(0, tok)], sem_a.at[0])]
    in_rows[0].start()
    for k in range(1, n_seq):
        spot = a_v.at[pl.ds(k * tok, tok)]
        below = pltpu.make_async_copy(up[n_seq - k - 1], spot, sem_a.at[k])
        above = pltpu.make_async_copy(down[k - 1], spot, sem_a.at[k])
        pl.when(z + k < n_seq)(above.start)
        pl.when(z + k >= n_seq)(below.start)
        in_rows.append(above)
    for copy in in_w:
        copy.start()
    for copy in in_rows:
        copy.wait()
    for j in range(n_fsdp // 2):
        in_w[2 * j].wait()
        in_w[2 * j + 1].wait()
        start = pl.multiple_of(((me >> 1) ^ j) * (2 * depth), 2 * depth)
        part = jnp.dot(
            a_v[:, pl.ds(start, 2 * depth)],
            w_v[pl.ds(start, 2 * depth), :],
            preferred_element_type=jnp.float32,
        )
        if j == 0:
            acc[...] = part
        else:
            acc[...] += part
    qkv = acc[...].astype(jnp.bfloat16)
    slot = slot_ref[...]
    order = lax.broadcasted_iota(jnp.int32, (n_fsdp * cap, slot.shape[1]), 0)
    pick = (slot == order).astype(jnp.bfloat16)
    out_ref[...] = jnp.dot(pick, qkv, preferred_element_type=jnp.float32).astype(jnp.bfloat16)


def project(place, slot, own, up, down, chunks, cap):
    n_seq, n_fsdp = len(up) + 1, len(chunks)
    tok, width = own.shape
    cols = chunks[0].shape[1]
    length = n_seq * tok
    return pl.pallas_call(
        functools.partial(project_kernel, n_seq, n_fsdp, cap),
        out_shape=jax.ShapeDtypeStruct((n_fsdp * cap, cols), jnp.bfloat16),
        in_specs=[SMEM, VMEM] + [ANY] * (2 * n_seq - 1 + n_fsdp),
        out_specs=VMEM,
        scratch_shapes=[
            pltpu.VMEM((length, width), jnp.bfloat16),
            pltpu.VMEM((width, cols), jnp.bfloat16),
            pltpu.VMEM((length, cols), jnp.float32),
            pltpu.SemaphoreType.DMA((n_seq,)),
            pltpu.SemaphoreType.DMA((n_fsdp,)),
        ],
        compiler_params=pltpu.CompilerParams(vmem_limit_bytes=VMEM_LIMIT),
        cost_estimate=pl.CostEstimate(
            flops=2 * length * width * cols + 2 * n_fsdp * cap * length * cols,
            bytes_accessed=2 * (length * width + width * cols + n_fsdp * cap * cols),
            transcendentals=0,
        ),
        name="project",
    )(place, slot, own, *up, *down, *chunks)


def attend_kernel(heads, block, place_ref, seg_row, seg_col, cot_ref, in_ref, *refs):
    out_ref, grad_ref, qkv, bias, dk_sum, dv_sum = refs
    size = HEAD_DIMENSION
    length = qkv.shape[0]
    scale = 1.0 / math.sqrt(size)
    key_pos = lax.broadcasted_iota(jnp.int32, (length, length), 0)
    query_pos = lax.broadcasted_iota(jnp.int32, (length, length), 1)
    allowed = (seg_col[...] == seg_row[...]) & (key_pos <= query_pos)
    bias[...] = jnp.where(allowed, 0.0, -1e30)
    spots = lax.broadcasted_iota(jnp.int32, (length, in_ref.shape[0]), 0)
    pick = (spots == place_ref[...]).astype(jnp.bfloat16)
    qkv[...] = jnp.dot(pick, in_ref[...], preferred_element_type=jnp.float32).astype(jnp.bfloat16)
    keys = qkv[:, heads * size : (heads + 1) * size]
    values = qkv[:, (heads + 1) * size : (heads + 2) * size]
    keys_t = keys.T
    values_t = values.T
    dk_sum[...] = jnp.zeros_like(dk_sum)
    dv_sum[...] = jnp.zeros_like(dv_sum)
    for h in range(heads):
        q_h = qkv[:, h * size : (h + 1) * size]
        d_h = cot_ref[:, h * size : (h + 1) * size]
        q_t = q_h.T
        d_t = d_h.T
        for start in range(0, length, block):
            stop = start + block
            scores = jnp.dot(keys[:stop], q_t[:, start:stop], preferred_element_type=jnp.float32)
            scores = scores + bias[:stop, start:stop]
            top = jnp.max(scores, axis=0, keepdims=True)
            weights = jnp.exp2((scores - top) * (scale * math.log2(math.e)))
            probs = weights * (1.0 / jnp.sum(weights, axis=0, keepdims=True))
            probs_b = probs.astype(jnp.bfloat16)
            out_t = jnp.dot(values_t[:, :stop], probs_b, preferred_element_type=jnp.float32).astype(
                jnp.bfloat16
            )
            delta = jnp.sum(
                d_t[:, start:stop].astype(jnp.float32) * out_t.astype(jnp.float32), axis=0, keepdims=True
            )
            dprob = jnp.dot(values[:stop], d_t[:, start:stop], preferred_element_type=jnp.float32)
            dscore = (probs * (dprob - delta)).astype(jnp.bfloat16)
            dq_t = (
                jnp.dot(keys_t[:, :stop], dscore, preferred_element_type=jnp.float32) * scale
            ).astype(jnp.bfloat16)
            dk_sum[:stop] += jnp.dot(dscore, q_h[start:stop], preferred_element_type=jnp.float32)
            dv_sum[:stop] += jnp.dot(probs_b, d_h[start:stop], preferred_element_type=jnp.float32)
            out_ref[start:stop, h * size : (h + 1) * size] = out_t.T
            grad_ref[start:stop, h * size : (h + 1) * size] = dq_t.T
    grad_ref[:, heads * size : (heads + 1) * size] = (dk_sum[...] * scale).astype(jnp.bfloat16)
    grad_ref[:, (heads + 1) * size : (heads + 2) * size] = dv_sum[...].astype(jnp.bfloat16)


def attend(place, segments, cotangent, group, arrived):
    slots, cols = arrived.shape
    size = HEAD_DIMENSION
    heads = cols // size - 2
    length = cotangent.shape[0]
    return pl.pallas_call(
        functools.partial(attend_kernel, heads, 256),
        grid=(1,),
        out_shape=[
            jax.ShapeDtypeStruct((length, heads * size), jnp.bfloat16),
            jax.ShapeDtypeStruct((length, cols), jnp.bfloat16),
        ],
        in_specs=[VMEM, VMEM, VMEM, pl.BlockSpec((length, heads * size), lambda i: (0, group)), VMEM],
        out_specs=[VMEM, VMEM],
        scratch_shapes=[
            pltpu.VMEM((length, cols), jnp.bfloat16),
            pltpu.VMEM((length, length), jnp.float32),
            pltpu.VMEM((length, size), jnp.float32),
            pltpu.VMEM((length, size), jnp.float32),
        ],
        compiler_params=pltpu.CompilerParams(vmem_limit_bytes=VMEM_LIMIT),
        cost_estimate=pl.CostEstimate(
            flops=12 * heads * length * length * size + 2 * length * slots * cols,
            bytes_accessed=2 * (slots * cols + 3 * length * cols),
            transcendentals=heads * length * length,
        ),
        name="attend",
    )(place, segments[None, :], segments[:, None], cotangent, arrived)


def pack_kernel(count, length, has_before, *refs):
    rows, spots = refs[:count], refs[count : 2 * count]
    out_ref = refs[-1]
    base = pl.program_id(0) * length
    order = lax.broadcasted_iota(jnp.int32, (rows[0].shape[1], length), 1) + base
    total = refs[2 * count][...].astype(jnp.float32) if has_before else None
    for k in range(count):
        pick = (order == spots[k][...]).astype(jnp.bfloat16)
        part = jnp.dot(rows[k][...], pick, preferred_element_type=jnp.float32)
        total = part if total is None else total + part
    out_ref[...] = total.astype(jnp.bfloat16)


def pack_columns(rows, spots, tokens, length, before):
    count = len(rows)
    cols, each = rows[0].shape
    extra = [] if before is None else [before]
    block = pl.BlockSpec((cols, length), lambda i: (0, i))
    return pl.pallas_call(
        functools.partial(pack_kernel, count, length, before is not None),
        grid=(tokens // length,),
        out_shape=jax.ShapeDtypeStruct((cols, tokens), jnp.bfloat16),
        in_specs=[pl.BlockSpec((cols, each), lambda i: (0, 0))] * count
        + [pl.BlockSpec((each, 1), lambda i: (0, 0))] * count
        + [block] * len(extra),
        out_specs=block,
        compiler_params=pltpu.CompilerParams(vmem_limit_bytes=VMEM_LIMIT),
        cost_estimate=pl.CostEstimate(
            flops=2 * tokens * each * count * cols,
            bytes_accessed=4 * tokens * cols,
            transcendentals=0,
        ),
        name="pack_columns",
    )(*rows, *spots, *extra)


def grads_kernel(layout, group, aliased, me_ref, packed_ref, *refs):
    count = sum(len(parts) for parts in layout)
    gq_ref, gk_ref, gv_ref, d_v, acc, sem, sem_o = refs[count + (3 if aliased else 0) :]
    me = me_ref[0]
    length = packed_ref.shape[1] // len(layout)
    cols = d_v.shape[1]
    size = HEAD_DIMENSION
    copies = []
    at = 0
    for m, parts in enumerate(layout):
        copies.append([])
        for offset, rows in parts:
            start = pl.multiple_of((me ^ m) * length + offset, rows)
            copies[m].append(
                pltpu.make_async_copy(refs[at], d_v.at[pl.ds(start, rows)], sem.at[at])
            )
            copies[m][-1].start()
            at += 1
    for j in range(len(layout) // 2):
        for copy in copies[2 * j] + copies[2 * j + 1]:
            copy.wait()
        start = pl.multiple_of(((me >> 1) ^ j) * (2 * length), 2 * length)
        part = jnp.dot(
            packed_ref[:, pl.ds(start, 2 * length)],
            d_v[pl.ds(start, 2 * length), :],
            preferred_element_type=jnp.float32,
        )
        if j == 0:
            acc[...] = part
        else:
            acc[...] += part
    q_cols = cols - 2 * size
    outs = (
        pltpu.make_async_copy(
            acc.at[:, pl.ds(0, q_cols)], gq_ref.at[:, pl.ds(group * q_cols, q_cols)], sem_o.at[0]
        ),
        pltpu.make_async_copy(
            acc.at[:, pl.ds(q_cols, size)], gk_ref.at[:, pl.ds(group * size, size)], sem_o.at[1]
        ),
        pltpu.make_async_copy(
            acc.at[:, pl.ds(q_cols + size, size)], gv_ref.at[:, pl.ds(group * size, size)], sem_o.at[2]
        ),
    )
    for copy in outs:
        copy.start()
    for copy in outs:
        copy.wait()


def gradients(place, packed, chunks, group, groups, before):
    layout = [[(at, part.shape[0]) for at, part in parts] for parts in chunks]
    pieces = [part for parts in chunks for _, part in parts]
    width, tokens = packed.shape
    cols = pieces[0].shape[1]
    size = HEAD_DIMENSION
    shapes = [
        jax.ShapeDtypeStruct((width, groups * (cols - 2 * size)), jnp.float32),
        jax.ShapeDtypeStruct((width, groups * size), jnp.float32),
        jax.ShapeDtypeStruct((width, groups * size), jnp.float32),
    ]
    extra = [] if before is None else list(before)
    return pl.pallas_call(
        functools.partial(grads_kernel, layout, group, before is not None),
        out_shape=shapes,
        in_specs=[SMEM, VMEM] + [ANY] * (len(pieces) + len(extra)),
        out_specs=[ANY] * 3,
        input_output_aliases={2 + len(pieces) + i: i for i in range(len(extra))},
        scratch_shapes=[
            pltpu.VMEM((tokens, cols), jnp.bfloat16),
            pltpu.VMEM((width, cols), jnp.float32),
            pltpu.SemaphoreType.DMA((len(pieces),)),
            pltpu.SemaphoreType.DMA((3,)),
        ],
        compiler_params=pltpu.CompilerParams(vmem_limit_bytes=VMEM_LIMIT),
        cost_estimate=pl.CostEstimate(
            flops=2 * tokens * width * cols,
            bytes_accessed=2 * tokens * (width + cols) + 4 * width * cols,
            transcendentals=0,
        ),
        name="gradients",
    )(place, packed, *pieces, *extra)


def on_device(hidden, destination, segment_ids, cotangent, w_query, key_weight, value_weight):
    tok_rows, width = hidden.shape
    n_fsdp = lax.axis_size("fsdp")
    n_seq = lax.axis_size("seq")
    length = n_seq * tok_rows
    size = HEAD_DIMENSION
    groups = key_weight.shape[1] // size
    q_cols = w_query.shape[1] // groups
    cap = n_seq * n_seq * (2 * tok_rows // (n_fsdp * n_seq))
    f = lax.axis_index("fsdp")
    z = lax.axis_index("seq")
    here = jnp.stack([f, z]).astype(jnp.int32)

    blocks = [
        jnp.concatenate(
            [
                w_query[:, g * q_cols : (g + 1) * q_cols],
                key_weight[:, g * size : (g + 1) * size],
                value_weight[:, g * size : (g + 1) * size],
            ],
            axis=1,
        )
        for g in range(groups)
    ]
    weights, up, down, dest, mine = gather_all(blocks, hidden, destination)

    mine = mine.reshape(length)
    target = mine // length
    order = jnp.arange(length, dtype=jnp.int32)
    earlier = (target[:, None] == target[None, :]) & (order[:, None] < order[None, :])
    rank = jnp.sum(earlier.astype(jnp.int32), axis=0)
    slot = (target * cap + rank).reshape(n_seq, tok_rows)
    slot = lax.dynamic_slice_in_dim(jnp.concatenate([slot, slot], 0), z, n_seq, 0).reshape(1, length)
    blocks = dest.reshape(n_fsdp, length)
    coming = (blocks // length) == f
    before = (order[:, None] < order[None, :]).astype(jnp.bfloat16)
    rank_in = jnp.dot(coming.astype(jnp.bfloat16), before, preferred_element_type=jnp.float32)
    rank_in = rank_in.astype(jnp.int32)
    nth = jnp.arange(cap, dtype=jnp.int32)
    hit = coming[:, None, :] & (rank_in[:, None, :] == nth[None, :, None])
    place = jnp.sum(jnp.where(hit, (blocks % length + 1)[:, None, :], 0), axis=2) - 1
    place = place.reshape(1, n_fsdp * cap)

    columns = lax.all_to_all(
        after(hidden, weights[-1][-2]), "fsdp", split_axis=1, concat_axis=0, tiled=True
    ).T
    c_up, c_down = line_gather(columns)
    columns = line_pick(columns, c_up, c_down)
    twice = jnp.concatenate([dest, dest], axis=1)
    spots = [
        lax.dynamic_index_in_dim(twice, z + k, 1, keepdims=False).reshape(n_fsdp * tok_rows, 1)
        for k in range(n_seq)
    ]
    half = n_seq // 2
    tokens = n_fsdp * length

    arrived = []
    for g in range(groups):
        slots = project(here, slot, hidden, up, down, weights[g], cap)
        arrived.append(lax.all_to_all(slots, "fsdp", split_axis=0, concat_axis=0, tiled=True))

    packed = pack_columns(columns[:half], spots[:half], tokens, length, None)
    arrived[-1] = after(arrived[-1], packed)
    outs, d_chunks = [], []
    for g in range(groups):
        out_g, grad_g = attend(place, segment_ids[0], cotangent, g, arrived[g])
        outs.append(out_g)
        d_chunks.append(gather_plane(grad_g))
    packed = pack_columns(columns[half:], spots[half:], tokens, length, packed)
    grads = None
    for g in range(groups):
        grads = gradients(here, packed, d_chunks[g], g, groups, grads)
    attn_out = jnp.concatenate(outs, axis=1) if groups > 1 else outs[0]
    return (attn_out, *grads)


def solution(mesh):
    placed = (
        P(("fsdp", "seq"), None),
        P(("fsdp", "seq")),
        P("fsdp", None),
        P("fsdp", "seq"),
        P("fsdp", "seq"),
        P("fsdp", "seq"),
        P("fsdp", "seq"),
    )
    return jax.shard_map(
        on_device,
        mesh=mesh,
        in_specs=placed,
        out_specs=(P("fsdp", "seq"), P("fsdp", "seq"), P("fsdp", "seq"), P("fsdp", "seq")),
        check_vma=False,
    )
```

time: 631 us -> 368 us (0.58); the launches traced: 630 us -> 361 us
  waiting for transfers between devices: 474 us -> 131 us
  Pallas kernels: 0 us -> 106 us
  matrix products: 86 us -> 0.18 us
  starting transfers between devices: 11.2 us -> 70.7 us
  blocking collectives: 0 us -> 21.7 us
  local copies, waits for them, and re-layouts: 39.1 us -> 19.7 us
  between operations: 13.9 us -> 1.64 us
    reduce_scatter x1 -> x0, waiting for transfers between devices: 220 us -> none  [on_device(): lax.psum_scatter(lax.dot_general(part, joined_grad, (((0,), (0,)), ((), (...]
    all_gather x4 -> x0, waiting for transfers between devices: 194 us -> none  [the longest x1 96.7 us: on_device(): packed = lax.all_gather(placed, 'seq', axis=0, tiled=True)]
    ppermute x0 -> x49, waiting for transfers between devices: none -> 131 us  [the longest x37 104 us: swap(): return lax.ppermute(x, axis, [(i, i ^ bit) for i in range(n)])]
    pallas_call x0 -> x8, Pallas kernels: none -> 106 us  [the longest x2 32.1 us: pack_columns(): pl.pallas_call(functools.partial(pack_kernel, count, length, before is no...]
    dot_general x64 -> x1, matrix products: 86 us -> 0.18 us  [on_device(): jnp.dot(coming.astype(jnp.bfloat16), before, preferred_element_type=jnp.f...]
    ppermute x0 -> x49, starting transfers between devices: none -> 62.8 us  [the longest x37 27.4 us: swap(): return lax.ppermute(x, axis, [(i, i ^ bit) for i in range(n)])]
    all_to_all x2, waiting for transfers between devices: 58.9 us -> 0.01 us  [on_device(): lax.all_to_all(slots, 'fsdp', split_axis=0, concat_axis=0, tiled=True)]
    all_to_all x0 -> x1, blocking collectives: none -> 21.7 us  [on_device(): lax.all_to_all(after(hidden, weights[-1][-2]), 'fsdp', split_axis=1, conc...]
  transfers between devices with their start and end apart: 7 -> 51, of which waited for: 6 -> 13; matrix products, arithmetic and copies ran while one was open for 3% -> 6% of each run, Pallas kernels for 0% -> 26%
where the time goes in v1:
time: 368 us; the launch traced here: 361 us
  waiting for transfers between devices  131 us (36%)
  Pallas kernels  106 us (29%)
  starting transfers between devices  70.7 us (19%)
  blocking collectives  21.7 us (6%)
  local copies, waits for them, and re-layouts  19.7 us (5%)
  other arithmetic  10.8 us (3%)
    ppermute x37, waiting for transfers between devices, swap(): return lax.ppermute(x, axis, [(i, i ^ bit) for i in range(n)])  104 us
    pallas_call x2, Pallas kernels, pack_columns(): pl.pallas_call(functools.partial(pack_kernel, count, length, before is no...  32.1 us
    ppermute x37, starting transfers between devices, swap(): return lax.ppermute(x, axis, [(i, i ^ bit) for i in range(n)])  27.4 us
    ppermute x6, starting transfers between devices, line_step(): lax.ppermute(up, 'seq', [(i, i + 1) for i in range(n - 1)])  27.3 us
    pallas_call x2, Pallas kernels, project(): pl.pallas_call(functools.partial(project_kernel, n_seq, n_fsdp, cap), out...  26.7 us
    ppermute x6, waiting for transfers between devices, line_step(): lax.ppermute(up, 'seq', [(i, i + 1) for i in range(n - 1)])  24 us
    pallas_call x2, Pallas kernels, attend(): pl.pallas_call(functools.partial(attend_kernel, heads, 256), grid=(1,), o...  23.6 us
    pallas_call x2, Pallas kernels, gradients(): pl.pallas_call(functools.partial(grads_kernel, layout, group, before is n...  23.1 us
  transfers between devices with their start and end apart: 51, of which 13 were waited for; matrix products, arithmetic and copies ran while one was open for 6% of the time, Pallas kernels for 26%

profile of v1, /device:TPU:0, one launch (start us, length us, event | category | flops | bytes accessed | tf_op | source)
XLA Modules:
  0.0 360.9 jit_solution(3405901269317807942)
XLA Ops:
  2.1 6.6 %collective-permute-start.2 = (bf16[128,5120]{1,0:T(8,128)(2,1)}, bf16[128,5120]{1,0:T(8,128)(2,1)}, u32[]{:S(2)}, u32[]{:S(2)}) collective-permute-start(bf16[128,5120]{1,0:T(8,128)(2,1)} %refs_0_.3), channel_id=1, source_target_pairs={{0,1},{1,2},{2,3},{4,5},{5,6},{6,7},{8,9},{9,10},{10,11},{12,13},{... | collective-permute-start | bytes 3932168 | tf_op jit(solution)/shard_map/ppermute | solution.py:57
  11.5 1.9 collective-permute-start
  15.7 20.3 %collective-permute-done.4 = s32[1,128]{1,0:T(1,128)S(1)} collective-permute-done((s32[1,128]{1,0:T(1,128)S(1)}, s32[1,128]{1,0:T(1,128)S(1)}, u32[]{:S(2)}, u32[]{:S(2)}) %collective-permute-start.4) | collective-permute-done | bytes 544 | tf_op jit(solution)/shard_map/ppermute | solution.py:20
  36.0 2.5 collective-permute-done.refs_9_
  40.5 2.6 collective-permute-start.9
  43.1 2.9 collective-permute-start.7
  52.4 22.3 %collective-permute-done.5.refs_11_ = bf16[640,896]{1,0:T(8,128)(2,1)} collective-permute-done((bf16[640,896]{1,0:T(8,128)(2,1)}, bf16[640,896]{1,0:T(8,128)(2,1)}, u32[]{:S(2)}, u32[]{:S(2)}) %collective-permute-start.5) | collective-permute-done | bytes 1146912 | tf_op jit(solution)/shard_map/ppermute | solution.py:20
  74.7 3.1 collective-permute-done.6.refs_9_
  80.3 3.5 collective-permute-start.16
  86.9 18.4 %collective-permute-done.14.refs_13_ = bf16[640,896]{1,0:T(8,128)(2,1)} collective-permute-done((bf16[640,896]{1,0:T(8,128)(2,1)}, bf16[640,896]{1,0:T(8,128)(2,1)}, u32[]{:S(2)}, u32[]{:S(2)}) %collective-permute-start.14) | collective-permute-done | bytes 1146912 | tf_op jit(solution)/shard_map/ppermute | solution.py:20
  105.3 7.9 %collective-permute-done.15.refs_13_ = bf16[640,896]{1,0:T(8,128)(2,1)} collective-permute-done((bf16[640,896]{1,0:T(8,128)(2,1)}, bf16[640,896]{1,0:T(8,128)(2,1)}, u32[]{:S(2)}, u32[]{:S(2)}) %collective-permute-start.15) | collective-permute-done | bytes 1146912 | tf_op jit(solution)/shard_map/ppermute | solution.py:20
  115.5 21.7 %all_to_all.42 = bf16[128,8,640]{0,2,1:T(8,128)(2,1)S(1)} all-to-all(bf16[128,8,640]{0,2,1:T(8,128)(2,1)S(1)} %bitcast.59), channel_id=1, replica_groups=mesh['fsdp'=8,'seq'=4] {'fsdp'}, dimensions={1} | all-to-all | bytes 2621440 | tf_op jit(solution)/shard_map/all_to_all | solution.py:456
  138.4 3.1 collective-permute-start.26
  144.8 2.3 collective-permute-done.21
  148.4 20.8 %collective-permute-done.26 = bf16[640,1024]{1,0:T(8,128)(2,1)S(1)} collective-permute-done((bf16[640,1024]{1,0:T(8,128)(2,1)}, bf16[640,1024]{1,0:T(8,128)(2,1)S(1)}, u32[]{:S(2)}, u32[]{:S(2)}) %collective-permute-start.26) | collective-permute-done | bytes 1310752 | tf_op jit(solution)/shard_map/ppermute | solution.py:57
  169.2 5.4 %collective-permute-start.27 = (bf16[640,1024]{1,0:T(8,128)(2,1)S(1)}, bf16[640,1024]{1,0:T(8,128)(2,1)}, u32[]{:S(2)}, u32[]{:S(2)}) collective-permute-start(bf16[640,1024]{1,0:T(8,128)(2,1)S(1)} %collective-permute-done.26), channel_id=1, source_target_pairs={{0,1},{1,2},{2,3},{4,5},{5,6},{6,7},{8,9},{9,10},{10,11},{12,13},{... | collective-permute-start | bytes 3932168 | tf_op jit(solution)/shard_map/ppermute | solution.py:57
  176.1 13.4 %project.2 = bf16[1024,896]{1,0:T(8,128)(2,1)} custom-call(s32[2]{0:T(128)} %pad_add_fusion.1.me_ref, s32[1,512]{1,0:T(1,128)} %bitcast.75, bf16[128,5120]{1,0:T(8,128)(2,1)} %refs_0_.3, bf16[128,5120]{1,0:T(8,128)(2,1)} %collective-permute-done.2.refs_1_, bf16[128,5120]{1,0:T(8,128)(2,1)} %collective-permute-done.7.refs_2_, ...), custom_call_target="tpu_custom_call" | custom-call | flops 5637144576 | bytes 16252928 | tf_op jit(solution)/shard_map/project/pallas_call | solution.py:192
  189.5 3.6 all-to-all-start
  196.8 3.2 collective-permute-done.27
  200.0 5.8 %collective-permute-start.28 = (bf16[640,1024]{1,0:T(8,128)(2,1)}, bf16[640,1024]{1,0:T(8,128)(2,1)}, u32[]{:S(2)}, u32[]{:S(2)}) collective-permute-start(bf16[640,1024]{1,0:T(8,128)(2,1)} %collective-permute-done.27), channel_id=1, source_target_pairs={{0,1},{1,2},{2,3},{4,5},{5,6},{6,7},{8,9},{9,10},{10,11},{12,13},{... | collective-permute-start | bytes 3932168 | tf_op jit(solution)/shard_map/ppermute | solution.py:57
  206.9 13.4 %project.3 = bf16[1024,896]{1,0:T(8,128)(2,1)} custom-call(s32[2]{0:T(128)} %pad_add_fusion.1.me_ref, s32[1,512]{1,0:T(1,128)} %bitcast.76, bf16[128,5120]{1,0:T(8,128)(2,1)} %refs_0_.3, bf16[128,5120]{1,0:T(8,128)(2,1)} %collective-permute-done.2.refs_1_, bf16[128,5120]{1,0:T(8,128)(2,1)} %collective-permute-done.7.refs_2_, ...), custom_call_target="tpu_custom_call" | custom-call | flops 5637144576 | bytes 16252928 | tf_op jit(solution)/shard_map/project/pallas_call | solution.py:192
  221.6 4.3 %all-to-all-start.1 = ((bf16[8,128,896]{2,1,0:T(8,128)(2,1)}), bf16[8,128,896]{2,1,0:T(8,128)(2,1)}, u32[]{:S(2)}, u32[]{:S(2)}) async-start(bf16[8,128,896]{2,1,0:T(8,128)(2,1)} %bitcast.62), calls=%async_computation.1 | async-start | bytes 3670016 | tf_op jit(solution)/shard_map/all_to_all | solution.py:472
  225.9 11.8 %attend.2 = (bf16[512,640]{1,0:T(8,128)(2,1)}, bf16[512,896]{1,0:T(8,128)(2,1)}) custom-call(s32[1,1024]{1,0:T(1,128)} %bitcast.72, s32[1,512]{1,0:T(1,128)} %seg_row.3, s32[512,1]{1,0:T(8,128)} %copy.30.seg_col, bf16[512,1280]{1,0:T(8,128)(2,1)} %cot_ref.3, bf16[1024,896]{1,0:T(8,128)(2,1)} %bitcast.60), custom_call_target="tpu_custom_call" | custom-call | flops 2952790016 | bytes 4587520 | tf_op jit(solution)/shard_map/attend/pallas_call | solution.py:269
  242.6 2.6 broadcast_select_fusion.2.refs_1_
  245.2 15.8 %pack_columns.2.refs_4_ = bf16[640,4096]{1,0:T(8,128)(2,1)} custom-call(bf16[640,1024]{1,0:T(8,128)(2,1)} %bitcast_bitcast_fusion.refs_0_, bf16[640,1024]{1,0:T(8,128)(2,1)} %broadcast_select_fusion.2.refs_1_, s32[1024,1]{1,0:T(8,128)} %copy.33.refs_2_, s32[1024,1]{1,0:T(8,128)} %copy.34.refs_3_), custom_call_target="tpu_custom_call" | custom-call | flops 10737418240 | bytes 10485760 | tf_op jit(solution)/shard_map/pack_columns/pallas_call | solution.py:312
  261.0 11.8 %attend.3 = (bf16[512,640]{1,0:T(8,128)(2,1)}, bf16[512,896]{1,0:T(8,128)(2,1)}) custom-call(s32[1,1024]{1,0:T(1,128)} %bitcast.73, s32[1,512]{1,0:T(1,128)} %seg_row.3, s32[512,1]{1,0:T(8,128)} %copy.30.seg_col, bf16[512,1280]{1,0:T(8,128)(2,1)} %cot_ref.3, bf16[1024,896]{1,0:T(8,128)(2,1)} %bitcast.12.in_ref), custom_call_target="tpu_custom_call" | custom-call | flops 2952790016 | bytes 4587520 | tf_op jit(solution)/shard_map/attend/pallas_call | solution.py:269
  274.6 2.1 collective-permute-start.46
  279.1 25.9 %collective-permute-done.46.refs_7_ = bf16[256,896]{1,0:T(8,128)(2,1)} collective-permute-done((bf16[256,896]{1,0:T(8,128)(2,1)S(1)}, bf16[256,896]{1,0:T(8,128)(2,1)}, u32[]{:S(2)}, u32[]{:S(2)}) %collective-permute-start.46) | collective-permute-done | bytes 458784 | tf_op jit(solution)/shard_map/ppermute | solution.py:20
  308.3 2.5 broadcast_select_fusion.1.refs_0_
  317.3 16.3 %pack_columns.3.packed_ref = bf16[640,4096]{1,0:T(8,128)(2,1)} custom-call(bf16[640,1024]{1,0:T(8,128)(2,1)} %broadcast_select_fusion.1.refs_0_, bf16[640,1024]{1,0:T(8,128)(2,1)} %broadcast_select_fusion.refs_1_, s32[1024,1]{1,0:T(8,128)} %copy.36.refs_2_, s32[1024,1]{1,0:T(8,128)} %copy.37.refs_3_, bf16[640,4096]{1,0:T(8,128)(2,1)} %pack_columns.2.refs_4_), custom_call_target="tpu_custom_call" | custom-call | flops 10737418240 | bytes 10485760 | tf_op jit(solution)/shard_map/pack_columns/pallas_call | solution.py:312
  335.4 11.5 %gradients.2 = (f32[640,1280]{1,0:T(8,128)}, f32[640,256]{1,0:T(8,128)}, f32[640,256]{1,0:T(8,128)}) custom-call(s32[2]{0:T(128)} %pad_add_fusion.1.me_ref, bf16[640,4096]{1,0:T(8,128)(2,1)} %pack_columns.3.packed_ref, bf16[512,896]{1,0:T(8,128)(2,1)} %get-tuple-element.71.refs_0_, bf16[512,896]{1,0:T(8,128)(2,1)} %collective-permute-done.40.refs_1_, ...), custom_call_target="tpu_custom_call" | custom-call | flops 4697620480 | bytes 14876672 | tf_op jit(solution)/shard_map/gradients/pallas_call | solution.py:391
  348.9 11.5 %gradients.3 = (f32[640,1280]{1,0:T(8,128)}, f32[640,256]{1,0:T(8,128)}, f32[640,256]{1,0:T(8,128)}) custom-call(s32[2]{0:T(128)} %pad_add_fusion.1.me_ref, bf16[640,4096]{1,0:T(8,128)(2,1)} %pack_columns.3.packed_ref, bf16[512,896]{1,0:T(8,128)(2,1)} %get-tuple-element.70.refs_0_, ...), custom_call_target="tpu_custom_call", output_to_operand_aliasing={{0}: (12, {}), {1}: (13, {}), {2}: (14, {})} | custom-call | flops 4697620480 | bytes 14876672 | tf_op jit(solution)/shard_map/gradients/pallas_call | solution.py:391
  (163 shorter events, 58.3 us)
Async XLA Ops:
  0.7 39.2 %collective-permute-start.3 = (bf16[128,5120]{1,0:T(8,128)(2,1)}, bf16[128,5120]{1,0:T(8,128)(2,1)}, u32[]{:S(2)}, u32[]{:S(2)}) collective-permute-start(bf16[128,5120]{1,0:T(8,128)(2,1)} %refs_0_.3), channel_id=1, source_target_pairs={{1,0},{2,1},{3,2},{5,4},{6,5},{7,6},{9,8},{10,9},{11,10},{13,12},{... | collective-permute-start | bytes 3932168 | tf_op jit(solution)/shard_map/ppermute | solution.py:58
  2.1 37.8 %collective-permute-start.2 = (bf16[128,5120]{1,0:T(8,128)(2,1)}, bf16[128,5120]{1,0:T(8,128)(2,1)}, u32[]{:S(2)}, u32[]{:S(2)}) collective-permute-start(bf16[128,5120]{1,0:T(8,128)(2,1)} %refs_0_.3), channel_id=1, source_target_pairs={{0,1},{1,2},{2,3},{4,5},{5,6},{6,7},{8,9},{9,10},{10,11},{12,13},{... | collective-permute-start | bytes 3932168 | tf_op jit(solution)/shard_map/ppermute | solution.py:57
  11.5 27.0 %collective-permute-start = (bf16[640,896]{1,0:T(8,128)(2,1)}, bf16[640,896]{1,0:T(8,128)(2,1)}, u32[]{:S(2)}, u32[]{:S(2)}) collective-permute-start(bf16[640,896]{1,0:T(8,128)(2,1)} %pad_maximum_fusion.1.refs_7_), channel_id=1, source_target_pairs={{0,8},{4,12},{8,0},{12,4},{16,24},{20,28},{24,16},{28,20},{1,9},{5... | collective-permute-start | bytes 3440648 | tf_op jit(solution)/shard_map/ppermute | solution.py:20
  13.6 26.3 %collective-permute-start.1 = (bf16[640,896]{1,0:T(8,128)(2,1)S(1)}, bf16[640,896]{1,0:T(8,128)(2,1)}, u32[]{:S(2)}, u32[]{:S(2)}) collective-permute-start(bf16[640,896]{1,0:T(8,128)(2,1)S(1)} %pad_maximum_fusion.2.refs_7_), channel_id=1, source_target_pairs={{0,16},{4,20},{8,24},{12,28},{16,0},{20,4},{24,8},{28,12},{1,17},{... | collective-permute-start | bytes 3440648 | tf_op jit(solution)/shard_map/ppermute | solution.py:20
  43.1 34.7 %collective-permute-start.7 = (bf16[128,5120]{1,0:T(8,128)(2,1)}, bf16[128,5120]{1,0:T(8,128)(2,1)}, u32[]{:S(2)}, u32[]{:S(2)}) collective-permute-start(bf16[128,5120]{1,0:T(8,128)(2,1)} %collective-permute-done.2.refs_1_), channel_id=1, source_target_pairs={{0,1},{1,2},{2,3},{4,5},{5,6},{6,7},{8,9},{9,10},{10,11},{12,13},{... | collective-permute-start | bytes 3932168 | tf_op jit(solution)/shard_map/ppermute | solution.py:57
  46.0 32.8 %collective-permute-start.8 = (bf16[128,5120]{1,0:T(8,128)(2,1)}, bf16[128,5120]{1,0:T(8,128)(2,1)}, u32[]{:S(2)}, u32[]{:S(2)}) collective-permute-start(bf16[128,5120]{1,0:T(8,128)(2,1)} %collective-permute-done.3.refs_4_), channel_id=1, source_target_pairs={{1,0},{2,1},{3,2},{5,4},{6,5},{7,6},{9,8},{10,9},{11,10},{13,12},{... | collective-permute-start | bytes 3932168 | tf_op jit(solution)/shard_map/ppermute | solution.py:58
  47.3 27.4 %collective-permute-start.5 = (bf16[640,896]{1,0:T(8,128)(2,1)}, bf16[640,896]{1,0:T(8,128)(2,1)}, u32[]{:S(2)}, u32[]{:S(2)}) collective-permute-start(bf16[640,896]{1,0:T(8,128)(2,1)} %pad_maximum_fusion.1.refs_7_), channel_id=1, source_target_pairs={{0,16},{4,20},{8,24},{12,28},{16,0},{20,4},{24,8},{28,12},{1,17},{... | collective-permute-start | bytes 3440648 | tf_op jit(solution)/shard_map/ppermute | solution.py:20
  50.9 26.9 %collective-permute-start.6 = (bf16[640,896]{1,0:T(8,128)(2,1)S(1)}, bf16[640,896]{1,0:T(8,128)(2,1)}, u32[]{:S(2)}, u32[]{:S(2)}) collective-permute-start(bf16[640,896]{1,0:T(8,128)(2,1)S(1)} %pad_maximum_fusion.2.refs_7_), channel_id=1, source_target_pairs={{0,8},{4,12},{8,0},{12,4},{16,24},{20,28},{24,16},{28,20},{1,9},{5... | collective-permute-start | bytes 3440648 | tf_op jit(solution)/shard_map/ppermute | solution.py:20
  78.8 26.5 %collective-permute-start.14 = (bf16[640,896]{1,0:T(8,128)(2,1)}, bf16[640,896]{1,0:T(8,128)(2,1)}, u32[]{:S(2)}, u32[]{:S(2)}) collective-permute-start(bf16[640,896]{1,0:T(8,128)(2,1)} %collective-permute-done.refs_9_), channel_id=1, source_target_pairs={{0,16},{4,20},{8,24},{12,28},{16,0},{20,4},{24,8},{28,12},{1,17},{... | collective-permute-start | bytes 3440648 | tf_op jit(solution)/shard_map/ppermute | solution.py:20
  80.3 32.9 %collective-permute-start.16 = (bf16[128,5120]{1,0:T(8,128)(2,1)}, bf16[128,5120]{1,0:T(8,128)(2,1)}, u32[]{:S(2)}, u32[]{:S(2)}) collective-permute-start(bf16[128,5120]{1,0:T(8,128)(2,1)} %collective-permute-done.7.refs_2_), channel_id=1, source_target_pairs={{0,1},{1,2},{2,3},{4,5},{5,6},{6,7},{8,9},{9,10},{10,11},{12,13},{... | collective-permute-start | bytes 3932168 | tf_op jit(solution)/shard_map/ppermute | solution.py:57
  83.8 30.9 %collective-permute-start.17 = (bf16[128,5120]{1,0:T(8,128)(2,1)}, bf16[128,5120]{1,0:T(8,128)(2,1)}, u32[]{:S(2)}, u32[]{:S(2)}) collective-permute-start(bf16[128,5120]{1,0:T(8,128)(2,1)} %collective-permute-done.8.refs_5_), channel_id=1, source_target_pairs={{1,0},{2,1},{3,2},{5,4},{6,5},{7,6},{9,8},{10,9},{11,10},{13,12},{... | collective-permute-start | bytes 3932168 | tf_op jit(solution)/shard_map/ppermute | solution.py:58
  85.2 28.0 %collective-permute-start.15 = (bf16[640,896]{1,0:T(8,128)(2,1)}, bf16[640,896]{1,0:T(8,128)(2,1)}, u32[]{:S(2)}, u32[]{:S(2)}) collective-permute-start(bf16[640,896]{1,0:T(8,128)(2,1)} %collective-permute-done.1.refs_11_), channel_id=1, source_target_pairs={{0,8},{4,12},{8,0},{12,4},{16,24},{20,28},{24,16},{28,20},{1,9},{5... | collective-permute-start | bytes 3440648 | tf_op jit(solution)/shard_map/ppermute | solution.py:20
  86.7 26.4 %collective-permute-start.18 = (bf16[640,896]{1,0:T(8,128)(2,1)}, bf16[640,896]{1,0:T(8,128)(2,1)}, u32[]{:S(2)}, u32[]{:S(2)}) collective-permute-start(bf16[640,896]{1,0:T(8,128)(2,1)} %collective-permute-done.5.refs_11_), channel_id=1, source_target_pairs={{0,4},{4,0},{8,12},{12,8},{16,20},{20,16},{24,28},{28,24},{1,5},{5... | collective-permute-start | bytes 3440648 | tf_op jit(solution)/shard_map/ppermute | solution.py:20
  138.4 30.7 %collective-permute-start.26 = (bf16[640,1024]{1,0:T(8,128)(2,1)}, bf16[640,1024]{1,0:T(8,128)(2,1)S(1)}, u32[]{:S(2)}, u32[]{:S(2)}) collective-permute-start(bf16[640,1024]{1,0:T(8,128)(2,1)} %bitcast_bitcast_fusion.refs_0_), channel_id=1, source_target_pairs={{0,1},{1,2},{2,3},{4,5},{5,6},{6,7},{8,9},{9,10},{10,11},{12,13},{... | collective-permute-start | bytes 3932168 | tf_op jit(solution)/shard_map/ppermute | solution.py:57
  141.6 33.5 %collective-permute-start.23 = (bf16[640,896]{1,0:T(8,128)(2,1)}, bf16[640,896]{1,0:T(8,128)(2,1)S(1)}, u32[]{:S(2)}, u32[]{:S(2)}) collective-permute-start(bf16[640,896]{1,0:T(8,128)(2,1)} %collective-permute-done.14.refs_13_), channel_id=1, source_target_pairs={{0,4},{4,0},{8,12},{12,8},{16,20},{20,16},{24,28},{28,24},{1,5},{5... | collective-permute-start | bytes 3440648 | tf_op jit(solution)/shard_map/ppermute | solution.py:20
  144.6 62.3 %collective-permute-start.24 = (bf16[640,896]{1,0:T(8,128)(2,1)}, bf16[640,896]{1,0:T(8,128)(2,1)}, u32[]{:S(2)}, u32[]{:S(2)}) collective-permute-start(bf16[640,896]{1,0:T(8,128)(2,1)} %collective-permute-done.15.refs_13_), channel_id=1, source_target_pairs={{0,4},{4,0},{8,12},{12,8},{16,20},{20,16},{24,28},{28,24},{1,5},{5... | collective-permute-start | bytes 3440648 | tf_op jit(solution)/shard_map/ppermute | solution.py:20
  147.1 48.5 %collective-permute-start.25 = (bf16[640,1024]{1,0:T(8,128)(2,1)}, bf16[640,1024]{1,0:T(8,128)(2,1)}, u32[]{:S(2)}, u32[]{:S(2)}) collective-permute-start(bf16[640,1024]{1,0:T(8,128)(2,1)} %bitcast_bitcast_fusion.refs_0_), channel_id=1, source_target_pairs={{1,0},{2,1},{3,2},{5,4},{6,5},{7,6},{9,8},{10,9},{11,10},{13,12},{... | collective-permute-start | bytes 3932168 | tf_op jit(solution)/shard_map/ppermute | solution.py:58
  169.2 30.8 %collective-permute-start.27 = (bf16[640,1024]{1,0:T(8,128)(2,1)S(1)}, bf16[640,1024]{1,0:T(8,128)(2,1)}, u32[]{:S(2)}, u32[]{:S(2)}) collective-permute-start(bf16[640,1024]{1,0:T(8,128)(2,1)S(1)} %collective-permute-done.26), channel_id=1, source_target_pairs={{0,1},{1,2},{2,3},{4,5},{5,6},{6,7},{8,9},{9,10},{10,11},{12,13},{... | collective-permute-start | bytes 3932168 | tf_op jit(solution)/shard_map/ppermute | solution.py:57
  189.5 30.8 %all-to-all-start = ((bf16[8,128,896]{2,1,0:T(8,128)(2,1)}), bf16[8,128,896]{2,1,0:T(8,128)(2,1)S(1)}, u32[]{:S(2)}, u32[]{:S(2)}) async-start(bf16[8,128,896]{2,1,0:T(8,128)(2,1)} %bitcast.61), calls=%async_computation | async-start | bytes 3670016 | tf_op jit(solution)/shard_map/all_to_all | solution.py:472
  195.5 45.6 %collective-permute-start.29 = (bf16[640,1024]{1,0:T(8,128)(2,1)}, bf16[640,1024]{1,0:T(8,128)(2,1)}, u32[]{:S(2)}, u32[]{:S(2)}) collective-permute-start(bf16[640,1024]{1,0:T(8,128)(2,1)} %collective-permute-done.25), channel_id=1, source_target_pairs={{1,0},{2,1},{3,2},{5,4},{6,5},{7,6},{9,8},{10,9},{11,10},{13,12},{... | collective-permute-start | bytes 3932168 | tf_op jit(solution)/shard_map/ppermute | solution.py:58
  200.0 42.6 %collective-permute-start.28 = (bf16[640,1024]{1,0:T(8,128)(2,1)}, bf16[640,1024]{1,0:T(8,128)(2,1)}, u32[]{:S(2)}, u32[]{:S(2)}) collective-permute-start(bf16[640,1024]{1,0:T(8,128)(2,1)} %collective-permute-done.27), channel_id=1, source_target_pairs={{0,1},{1,2},{2,3},{4,5},{5,6},{6,7},{8,9},{9,10},{10,11},{12,13},{... | collective-permute-start | bytes 3932168 | tf_op jit(solution)/shard_map/ppermute | solution.py:57
  221.6 39.4 %all-to-all-start.1 = ((bf16[8,128,896]{2,1,0:T(8,128)(2,1)}), bf16[8,128,896]{2,1,0:T(8,128)(2,1)}, u32[]{:S(2)}, u32[]{:S(2)}) async-start(bf16[8,128,896]{2,1,0:T(8,128)(2,1)} %bitcast.62), calls=%async_computation.1 | async-start | bytes 3670016 | tf_op jit(solution)/shard_map/all_to_all | solution.py:472
  237.7 35.8 %collective-permute-start.43 = (bf16[512,896]{1,0:T(8,128)(2,1)}, bf16[512,896]{1,0:T(8,128)(2,1)}, u32[]{:S(2)}, u32[]{:S(2)}) collective-permute-start(bf16[512,896]{1,0:T(8,128)(2,1)} %get-tuple-element.71.refs_0_), channel_id=1, source_target_pairs={{0,16},{4,20},{8,24},{12,28},{16,0},{20,4},{24,8},{28,12},{1,17},{... | collective-permute-start | bytes 2752520 | tf_op jit(solution)/shard_map/ppermute | solution.py:20
  239.6 37.1 %collective-permute-start.41 = (bf16[512,896]{1,0:T(8,128)(2,1)}, bf16[512,896]{1,0:T(8,128)(2,1)}, u32[]{:S(2)}, u32[]{:S(2)}) collective-permute-start(bf16[512,896]{1,0:T(8,128)(2,1)} %get-tuple-element.71.refs_0_), channel_id=1, source_target_pairs={{0,8},{4,12},{8,0},{12,4},{16,24},{20,28},{24,16},{28,20},{1,9},{5... | collective-permute-start | bytes 2752520 | tf_op jit(solution)/shard_map/ppermute | solution.py:20
  241.1 64.5 %collective-permute-start.30 = (bf16[640,1024]{1,0:T(8,128)(2,1)}, bf16[640,1024]{1,0:T(8,128)(2,1)S(1)}, u32[]{:S(2)}, u32[]{:S(2)}) collective-permute-start(bf16[640,1024]{1,0:T(8,128)(2,1)} %collective-permute-done.29), channel_id=1, source_target_pairs={{1,0},{2,1},{3,2},{5,4},{6,5},{7,6},{9,8},{10,9},{11,10},{13,12},{... | collective-permute-start | bytes 3932168 | tf_op jit(solution)/shard_map/ppermute | solution.py:58
  272.8 35.0 %collective-permute-start.34 = (bf16[512,896]{1,0:T(8,128)(2,1)}, bf16[512,896]{1,0:T(8,128)(2,1)}, u32[]{:S(2)}, u32[]{:S(2)}) collective-permute-start(bf16[512,896]{1,0:T(8,128)(2,1)} %get-tuple-element.70.refs_0_), channel_id=1, source_target_pairs={{0,16},{4,20},{8,24},{12,28},{16,0},{20,4},{24,8},{28,12},{1,17},{... | collective-permute-start | bytes 2752520 | tf_op jit(solution)/shard_map/ppermute | solution.py:20
  273.5 34.7 %collective-permute-start.32 = (bf16[512,896]{1,0:T(8,128)(2,1)}, bf16[512,896]{1,0:T(8,128)(2,1)}, u32[]{:S(2)}, u32[]{:S(2)}) collective-permute-start(bf16[512,896]{1,0:T(8,128)(2,1)} %get-tuple-element.70.refs_0_), channel_id=1, source_target_pairs={{0,8},{4,12},{8,0},{12,4},{16,24},{20,28},{24,16},{28,20},{1,9},{5... | collective-permute-start | bytes 2752520 | tf_op jit(solution)/shard_map/ppermute | solution.py:20
  274.6 30.5 %collective-permute-start.46 = (bf16[256,896]{1,0:T(8,128)(2,1)S(1)}, bf16[256,896]{1,0:T(8,128)(2,1)}, u32[]{:S(2)}, u32[]{:S(2)}) collective-permute-start(bf16[256,896]{1,0:T(8,128)(2,1)S(1)} %slice.43), channel_id=1, source_target_pairs={{0,8},{4,12},{8,0},{12,4},{16,24},{20,28},{24,16},{28,20},{1,9},{5... | collective-permute-start | bytes 1376264 | tf_op jit(solution)/shard_map/ppermute | solution.py:20
  277.7 27.3 %collective-permute-start.45 = (bf16[256,896]{1,0:T(8,128)(2,1)S(1)}, bf16[256,896]{1,0:T(8,128)(2,1)}, u32[]{:S(2)}, u32[]{:S(2)}) collective-permute-start(bf16[256,896]{1,0:T(8,128)(2,1)S(1)} %slice.42), channel_id=1, source_target_pairs={{0,16},{4,20},{8,24},{12,28},{16,0},{20,4},{24,8},{28,12},{1,17},{... | collective-permute-start | bytes 1376264 | tf_op jit(solution)/shard_map/ppermute | solution.py:20
  314.3 32.7 %collective-permute-start.31 = (bf16[512,896]{1,0:T(8,128)(2,1)S(1)}, bf16[512,896]{1,0:T(8,128)(2,1)S(1)}, u32[]{:S(2)}, u32[]{:S(2)}) collective-permute-start(bf16[512,896]{1,0:T(8,128)(2,1)S(1)} %copy-done.13), channel_id=1, source_target_pairs={{0,4},{4,0},{8,12},{12,8},{16,20},{20,16},{24,28},{28,24},{1,5},{5... | collective-permute-start | bytes 2752520 | tf_op jit(solution)/shard_map/ppermute | solution.py:20
  316.8 30.2 %collective-permute-start.35 = (bf16[512,896]{1,0:T(8,128)(2,1)}, bf16[512,896]{1,0:T(8,128)(2,1)S(1)}, u32[]{:S(2)}, u32[]{:S(2)}) collective-permute-start(bf16[512,896]{1,0:T(8,128)(2,1)} %collective-permute-done.34.refs_4_), channel_id=1, source_target_pairs={{0,4},{4,0},{8,12},{12,8},{16,20},{20,16},{24,28},{28,24},{1,5},{5... | collective-permute-start | bytes 2752520 | tf_op jit(solution)/shard_map/ppermute | solution.py:20
  316.8 30.2 %collective-permute-start.33 = (bf16[512,896]{1,0:T(8,128)(2,1)}, bf16[512,896]{1,0:T(8,128)(2,1)S(1)}, u32[]{:S(2)}, u32[]{:S(2)}) collective-permute-start(bf16[512,896]{1,0:T(8,128)(2,1)} %collective-permute-done.32.refs_2_), channel_id=1, source_target_pairs={{0,4},{4,0},{8,12},{12,8},{16,20},{20,16},{24,28},{28,24},{1,5},{5... | collective-permute-start | bytes 2752520 | tf_op jit(solution)/shard_map/ppermute | solution.py:20
  (41 other events, 528.3 us)

commit v2 on v1

v2 whole, which is shorter than its diff:
```python
import functools
import math

import jax
import jax.numpy as jnp
from jax import lax
from jax.experimental import pallas as pl
from jax.experimental.pallas import tpu as pltpu
from jax.sharding import PartitionSpec as P

HEAD_DIMENSION = 128
VMEM_LIMIT = 56 * 1024 * 1024
ANY = pl.BlockSpec(memory_space=pl.ANY)
SMEM = pl.BlockSpec(memory_space=pltpu.SMEM)
VMEM = pl.BlockSpec(memory_space=pltpu.VMEM)


def swap(x, axis, bit):
    n = lax.axis_size(axis)
    return lax.ppermute(x, axis, [(i, i ^ bit) for i in range(n)])


def after(x, *others):
    return lax.optimization_barrier((x, *others))[0] if others else x


def together(*groups):
    flat = lax.optimization_barrier(tuple(x for group in groups for x in group))
    out, at = [], 0
    for group in groups:
        out.append(list(flat[at : at + len(group)]))
        at += len(group)
    return out


def spread(chunk, bits):
    have = {0: chunk}
    for bit in bits:
        for m in sorted(have):
            have[m ^ bit] = swap(have[m], "fsdp", bit)
    return [have[m] for m in range(len(have))]


def axis_bits(n):
    return [1 << i for i in range(1, n.bit_length() - 1)]


def line_step(a, b):
    n_fsdp, n = lax.axis_size("fsdp"), lax.axis_size("seq")

    def pairs(up):
        out = []
        for i in range(n_fsdp):
            for z in range(n):
                to = z + (1 if (i & 1) == up else -1)
                out.append((i * n + z, i * n + to if 0 <= to < n else (i ^ 1) * n + z))
        return out

    return lax.ppermute(a, ("fsdp", "seq"), pairs(0)), lax.ppermute(b, ("fsdp", "seq"), pairs(1))


def line_gather(x):
    a, b = [x], [x]
    for _ in range(1, lax.axis_size("seq")):
        a_next, b_next = line_step(a[-1], b[-1])
        a.append(a_next)
        b.append(b_next)
    return a[1:], b[1:]


def everywhere(x):
    n_fsdp, n_seq = lax.axis_size("fsdp"), lax.axis_size("seq")
    sent = jnp.broadcast_to(x, (n_fsdp * n_seq, *x.shape))
    got = lax.all_to_all(sent, ("fsdp", "seq"), split_axis=0, concat_axis=0, tiled=True)
    return got.reshape(n_fsdp, n_seq, *x.shape)


def by_core(x, even, odd):
    n = lax.axis_size("fsdp")
    return lax.ppermute(x, "fsdp", [(i, i ^ (odd if i & 1 else even)) for i in range(n)])


def in_masks(have):
    return [(j, 0, [(0, have[2 * j]), (1, have[2 * j + 1])]) for j in range(len(have) // 2)]


def in_pairs(own, near, far, diagonal):
    return [
        (0, 0, [(0, own[0]), (1, own[1])]),
        (1, 1, [(0, near[0]), (1, near[1])]),
        (2, -1, [(1, far[0]), (0, far[1])]),
        (3, 0, [(0, diagonal[0]), (1, diagonal[1])]),
    ]


def exchange_columns(blocks):
    return lax.all_to_all(blocks, "fsdp", split_axis=0, concat_axis=0, tiled=True)


def gather_all(block, rows, short, columns):
    high = axis_bits(lax.axis_size("fsdp"))
    weights = in_masks(spread(block, high + [1]))
    rows_a, rows_b = line_gather(rows)
    short = everywhere(short)
    return weights, rows_a, rows_b, short, exchange_columns(columns)


def gather_all_rounds(block, rows, short, columns):
    x, y = axis_bits(lax.axis_size("fsdp"))
    a1, b1 = line_step(rows, rows)
    near = [by_core(block, x, y)]
    sibling = swap(block, "fsdp", 1)
    ((a1, b1, *near, sibling, columns),) = together((a1, b1, *near, sibling, columns))
    near.append(by_core(sibling, x, y))
    columns = exchange_columns(columns)
    a2, b2 = line_step(a1, b1)
    ((a2, b2, *near, short, columns),) = together((a2, b2, *near, short, columns))
    diagonal = by_core(near[0], y, x)
    a3, b3 = line_step(a2, b2)
    far = [swap(part, "fsdp", 1) for part in near]
    short = everywhere(short)
    ((a3, b3, diagonal, *far, short, columns),) = together((a3, b3, diagonal, *far, short, columns))
    weights = in_pairs([block, sibling], near, far, [diagonal, swap(diagonal, "fsdp", 1)])
    return weights, [a1, a2, a3], [b1, b2, b3], short, columns


def line_copy(own, a, b, k, z, odd, view, spot, sem):
    if k == 0:
        copy = pltpu.make_async_copy(view(own), spot, sem)
        return copy.start, copy.wait
    n = len(a) + 1
    above = [pltpu.make_async_copy(view(r[k - 1]), spot, sem) for r in (b, a)]
    below = [pltpu.make_async_copy(view(r[n - k - 1]), spot, sem) for r in (a, b)]

    def start():
        for i in range(2):
            pl.when((z + k < n) & (odd == i))(above[i].start)
            pl.when((z + k >= n) & (odd == i))(below[i].start)

    return start, above[0].wait


def project_kernel(n_seq, layout, cap, group, me_ref, slot_ref, *refs):
    own = refs[0]
    rows_a = refs[1:n_seq]
    rows_b = refs[n_seq : 2 * n_seq - 1]
    count = sum(len(flips) for _, _, flips in layout)
    chunks = refs[2 * n_seq - 1 : 2 * n_seq - 1 + count]
    out_ref, a_v, w_v, acc, sem_a, sem_w = refs[2 * n_seq - 1 + count :]
    me, z = me_ref[0], me_ref[1]
    tok = own.shape[0]
    pairs, both, cols = w_v.shape
    depth = both // 2
    steps = []
    at = 0
    for j, (mask, change, flips) in enumerate(layout):
        pair = (me >> 1) ^ (mask + change * (me & 1))
        columns = pl.ds(pl.multiple_of(pair * both, both), both)
        copies = []
        for k in range(n_seq):
            spot = a_v.at[j, pl.ds(k * tok, tok)]
            copies.append(
                line_copy(own, rows_a, rows_b, k, z, me & 1, lambda r, c=columns: r.at[:, c], spot, sem_a.at[j, k])
            )
        for flip in flips:
            start = pl.multiple_of(((me & 1) ^ flip) * depth, depth)
            copy = pltpu.make_async_copy(
                chunks[at].at[:, pl.ds(group * cols, cols)], w_v.at[j, pl.ds(start, depth)], sem_w.at[at]
            )
            copies.append((copy.start, copy.wait))
            at += 1
        steps.append(copies)
    for j in range(min(2, pairs)):
        for start, _ in steps[j]:
            start()
    slot = slot_ref[...]
    order = lax.broadcasted_iota(jnp.int32, (out_ref.shape[0], slot.shape[1]), 0)
    pick = (slot == order).astype(jnp.bfloat16)
    for j in range(pairs):
        for _, wait in steps[j]:
            wait()
        if j + 2 < pairs:
            for start, _ in steps[j + 2]:
                start()
        part = jnp.dot(a_v[j], w_v[j], preferred_element_type=jnp.float32)
        if j == 0:
            acc[...] = part
        else:
            acc[...] += part
    qkv = acc[...].astype(jnp.bfloat16)
    out_ref[...] = jnp.dot(pick, qkv, preferred_element_type=jnp.float32).astype(jnp.bfloat16)


def project(place, slot, own, rows_a, rows_b, chunks, cap, group, groups):
    n_seq, n_fsdp = len(rows_a) + 1, 2 * len(chunks)
    layout = [(mask, change, [flip for flip, _ in parts]) for mask, change, parts in chunks]
    pieces = [part for _, _, parts in chunks for _, part in parts]
    tok, width = own.shape
    depth, cols = width // n_fsdp, pieces[0].shape[1] // groups
    length = n_seq * tok
    pairs = n_fsdp // 2
    return pl.pallas_call(
        functools.partial(project_kernel, n_seq, layout, cap, group),
        out_shape=jax.ShapeDtypeStruct((n_fsdp * cap, cols), jnp.bfloat16),
        in_specs=[SMEM, VMEM] + [ANY] * (2 * n_seq - 1 + len(pieces)),
        out_specs=VMEM,
        scratch_shapes=[
            pltpu.VMEM((pairs, length, 2 * depth), jnp.bfloat16),
            pltpu.VMEM((pairs, 2 * depth, cols), jnp.bfloat16),
            pltpu.VMEM((length, cols), jnp.float32),
            pltpu.SemaphoreType.DMA((pairs, n_seq)),
            pltpu.SemaphoreType.DMA((len(pieces),)),
        ],
        compiler_params=pltpu.CompilerParams(vmem_limit_bytes=VMEM_LIMIT),
        cost_estimate=pl.CostEstimate(
            flops=2 * length * width * cols + 2 * n_fsdp * cap * length * cols,
            bytes_accessed=2 * (length * width + width * cols + n_fsdp * cap * cols),
            transcendentals=0,
        ),
        name="project",
    )(place, slot, own, *rows_a, *rows_b, *pieces)


def attend_kernel(heads, block, place_ref, seg_row, seg_col, cot_ref, in_ref, *refs):
    out_ref, grad_ref, qkv, bias, dk_sum, dv_sum = refs
    size = HEAD_DIMENSION
    length = qkv.shape[0]
    scale = 1.0 / math.sqrt(size)
    key_pos = lax.broadcasted_iota(jnp.int32, (length, length), 0)
    query_pos = lax.broadcasted_iota(jnp.int32, (length, length), 1)
    allowed = (seg_col[...] == seg_row[...]) & (key_pos <= query_pos)
    bias[...] = jnp.where(allowed, 0.0, -1e30)
    spots = lax.broadcasted_iota(jnp.int32, (length, in_ref.shape[0]), 0)
    pick = (spots == place_ref[...]).astype(jnp.bfloat16)
    qkv[...] = jnp.dot(pick, in_ref[...], preferred_element_type=jnp.float32).astype(jnp.bfloat16)
    keys = qkv[:, heads * size : (heads + 1) * size]
    values = qkv[:, (heads + 1) * size : (heads + 2) * size]
    keys_t = keys.T
    values_t = values.T
    dk_sum[...] = jnp.zeros_like(dk_sum)
    dv_sum[...] = jnp.zeros_like(dv_sum)
    for h in range(heads):
        q_h = qkv[:, h * size : (h + 1) * size]
        d_h = cot_ref[:, h * size : (h + 1) * size]
        q_t = q_h.T
        d_t = d_h.T
        for start in range(0, length, block):
            stop = start + block
            scores = jnp.dot(keys[:stop], q_t[:, start:stop], preferred_element_type=jnp.float32)
            scores = scores + bias[:stop, start:stop]
            top = jnp.max(scores, axis=0, keepdims=True)
            weights = jnp.exp2((scores - top) * (scale * math.log2(math.e)))
            probs = weights * (1.0 / jnp.sum(weights, axis=0, keepdims=True))
            probs_b = probs.astype(jnp.bfloat16)
            out_t = jnp.dot(values_t[:, :stop], probs_b, preferred_element_type=jnp.float32).astype(
                jnp.bfloat16
            )
            delta = jnp.sum(
                d_t[:, start:stop].astype(jnp.float32) * out_t.astype(jnp.float32), axis=0, keepdims=True
            )
            dprob = jnp.dot(values[:stop], d_t[:, start:stop], preferred_element_type=jnp.float32)
            dscore = (probs * (dprob - delta)).astype(jnp.bfloat16)
            dq_t = (
                jnp.dot(keys_t[:, :stop], dscore, preferred_element_type=jnp.float32) * scale
            ).astype(jnp.bfloat16)
            dk_sum[:stop] += jnp.dot(dscore, q_h[start:stop], preferred_element_type=jnp.float32)
            dv_sum[:stop] += jnp.dot(probs_b, d_h[start:stop], preferred_element_type=jnp.float32)
            out_ref[start:stop, h * size : (h + 1) * size] = out_t.T
            grad_ref[start:stop, h * size : (h + 1) * size] = dq_t.T
    grad_ref[:, heads * size : (heads + 1) * size] = (dk_sum[...] * scale).astype(jnp.bfloat16)
    grad_ref[:, (heads + 1) * size : (heads + 2) * size] = dv_sum[...].astype(jnp.bfloat16)


def attend(place, segments, cotangent, group, arrived):
    slots, cols = arrived.shape
    size = HEAD_DIMENSION
    heads = cols // size - 2
    length = cotangent.shape[0]
    return pl.pallas_call(
        functools.partial(attend_kernel, heads, 256),
        grid=(1,),
        out_shape=[
            jax.ShapeDtypeStruct((length, heads * size), jnp.bfloat16),
            jax.ShapeDtypeStruct((length, cols), jnp.bfloat16),
        ],
        in_specs=[VMEM, VMEM, VMEM, pl.BlockSpec((length, heads * size), lambda i: (0, group)), VMEM],
        out_specs=[VMEM, VMEM],
        scratch_shapes=[
            pltpu.VMEM((length, cols), jnp.bfloat16),
            pltpu.VMEM((length, length), jnp.float32),
            pltpu.VMEM((length, size), jnp.float32),
            pltpu.VMEM((length, size), jnp.float32),
        ],
        compiler_params=pltpu.CompilerParams(vmem_limit_bytes=VMEM_LIMIT),
        cost_estimate=pl.CostEstimate(
            flops=12 * heads * length * length * size + 2 * length * slots * cols,
            bytes_accessed=2 * (slots * cols + 3 * length * cols),
            transcendentals=heads * length * length,
        ),
        name="attend",
    )(place, segments[None, :], segments[:, None], cotangent, arrived)


def pack_kernel(n_seq, me_ref, slot_ref, spot_ref, *refs):
    own = refs[0]
    rows_a = refs[1:n_seq]
    rows_b = refs[n_seq : 2 * n_seq - 1]
    out_ref, rows_v, slots_v, sem = refs[2 * n_seq - 1 :]
    packs, _, total = slots_v.shape
    sets = slot_ref.shape[0] // n_seq
    span = slot_ref.shape[1]
    each = total // (n_seq * sets)
    odd, z = me_ref[0] & 1, me_ref[1]
    p = pl.program_id(0)
    across = (((1,), (1,)), ((), ()))

    @pl.when(p == 0)
    def _():
        copies = [
            line_copy(own, rows_a, rows_b, k, z, odd, lambda r: r, rows_v.at[k], sem.at[k])
            for k in range(n_seq)
        ]
        for start, _ in copies:
            start()
        order = lax.broadcasted_iota(jnp.int32, (packs * each, span), 0)
        for k in range(n_seq):
            copies[k][1]()
            for g in range(sets):
                at = k * sets + g
                pick = (order == slot_ref[at : at + 1, :]).astype(jnp.bfloat16)
                moved = lax.dot_general(
                    rows_v[k, :, g * span : (g + 1) * span],
                    pick,
                    across,
                    preferred_element_type=jnp.float32,
                ).astype(jnp.bfloat16)
                for q in range(packs):
                    slots_v[q, :, at * each : (at + 1) * each] = moved[:, q * each : (q + 1) * each]

    spots = lax.broadcasted_iota(jnp.int32, (out_ref.shape[1], total), 0)
    pick = (spots == spot_ref[pl.ds(p, 1), :]).astype(jnp.bfloat16)
    out_ref[...] = lax.dot_general(
        slots_v[p], pick, across, preferred_element_type=jnp.float32
    ).astype(jnp.bfloat16)


def pack_columns(place, slot, spot, own, rows_a, rows_b):
    packs, total = spot.shape
    cols, count = own.shape
    n_seq = len(rows_a) + 1
    tokens = n_seq * count
    length = tokens // packs
    return pl.pallas_call(
        functools.partial(pack_kernel, n_seq),
        grid=(packs,),
        out_shape=jax.ShapeDtypeStruct((cols, tokens), jnp.bfloat16),
        in_specs=[
            SMEM,
            pl.BlockSpec(slot.shape, lambda i: (0, 0)),
            pl.BlockSpec(spot.shape, lambda i: (0, 0)),
        ]
        + [ANY] * (2 * n_seq - 1),
        out_specs=pl.BlockSpec((cols, length), lambda i: (0, i)),
        scratch_shapes=[
            pltpu.VMEM((n_seq, cols, count), jnp.bfloat16),
            pltpu.VMEM((packs, cols, total), jnp.bfloat16),
            pltpu.SemaphoreType.DMA((n_seq,)),
        ],
        compiler_params=pltpu.CompilerParams(vmem_limit_bytes=VMEM_LIMIT),
        cost_estimate=pl.CostEstimate(
            flops=4 * packs * total * length * cols,
            bytes_accessed=4 * tokens * cols,
            transcendentals=0,
        ),
        name="pack_columns",
    )(place, slot, spot, own, *rows_a, *rows_b)


def grads_kernel(layout, group, adds, has_before, me_ref, packed_ref, *refs):
    count = sum(len(flips) for _, _, flips in layout)
    before = refs[count : count + 3]
    gq_ref, gk_ref, gv_ref, packed_v, d_v, acc, sem, sem_p, sem_o = refs[
        count + (3 if has_before else 0) :
    ]
    me = me_ref[0]
    steps, width, both = packed_v.shape
    length = both // 2
    cols = d_v.shape[2]
    size = HEAD_DIMENSION
    q_cols = cols - 2 * size

    def results(refs):
        return (
            (acc.at[:, pl.ds(0, q_cols)], refs[0].at[:, pl.ds(group * q_cols, q_cols)]),
            (acc.at[:, pl.ds(q_cols, size)], refs[1].at[:, pl.ds(group * size, size)]),
            (acc.at[:, pl.ds(q_cols + size, size)], refs[2].at[:, pl.ds(group * size, size)]),
        )

    copies = [[] for _ in range(steps)]
    at = 0
    for j, (mask, change, flips) in enumerate(layout):
        for flip in flips:
            start = pl.multiple_of(((me & 1) ^ flip) * length, length)
            copies[j].append(
                pltpu.make_async_copy(refs[at], d_v.at[j, pl.ds(start, length)], sem.at[at])
            )
            at += 1
        start = pl.multiple_of(((me >> 1) ^ (mask + change * (me & 1))) * both, both)
        copies[j].append(
            pltpu.make_async_copy(packed_ref.at[:, pl.ds(start, both)], packed_v.at[j], sem_p.at[j])
        )
    for j in range(min(2, steps)):
        for copy in copies[j]:
            copy.start()
    if adds:
        old = [pltpu.make_async_copy(r, a, sem_o.at[i]) for i, (a, r) in enumerate(results(before))]
        for copy in old:
            copy.start()
        for copy in old:
            copy.wait()
    for j in range(steps):
        for copy in copies[j]:
            copy.wait()
        if j + 2 < steps:
            for copy in copies[j + 2]:
                copy.start()
        part = jnp.dot(packed_v[j], d_v[j], preferred_element_type=jnp.float32)
        if j == 0 and not adds:
            acc[...] = part
        else:
            acc[...] += part
    outs = [
        pltpu.make_async_copy(a, r, sem_o.at[i])
        for i, (a, r) in enumerate(results((gq_ref, gk_ref, gv_ref)))
    ]
    for copy in outs:
        copy.start()
    for copy in outs:
        copy.wait()


def gradients(place, packed, chunks, group, groups, before, adds):
    layout = [(mask, change, [flip for flip, _ in parts]) for mask, change, parts in chunks]
    pieces = [part for _, _, parts in chunks for _, part in parts]
    width = packed.shape[0]
    length, cols = pieces[0].shape
    steps = len(chunks)
    size = HEAD_DIMENSION
    shapes = [
        jax.ShapeDtypeStruct((width, groups * (cols - 2 * size)), jnp.float32),
        jax.ShapeDtypeStruct((width, groups * size), jnp.float32),
        jax.ShapeDtypeStruct((width, groups * size), jnp.float32),
    ]
    extra = [] if before is None else list(before)
    return pl.pallas_call(
        functools.partial(grads_kernel, layout, group, adds, before is not None),
        out_shape=shapes,
        in_specs=[SMEM] + [ANY] * (1 + len(pieces) + len(extra)),
        out_specs=[ANY] * 3,
        input_output_aliases={2 + len(pieces) + i: i for i in range(len(extra))},
        scratch_shapes=[
            pltpu.VMEM((steps, width, 2 * length), jnp.bfloat16),
            pltpu.VMEM((steps, 2 * length, cols), jnp.bfloat16),
            pltpu.VMEM((width, cols), jnp.float32),
            pltpu.SemaphoreType.DMA((len(pieces),)),
            pltpu.SemaphoreType.DMA((steps,)),
            pltpu.SemaphoreType.DMA((3,)),
        ],
        compiler_params=pltpu.CompilerParams(vmem_limit_bytes=VMEM_LIMIT),
        cost_estimate=pl.CostEstimate(
            flops=4 * steps * length * width * cols,
            bytes_accessed=4 * steps * length * (width + cols) + 4 * width * cols,
            transcendentals=0,
        ),
        name="gradients",
    )(place, packed, *pieces, *extra)


def on_device(hidden, destination, segment_ids, cotangent, w_query, key_weight, value_weight):
    tok_rows, width = hidden.shape
    n_fsdp = lax.axis_size("fsdp")
    n_seq = lax.axis_size("seq")
    length = n_seq * tok_rows
    size = HEAD_DIMENSION
    groups = key_weight.shape[1] // size
    q_cols = w_query.shape[1] // groups
    cap = n_seq * n_seq * (2 * tok_rows // (n_fsdp * n_seq))
    f = lax.axis_index("fsdp")
    z = lax.axis_index("seq")
    here = jnp.stack([f, z]).astype(jnp.int32)

    block = jnp.concatenate(
        [
            part[:, g * part.shape[1] // groups : (g + 1) * part.shape[1] // groups]
            for g in range(groups)
            for part in (w_query, key_weight, value_weight)
        ],
        axis=1,
    )
    high = axis_bits(n_fsdp)
    rounds = len(high) == 2 and n_seq == 4 and groups == 2
    gather = gather_all_rounds if rounds else gather_all
    columns = jnp.swapaxes(hidden.reshape(tok_rows, n_fsdp, width // n_fsdp), 0, 1)
    weights, rows_a, rows_b, dest, columns = gather(block, hidden, destination, columns)
    columns = columns.reshape(n_fsdp * tok_rows, -1).T
    mine = lax.dynamic_index_in_dim(dest, f, 0, keepdims=False)

    each = n_seq * (2 * tok_rows // (n_fsdp * n_seq))
    order = jnp.arange(tok_rows, dtype=jnp.int32)
    earlier = order[:, None] < order[None, :]

    def ranks(target):
        same = target[..., :, None] == target[..., None, :]
        return jnp.sum((same & earlier).astype(jnp.int32), axis=-2)

    def from_here(x, axis):
        return lax.dynamic_slice_in_dim(jnp.concatenate([x, x], axis), z, n_seq, axis)

    target = mine // length
    slot = target * cap + jnp.arange(n_seq, dtype=jnp.int32)[:, None] * each + ranks(target)
    slot = from_here(slot, 0).reshape(1, length)
    target = dest // length
    slots = target * each + ranks(target)
    numbers = jnp.arange(n_fsdp * each, dtype=jnp.int32)
    hit = slots[:, :, None, :] == numbers[None, None, :, None]
    spots = jnp.sum(jnp.where(hit, (dest % length + 1)[:, :, None, :], 0), axis=-1) - 1
    span = 128 // each
    within = (jnp.arange(n_fsdp, dtype=jnp.int32) % span)[:, None, None]
    slots = target * (span * each - each) + within * each + slots
    spots = spots.reshape(n_fsdp, n_seq, n_fsdp, each)
    place = lax.dynamic_index_in_dim(spots, f, 2, keepdims=False).reshape(1, n_fsdp * cap)
    slots = jnp.swapaxes(from_here(slots, 1), 0, 1).reshape(-1, span * tok_rows)
    spots = jnp.transpose(from_here(spots, 1), (2, 1, 0, 3)).reshape(n_fsdp, -1)

    def grads_of(packed, parts, group, before, adds=False):
        return gradients(here, packed, parts, group, groups, before, adds)

    exchange = lambda x: lax.all_to_all(x, "fsdp", split_axis=0, concat_axis=0, tiled=True)
    if not rounds:
        sent = [
            project(here, slot, hidden, rows_a, rows_b, weights, cap, g, groups)
            for g in range(groups)
        ]
        results = [
            attend(place, segment_ids[0], cotangent, g, exchange(sent[g])) for g in range(groups)
        ]
        packed = pack_columns(here, slots, spots, columns, *line_gather(columns))
        grads = None
        for g in range(groups):
            grads = grads_of(packed, in_masks(spread(results[g][1], high + [1])), g, grads)
        outs = [out for out, _ in results]
        return (jnp.concatenate(outs, axis=1) if groups > 1 else outs[0], *grads)

    x, y = high
    a1, b1 = line_step(columns, columns)
    sent0 = project(here, slot, hidden, rows_a, rows_b, weights, cap, 0, 2)
    arrived0 = exchange(sent0)
    ((slot, a1, b1, _),) = together((slot, a1, b1, sent0))
    sent1 = project(here, slot, hidden, rows_a, rows_b, weights, cap, 1, 2)
    arrived1 = exchange(sent1)
    a2, b2 = line_step(a1, b1)
    out0, g0 = attend(place, segment_ids[0], cotangent, 0, after(arrived0, sent1))
    ((g0, a2, b2),) = together((g0, a2, b2))
    s0, n0 = swap(g0, "fsdp", 1), by_core(g0, x, y)
    a3, b3 = line_step(a2, b2)
    out1, g1 = attend(place, segment_ids[0], cotangent, 1, after(arrived1, g0))
    ((s0, n0, g1),) = together((s0, n0, g1))
    m0, n1, d0 = by_core(s0, x, y), by_core(g1, x, y), by_core(n0, y, x)
    s1 = swap(g1, "fsdp", 1)
    packed = pack_columns(here, slots, spots, columns, [a1, a2, a3], [b1, b2, b3])
    ((packed, m0, n0, n1, d0, s1),) = together((packed, m0, n0, n1, d0, s1))
    m1, d1 = by_core(s1, x, y), by_core(n1, y, x)
    f0 = [swap(n0, "fsdp", 1), swap(m0, "fsdp", 1)]
    e0 = swap(d0, "fsdp", 1)
    grads = grads_of(packed, in_pairs([g0, s0], [n0, m0], f0, [d0, e0]), 0, None)
    ((m1, d1, n1, *grads),) = together((m1, d1, n1, *grads))
    f1 = [swap(n1, "fsdp", 1), swap(m1, "fsdp", 1)]
    e1 = swap(d1, "fsdp", 1)
    parts = in_pairs([g1, s1], [n1, m1], f1, [d1, e1])
    grads = grads_of(packed, parts[:2], 1, grads)
    grads = grads_of(packed, parts[2:], 1, grads, True)
    return (jnp.concatenate([out0, out1], axis=1), *grads)


def solution(mesh):
    placed = (
        P(("fsdp", "seq"), None),
        P(("fsdp", "seq")),
        P("fsdp", None),
        P("fsdp", "seq"),
        P("fsdp", "seq"),
        P("fsdp", "seq"),
        P("fsdp", "seq"),
    )
    return jax.shard_map(
        on_device,
        mesh=mesh,
        in_specs=placed,
        out_specs=(P("fsdp", "seq"), P("fsdp", "seq"), P("fsdp", "seq"), P("fsdp", "seq")),
        check_vma=False,
    )
```

time: 368 us -> 291 us (0.79)
  waiting for transfers between devices: 131 us -> 68 us
  blocking collectives: 21.7 us -> 73.1 us
  starting transfers between devices: 70.7 us -> 30.4 us
  Pallas kernels: 106 us -> 90 us
  other arithmetic: 10.8 us -> 4.61 us
    ppermute x37 -> x12, waiting for transfers between devices: 104 us -> 3.11 us  [swap(): return lax.ppermute(x, axis, [(i, i ^ bit) for i in range(n)])]
    all_to_all x1 -> x2, blocking collectives: 21.7 us -> 73.1 us  [the longest x1 41.1 us: exchange_columns(): lax.all_to_all(blocks, 'fsdp', split_axis=0, concat_axis=0, tiled=True)]
    ppermute x12 -> x21, waiting for transfers between devices: 26.5 us -> 59.1 us  [the longest x6 43.4 us: line_step(): lax.ppermute(a, ('fsdp', 'seq'), pairs(0))]
    ppermute x37 -> x12, starting transfers between devices: 27.4 us -> 1.52 us  [swap(): return lax.ppermute(x, axis, [(i, i ^ bit) for i in range(n)])]
    pallas_call x6, Pallas kernels: 81.9 us -> 66.2 us  [the longest x3 25.8 us: gradients(): pl.pallas_call(functools.partial(grads_kernel, layout, group, adds, befor...]
    ppermute x12 -> x21, starting transfers between devices: 35.4 us -> 20 us  [the longest x9 10.7 us: by_core(): lax.ppermute(x, 'fsdp', [(i, i ^ (odd if i & 1 else even)) for i in range...]
    select_n x9 -> x1, other arithmetic: 6.31 us -> 0.03 us  [on_device(): target = dest // length]
    slice x6 -> x0, local copies, waits for them, and re-layouts: 5.95 us -> none  [the longest x2 2.19 us: gather_plane(): from_y[half:]]
  transfers between devices with their start and end apart: 51 -> 35, of which waited for: 13 -> 10; matrix products, arithmetic and copies ran while one was open for 6% -> 5% of each run, Pallas kernels for 26% -> 29%
where the time goes in v2:
time: 291 us; the launch traced here: 285 us
  Pallas kernels  90 us (31%)
  blocking collectives  73.1 us (25%)
  waiting for transfers between devices  68 us (23%)
  starting transfers between devices  30.4 us (10%)
  local copies, waits for them, and re-layouts  17.6 us (6%)
  other arithmetic  4.61 us (2%)
    ppermute x6, waiting for transfers between devices, line_step(): lax.ppermute(a, ('fsdp', 'seq'), pairs(0))  43.4 us
    all_to_all x1, blocking collectives, exchange_columns(): lax.all_to_all(blocks, 'fsdp', split_axis=0, concat_axis=0, tiled=True)  41.1 us
    all_to_all x1, blocking collectives, everywhere(): lax.all_to_all(sent, ('fsdp', 'seq'), split_axis=0, concat_axis=0, tiled=...  32 us
    pallas_call x3, Pallas kernels, gradients(): pl.pallas_call(functools.partial(grads_kernel, layout, group, adds, befor...  25.8 us
    pallas_call x2, Pallas kernels, attend(): pl.pallas_call(functools.partial(attend_kernel, heads, 256), grid=(1,), o...  23.9 us
    pallas_call x2, Pallas kernels, project(): pl.pallas_call(functools.partial(project_kernel, n_seq, layout, cap, grou...  22.8 us
    pallas_call x1, Pallas kernels, pack_columns(): pl.pallas_call(functools.partial(pack_kernel, n_seq), grid=(packs,), out_...  17.6 us
    ppermute x9, waiting for transfers between devices, by_core(): lax.ppermute(x, 'fsdp', [(i, i ^ (odd if i & 1 else even)) for i in range...  14.1 us
  transfers between devices with their start and end apart: 35, of which 10 were waited for; matrix products, arithmetic and copies ran while one was open for 5% of the time, Pallas kernels for 29%

profile of v2, /device:TPU:0, one launch (start us, length us, event | category | flops | bytes accessed | tf_op | source)
XLA Modules:
  0.0 285.2 jit_solution(4082152209428317155)
XLA Ops:
  4.2 3.0 %collective-permute-start.2 = (bf16[640,1792]{1,0:T(8,128)(2,1)S(1)}, bf16[640,1792]{1,0:T(8,128)(2,1)}, u32[]{:S(2)}, u32[]{:S(2)}) collective-permute-start(bf16[640,1792]{1,0:T(8,128)(2,1)S(1)} %slice_dynamic-update-slice_fusion.2.refs_7_), channel_id=1, source_target_pairs={{0,8},{4,20},{8,0},{12,28},{16,24},{20,4},{24,16},{28,12},{1,9},{5... | collective-permute-start | bytes 6881288 | tf_op jit(solution)/shard_map/ppermute | solution.py:80
  7.2 1.6 collective-permute-start
  8.8 2.4 copy.44
  11.3 26.7 %collective-permute-done.refs_1_ = bf16[128,5120]{1,0:T(8,128)(2,1)} collective-permute-done((bf16[128,5120]{1,0:T(8,128)(2,1)}, bf16[128,5120]{1,0:T(8,128)(2,1)}, u32[]{:S(2)}, u32[]{:S(2)}) %collective-permute-start) | collective-permute-done | bytes 1310752 | tf_op jit(solution)/shard_map/ppermute | solution.py:59
  39.3 1.8 collective-permute-start.4
  41.1 41.1 %all_to_all.35 = bf16[8,128,640]{1,2,0:T(8,128)(2,1)} all-to-all(bf16[8,128,640]{1,2,0:T(8,128)(2,1)} %bitcast.49), channel_id=1, replica_groups=mesh['fsdp'=8,'seq'=4] {'fsdp'}, dimensions={0} | all-to-all | bytes 2621440 | tf_op jit(solution)/shard_map/all_to_all | solution.py:97
  83.7 1.8 collective-permute-start.7
  85.5 32.0 %all_to_all.36 = s32[32,1,128]{2,1,0:T(1,128)S(1)} all-to-all(s32[32,1,128]{2,1,0:T(1,128)S(1)} %broadcast_in_dim.10), channel_id=1, replica_groups=mesh['fsdp'=8,'seq'=4] {'fsdp','seq'}, dimensions={0} | all-to-all | bytes 32768 | tf_op jit(solution)/shard_map/all_to_all | solution.py:74
  120.5 2.6 bitcast_bitcast_fusion.refs_0_
  124.4 11.4 %project.2 = bf16[1024,896]{1,0:T(8,128)(2,1)} custom-call(s32[2]{0:T(128)} %pad_add_fusion.1.me_ref, s32[1,512]{1,0:T(1,128)} %bitcast.54, bf16[128,5120]{1,0:T(8,128)(2,1)} %refs_0_.3, bf16[128,5120]{1,0:T(8,128)(2,1)} %collective-permute-done.refs_1_, bf16[128,5120]{1,0:T(8,128)(2,1)} %copy-done.4, bf16[128,5120]{1,0:T(8,128)(2,1)} %copy-done.6, ...), custom_call_target="tpu_custom_call" | custom-call | flops 5637144576 | bytes 16252928 | tf_op jit(solution)/shard_map/project/pallas_call | solution.py:202
  135.8 4.4 %all-to-all-start.2 = ((bf16[8,128,896]{2,1,0:T(8,128)(2,1)}), bf16[8,128,896]{2,1,0:T(8,128)(2,1)S(1)}, u32[]{:S(2)}, u32[]{:S(2)}) async-start(bf16[8,128,896]{2,1,0:T(8,128)(2,1)} %bitcast.48), calls=%async_computation.2 | async-start | bytes 3670016 | tf_op jit(solution)/shard_map/all_to_all | solution.py:538
  141.9 11.0 %collective-permute-done.13.refs_1_ = bf16[640,1024]{1,0:T(8,128)(2,1)} collective-permute-done((bf16[640,1024]{1,0:T(8,128)(2,1)}, bf16[640,1024]{1,0:T(8,128)(2,1)}, u32[]{:S(2)}, u32[]{:S(2)}) %collective-permute-start.13) | collective-permute-done | bytes 1310752 | tf_op jit(solution)/shard_map/ppermute | solution.py:59
  153.8 1.6 collective-permute-start.15
  155.4 1.6 select_reduce_fusion
  157.0 11.4 %project.3 = bf16[1024,896]{1,0:T(8,128)(2,1)} custom-call(s32[2]{0:T(128)} %pad_add_fusion.1.me_ref, s32[1,512]{1,0:T(1,128)} %bitcast.55, bf16[128,5120]{1,0:T(8,128)(2,1)} %refs_0_.3, bf16[128,5120]{1,0:T(8,128)(2,1)} %collective-permute-done.refs_1_, bf16[128,5120]{1,0:T(8,128)(2,1)} %copy-done.4, bf16[128,5120]{1,0:T(8,128)(2,1)} %copy-done.6, ...), custom_call_target="tpu_custom_call" | custom-call | flops 5637144576 | bytes 16252928 | tf_op jit(solution)/shard_map/project/pallas_call | solution.py:202
  168.5 4.5 %all-to-all-start.3 = ((bf16[8,128,896]{2,1,0:T(8,128)(2,1)}), bf16[8,128,896]{2,1,0:T(8,128)(2,1)}, u32[]{:S(2)}, u32[]{:S(2)}) async-start(bf16[8,128,896]{2,1,0:T(8,128)(2,1)} %bitcast.47), calls=%async_computation.3 | async-start | bytes 3670016 | tf_op jit(solution)/shard_map/all_to_all | solution.py:538
  173.9 11.8 %attend.2 = (bf16[512,640]{1,0:T(8,128)(2,1)}, bf16[512,896]{1,0:T(8,128)(2,1)}) custom-call(s32[1,1024]{1,0:T(1,128)} %reshape.145.place_ref, s32[1,512]{1,0:T(1,128)} %seg_row.3, s32[512,1]{1,0:T(8,128)} %copy.48.seg_col, bf16[512,1280]{1,0:T(8,128)(2,1)} %cot_ref.3, bf16[1024,896]{1,0:T(8,128)(2,1)} %bitcast.50), custom_call_target="tpu_custom_call" | custom-call | flops 2952790016 | bytes 4587520 | tf_op jit(solution)/shard_map/attend/pallas_call | solution.py:279
  185.7 2.0 collective-permute-start.17
  187.9 1.7 collective-permute-start.20
  191.0 5.8 %all-to-all-done.3 = bf16[8,128,896]{2,1,0:T(8,128)(2,1)} async-done(((bf16[8,128,896]{2,1,0:T(8,128)(2,1)}), bf16[8,128,896]{2,1,0:T(8,128)(2,1)}, u32[]{:S(2)}, u32[]{:S(2)}) %all-to-all-start.3) | async-done | bytes 1835040 | tf_op jit(solution)/shard_map/all_to_all | solution.py:538
  196.8 12.0 %attend.3 = (bf16[512,640]{1,0:T(8,128)(2,1)}, bf16[512,896]{1,0:T(8,128)(2,1)}) custom-call(s32[1,1024]{1,0:T(1,128)} %reshape.145.place_ref, s32[1,512]{1,0:T(1,128)} %seg_row.3, s32[512,1]{1,0:T(8,128)} %copy.48.seg_col, bf16[512,1280]{1,0:T(8,128)(2,1)} %cot_ref.3, bf16[1024,896]{1,0:T(8,128)(2,1)} %bitcast.12.in_ref), custom_call_target="tpu_custom_call" | custom-call | flops 2952790016 | bytes 4587520 | tf_op jit(solution)/shard_map/attend/pallas_call | solution.py:279
  209.4 1.6 collective-permute-start.21
  211.0 5.6 %collective-permute-done.17.refs_3_ = bf16[640,1024]{1,0:T(8,128)(2,1)S(1)} collective-permute-done((bf16[640,1024]{1,0:T(8,128)(2,1)S(1)}, bf16[640,1024]{1,0:T(8,128)(2,1)S(1)}, u32[]{:S(2)}, u32[]{:S(2)}) %collective-permute-start.17) | collective-permute-done | bytes 1310752 | tf_op jit(solution)/shard_map/ppermute | solution.py:59
  216.6 1.6 collective-permute-start.23
  218.2 17.6 %pack_columns.1.packed_ref = bf16[640,4096]{1,0:T(8,128)(2,1)} custom-call(s32[2]{0:T(128)} %pad_add_fusion.1.me_ref, s32[8,512]{1,0:T(8,128)} %reshape.148.slot_ref, s32[8,1024]{1,0:T(8,128)} %reshape.149.spot_ref, bf16[640,1024]{1,0:T(8,128)(2,1)} %bitcast_bitcast_fusion.refs_0_, bf16[640,1024]{1,0:T(8,128)(2,1)} %collective-permute-done.13.refs_1_, ...), custom_call_target="tpu_custom_call" | custom-call | flops 10737418240 | bytes 10485760 | tf_op jit(solution)/shard_map/pack_columns/pallas_call | solution.py:353
  235.8 6.4 %collective-permute-done.21.refs_3_ = bf16[512,896]{1,0:T(8,128)(2,1)S(1)} collective-permute-done((bf16[512,896]{1,0:T(8,128)(2,1)}, bf16[512,896]{1,0:T(8,128)(2,1)S(1)}, u32[]{:S(2)}, u32[]{:S(2)}) %collective-permute-start.21) | collective-permute-done | bytes 917536 | tf_op jit(solution)/shard_map/ppermute | solution.py:80
  244.0 1.6 collective-permute-done.27.refs_4_
  245.5 1.5 collective-permute-done.28.refs_5_
  248.0 10.1 %gradients.3 = (f32[640,1280]{1,0:T(8,128)}, f32[640,256]{1,0:T(8,128)}, f32[640,256]{1,0:T(8,128)}) custom-call(s32[2]{0:T(128)} %pad_add_fusion.1.me_ref, bf16[640,4096]{1,0:T(8,128)(2,1)} %pack_columns.1.packed_ref, bf16[512,896]{1,0:T(8,128)(2,1)} %get-tuple-element.82.refs_0_, bf16[512,896]{1,0:T(8,128)(2,1)} %collective-permute-done.19.refs_1_, ...), custom_call_target="tpu_custom_call" | custom-call | flops 4697620480 | bytes 14876672 | tf_op jit(solution)/shard_map/gradients/pallas_call | solution.py:455
  258.2 7.7 %collective-permute-done.25.refs_3_ = bf16[512,896]{1,0:T(8,128)(2,1)S(1)} collective-permute-done((bf16[512,896]{1,0:T(8,128)(2,1)S(1)}, bf16[512,896]{1,0:T(8,128)(2,1)S(1)}, u32[]{:S(2)}, u32[]{:S(2)}) %collective-permute-start.25) | collective-permute-done | bytes 917536 | tf_op jit(solution)/shard_map/ppermute | solution.py:80
  267.7 7.0 %gradients.4 = (f32[640,1280]{1,0:T(8,128)}, f32[640,256]{1,0:T(8,128)}, f32[640,256]{1,0:T(8,128)}) custom-call(s32[2]{0:T(128)} %pad_add_fusion.1.me_ref, bf16[640,4096]{1,0:T(8,128)(2,1)} %pack_columns.1.packed_ref, bf16[512,896]{1,0:T(8,128)(2,1)} %get-tuple-element.90.refs_0_, ...), custom_call_target="tpu_custom_call", output_to_operand_aliasing={{0}: (6, {}), {1}: (7, {}), {2}: (8, {})} | custom-call | flops 2348810240 | bytes 8585216 | tf_op jit(solution)/shard_map/gradients/pallas_call | solution.py:455
  276.3 8.6 %gradients.5 = (f32[640,1280]{1,0:T(8,128)}, f32[640,256]{1,0:T(8,128)}, f32[640,256]{1,0:T(8,128)}) custom-call(s32[2]{0:T(128)} %pad_add_fusion.1.me_ref, bf16[640,4096]{1,0:T(8,128)(2,1)} %pack_columns.1.packed_ref, bf16[512,896]{1,0:T(8,128)(2,1)} %copy-done.14, ...), custom_call_target="tpu_custom_call", output_to_operand_aliasing={{0}: (6, {}), {1}: (7, {}), {2}: (8, {})} | custom-call | flops 2348810240 | bytes 8585216 | tf_op jit(solution)/shard_map/gradients/pallas_call | solution.py:455
  (141 shorter events, 22.0 us)
Async XLA Ops:
  4.2 34.5 %collective-permute-start.2 = (bf16[640,1792]{1,0:T(8,128)(2,1)S(1)}, bf16[640,1792]{1,0:T(8,128)(2,1)}, u32[]{:S(2)}, u32[]{:S(2)}) collective-permute-start(bf16[640,1792]{1,0:T(8,128)(2,1)S(1)} %slice_dynamic-update-slice_fusion.2.refs_7_), channel_id=1, source_target_pairs={{0,8},{4,20},{8,0},{12,28},{16,24},{20,4},{24,16},{28,12},{1,9},{5... | collective-permute-start | bytes 6881288 | tf_op jit(solution)/shard_map/ppermute | solution.py:80
  7.2 31.5 %collective-permute-start.3 = (bf16[640,1792]{1,0:T(8,128)(2,1)S(1)}, bf16[640,1792]{1,0:T(8,128)(2,1)}, u32[]{:S(2)}, u32[]{:S(2)}) collective-permute-start(bf16[640,1792]{1,0:T(8,128)(2,1)S(1)} %slice_dynamic-update-slice_fusion.2.refs_7_), channel_id=1, source_target_pairs={{0,4},{4,0},{8,12},{12,8},{16,20},{20,16},{24,28},{28,24},{1,5},{5... | collective-permute-start | bytes 6881288 | tf_op jit(solution)/shard_map/ppermute | solution.py:20
  7.2 30.8 %collective-permute-start = (bf16[128,5120]{1,0:T(8,128)(2,1)}, bf16[128,5120]{1,0:T(8,128)(2,1)}, u32[]{:S(2)}, u32[]{:S(2)}) collective-permute-start(bf16[128,5120]{1,0:T(8,128)(2,1)} %refs_0_.3), channel_id=1, source_target_pairs={{0,1},{1,2},{2,3},{3,7},{4,0},{5,4},{6,5},{7,6},{8,9},{9,10},{10,1... | collective-permute-start | bytes 3932168 | tf_op jit(solution)/shard_map/ppermute | solution.py:59
  8.8 29.9 %collective-permute-start.1 = (bf16[128,5120]{1,0:T(8,128)(2,1)}, bf16[128,5120]{1,0:T(8,128)(2,1)}, u32[]{:S(2)}, u32[]{:S(2)}) collective-permute-start(bf16[128,5120]{1,0:T(8,128)(2,1)} %refs_0_.3), channel_id=1, source_target_pairs={{0,4},{1,0},{2,1},{3,2},{4,5},{5,6},{6,7},{7,3},{8,12},{9,8},{10,9... | collective-permute-start | bytes 3932168 | tf_op jit(solution)/shard_map/ppermute | solution.py:59
  38.8 43.5 %collective-permute-start.6 = (bf16[640,1792]{1,0:T(8,128)(2,1)}, bf16[640,1792]{1,0:T(8,128)(2,1)S(1)}, u32[]{:S(2)}, u32[]{:S(2)}) collective-permute-start(bf16[640,1792]{1,0:T(8,128)(2,1)} %collective-permute-done.3.refs_8_), channel_id=1, source_target_pairs={{0,8},{4,20},{8,0},{12,28},{16,24},{20,4},{24,16},{28,12},{1,9},{5... | collective-permute-start | bytes 6881288 | tf_op jit(solution)/shard_map/ppermute | solution.py:80
  39.3 42.9 %collective-permute-start.4 = (bf16[128,5120]{1,0:T(8,128)(2,1)}, bf16[128,5120]{1,0:T(8,128)(2,1)S(1)}, u32[]{:S(2)}, u32[]{:S(2)}) collective-permute-start(bf16[128,5120]{1,0:T(8,128)(2,1)} %collective-permute-done.refs_1_), channel_id=1, source_target_pairs={{0,1},{1,2},{2,3},{3,7},{4,0},{5,4},{6,5},{7,6},{8,9},{9,10},{10,1... | collective-permute-start | bytes 3932168 | tf_op jit(solution)/shard_map/ppermute | solution.py:59
  41.1 41.1 %collective-permute-start.5 = (bf16[128,5120]{1,0:T(8,128)(2,1)}, bf16[128,5120]{1,0:T(8,128)(2,1)S(1)}, u32[]{:S(2)}, u32[]{:S(2)}) collective-permute-start(bf16[128,5120]{1,0:T(8,128)(2,1)} %collective-permute-done.1.refs_4_), channel_id=1, source_target_pairs={{0,4},{1,0},{2,1},{3,2},{4,5},{5,6},{6,7},{7,3},{8,12},{9,8},{10,9... | collective-permute-start | bytes 3932168 | tf_op jit(solution)/shard_map/ppermute | solution.py:59
  82.3 35.3 %collective-permute-start.10 = (bf16[640,1792]{1,0:T(8,128)(2,1)}, bf16[640,1792]{1,0:T(8,128)(2,1)S(1)}, u32[]{:S(2)}, u32[]{:S(2)}) collective-permute-start(bf16[640,1792]{1,0:T(8,128)(2,1)} %collective-permute-done.2.refs_9_), channel_id=1, source_target_pairs={{0,4},{4,0},{8,12},{12,8},{16,20},{20,16},{24,28},{28,24},{1,5},{5... | collective-permute-start | bytes 6881288 | tf_op jit(solution)/shard_map/ppermute | solution.py:20
  82.3 35.3 %collective-permute-start.9 = (bf16[640,1792]{1,0:T(8,128)(2,1)}, bf16[640,1792]{1,0:T(8,128)(2,1)}, u32[]{:S(2)}, u32[]{:S(2)}) collective-permute-start(bf16[640,1792]{1,0:T(8,128)(2,1)} %collective-permute-done.2.refs_9_), channel_id=1, source_target_pairs={{0,16},{4,12},{8,24},{12,4},{16,0},{20,28},{24,8},{28,20},{1,17},{... | collective-permute-start | bytes 6881288 | tf_op jit(solution)/shard_map/ppermute | solution.py:80
  83.7 33.9 %collective-permute-start.11 = (bf16[640,1792]{1,0:T(8,128)(2,1)S(1)}, bf16[640,1792]{1,0:T(8,128)(2,1)S(1)}, u32[]{:S(2)}, u32[]{:S(2)}) collective-permute-start(bf16[640,1792]{1,0:T(8,128)(2,1)S(1)} %collective-permute-done.6.refs_10_), channel_id=1, source_target_pairs={{0,4},{4,0},{8,12},{12,8},{16,20},{20,16},{24,28},{28,24},{1,5},{5... | collective-permute-start | bytes 6881288 | tf_op jit(solution)/shard_map/ppermute | solution.py:20
  83.7 33.9 %collective-permute-start.7 = (bf16[128,5120]{1,0:T(8,128)(2,1)S(1)}, bf16[128,5120]{1,0:T(8,128)(2,1)S(1)}, u32[]{:S(2)}, u32[]{:S(2)}) collective-permute-start(bf16[128,5120]{1,0:T(8,128)(2,1)S(1)} %collective-permute-done.4.refs_2_), channel_id=1, source_target_pairs={{0,1},{1,2},{2,3},{3,7},{4,0},{5,4},{6,5},{7,6},{8,9},{9,10},{10,1... | collective-permute-start | bytes 3932168 | tf_op jit(solution)/shard_map/ppermute | solution.py:59
  85.5 32.1 %collective-permute-start.8 = (bf16[128,5120]{1,0:T(8,128)(2,1)S(1)}, bf16[128,5120]{1,0:T(8,128)(2,1)S(1)}, u32[]{:S(2)}, u32[]{:S(2)}) collective-permute-start(bf16[128,5120]{1,0:T(8,128)(2,1)S(1)} %collective-permute-done.5.refs_5_), channel_id=1, source_target_pairs={{0,4},{1,0},{2,1},{3,2},{4,5},{5,6},{6,7},{7,3},{8,12},{9,8},{10,9... | collective-permute-start | bytes 3932168 | tf_op jit(solution)/shard_map/ppermute | solution.py:59
  119.0 5.4 %collective-permute-start.12 = (bf16[640,1792]{1,0:T(8,128)(2,1)}, bf16[640,1792]{1,0:T(8,128)(2,1)}, u32[]{:S(2)}, u32[]{:S(2)}) collective-permute-start(bf16[640,1792]{1,0:T(8,128)(2,1)} %collective-permute-done.9.refs_13_), channel_id=1, source_target_pairs={{0,4},{4,0},{8,12},{12,8},{16,20},{20,16},{24,28},{28,24},{1,5},{5... | collective-permute-start | bytes 6881288 | tf_op jit(solution)/shard_map/ppermute | solution.py:20
  123.0 29.9 %collective-permute-start.13 = (bf16[640,1024]{1,0:T(8,128)(2,1)}, bf16[640,1024]{1,0:T(8,128)(2,1)}, u32[]{:S(2)}, u32[]{:S(2)}) collective-permute-start(bf16[640,1024]{1,0:T(8,128)(2,1)} %bitcast_bitcast_fusion.refs_0_), channel_id=1, source_target_pairs={{0,1},{1,2},{2,3},{3,7},{4,0},{5,4},{6,5},{7,6},{8,9},{9,10},{10,1... | collective-permute-start | bytes 3932168 | tf_op jit(solution)/shard_map/ppermute | solution.py:59
  123.5 30.3 %collective-permute-start.14 = (bf16[640,1024]{1,0:T(8,128)(2,1)}, bf16[640,1024]{1,0:T(8,128)(2,1)}, u32[]{:S(2)}, u32[]{:S(2)}) collective-permute-start(bf16[640,1024]{1,0:T(8,128)(2,1)} %bitcast_bitcast_fusion.refs_0_), channel_id=1, source_target_pairs={{0,4},{1,0},{2,1},{3,2},{4,5},{5,6},{6,7},{7,3},{8,12},{9,8},{10,9... | collective-permute-start | bytes 3932168 | tf_op jit(solution)/shard_map/ppermute | solution.py:59
  135.8 32.7 %all-to-all-start.2 = ((bf16[8,128,896]{2,1,0:T(8,128)(2,1)}), bf16[8,128,896]{2,1,0:T(8,128)(2,1)S(1)}, u32[]{:S(2)}, u32[]{:S(2)}) async-start(bf16[8,128,896]{2,1,0:T(8,128)(2,1)} %bitcast.48), calls=%async_computation.2 | async-start | bytes 3670016 | tf_op jit(solution)/shard_map/all_to_all | solution.py:538
  153.8 31.9 %collective-permute-start.15 = (bf16[640,1024]{1,0:T(8,128)(2,1)}, bf16[640,1024]{1,0:T(8,128)(2,1)S(1)}, u32[]{:S(2)}, u32[]{:S(2)}) collective-permute-start(bf16[640,1024]{1,0:T(8,128)(2,1)} %collective-permute-done.13.refs_1_), channel_id=1, source_target_pairs={{0,1},{1,2},{2,3},{3,7},{4,0},{5,4},{6,5},{7,6},{8,9},{9,10},{10,1... | collective-permute-start | bytes 3932168 | tf_op jit(solution)/shard_map/ppermute | solution.py:59
  155.4 30.3 %collective-permute-start.16 = (bf16[640,1024]{1,0:T(8,128)(2,1)}, bf16[640,1024]{1,0:T(8,128)(2,1)}, u32[]{:S(2)}, u32[]{:S(2)}) collective-permute-start(bf16[640,1024]{1,0:T(8,128)(2,1)} %collective-permute-done.14.refs_4_), channel_id=1, source_target_pairs={{0,4},{1,0},{2,1},{3,2},{4,5},{5,6},{6,7},{7,3},{8,12},{9,8},{10,9... | collective-permute-start | bytes 3932168 | tf_op jit(solution)/shard_map/ppermute | solution.py:59
  168.5 28.3 %all-to-all-start.3 = ((bf16[8,128,896]{2,1,0:T(8,128)(2,1)}), bf16[8,128,896]{2,1,0:T(8,128)(2,1)}, u32[]{:S(2)}, u32[]{:S(2)}) async-start(bf16[8,128,896]{2,1,0:T(8,128)(2,1)} %bitcast.47), calls=%async_computation.3 | async-start | bytes 3670016 | tf_op jit(solution)/shard_map/all_to_all | solution.py:538
  185.7 30.9 %collective-permute-start.17 = (bf16[640,1024]{1,0:T(8,128)(2,1)S(1)}, bf16[640,1024]{1,0:T(8,128)(2,1)S(1)}, u32[]{:S(2)}, u32[]{:S(2)}) collective-permute-start(bf16[640,1024]{1,0:T(8,128)(2,1)S(1)} %collective-permute-done.15.refs_2_), channel_id=1, source_target_pairs={{0,1},{1,2},{2,3},{3,7},{4,0},{5,4},{6,5},{7,6},{8,9},{9,10},{10,1... | collective-permute-start | bytes 3932168 | tf_op jit(solution)/shard_map/ppermute | solution.py:59
  187.7 30.5 %collective-permute-start.18 = (bf16[640,1024]{1,0:T(8,128)(2,1)}, bf16[640,1024]{1,0:T(8,128)(2,1)}, u32[]{:S(2)}, u32[]{:S(2)}) collective-permute-start(bf16[640,1024]{1,0:T(8,128)(2,1)} %collective-permute-done.16.refs_5_), channel_id=1, source_target_pairs={{0,4},{1,0},{2,1},{3,2},{4,5},{5,6},{6,7},{7,3},{8,12},{9,8},{10,9... | collective-permute-start | bytes 3932168 | tf_op jit(solution)/shard_map/ppermute | solution.py:59
  187.7 21.1 %collective-permute-start.19 = (bf16[512,896]{1,0:T(8,128)(2,1)}, bf16[512,896]{1,0:T(8,128)(2,1)}, u32[]{:S(2)}, u32[]{:S(2)}) collective-permute-start(bf16[512,896]{1,0:T(8,128)(2,1)} %get-tuple-element.82.refs_0_), channel_id=1, source_target_pairs={{0,4},{4,0},{8,12},{12,8},{16,20},{20,16},{24,28},{28,24},{1,5},{5... | collective-permute-start | bytes 2752520 | tf_op jit(solution)/shard_map/ppermute | solution.py:20
  187.9 21.0 %collective-permute-start.20 = (bf16[512,896]{1,0:T(8,128)(2,1)}, bf16[512,896]{1,0:T(8,128)(2,1)}, u32[]{:S(2)}, u32[]{:S(2)}) collective-permute-start(bf16[512,896]{1,0:T(8,128)(2,1)} %get-tuple-element.82.refs_0_), channel_id=1, source_target_pairs={{0,8},{4,20},{8,0},{12,28},{16,24},{20,4},{24,16},{28,12},{1,9},{5... | collective-permute-start | bytes 2752520 | tf_op jit(solution)/shard_map/ppermute | solution.py:80
  208.9 33.3 %collective-permute-start.22 = (bf16[512,896]{1,0:T(8,128)(2,1)}, bf16[512,896]{1,0:T(8,128)(2,1)S(1)}, u32[]{:S(2)}, u32[]{:S(2)}) collective-permute-start(bf16[512,896]{1,0:T(8,128)(2,1)} %get-tuple-element.90.refs_0_), channel_id=1, source_target_pairs={{0,8},{4,20},{8,0},{12,28},{16,24},{20,4},{24,16},{28,12},{1,9},{5... | collective-permute-start | bytes 2752520 | tf_op jit(solution)/shard_map/ppermute | solution.py:80
  209.4 32.9 %collective-permute-start.24 = (bf16[512,896]{1,0:T(8,128)(2,1)}, bf16[512,896]{1,0:T(8,128)(2,1)S(1)}, u32[]{:S(2)}, u32[]{:S(2)}) collective-permute-start(bf16[512,896]{1,0:T(8,128)(2,1)} %get-tuple-element.90.refs_0_), channel_id=1, source_target_pairs={{0,4},{4,0},{8,12},{12,8},{16,20},{20,16},{24,28},{28,24},{1,5},{5... | collective-permute-start | bytes 2752520 | tf_op jit(solution)/shard_map/ppermute | solution.py:20
  209.4 32.8 %collective-permute-start.21 = (bf16[512,896]{1,0:T(8,128)(2,1)}, bf16[512,896]{1,0:T(8,128)(2,1)S(1)}, u32[]{:S(2)}, u32[]{:S(2)}) collective-permute-start(bf16[512,896]{1,0:T(8,128)(2,1)} %collective-permute-done.19.refs_1_), channel_id=1, source_target_pairs={{0,8},{4,20},{8,0},{12,28},{16,24},{20,4},{24,16},{28,12},{1,9},{5... | collective-permute-start | bytes 2752520 | tf_op jit(solution)/shard_map/ppermute | solution.py:80
  216.6 25.7 %collective-permute-start.23 = (bf16[512,896]{1,0:T(8,128)(2,1)}, bf16[512,896]{1,0:T(8,128)(2,1)S(1)}, u32[]{:S(2)}, u32[]{:S(2)}) collective-permute-start(bf16[512,896]{1,0:T(8,128)(2,1)} %collective-permute-done.20.refs_2_), channel_id=1, source_target_pairs={{0,16},{4,12},{8,24},{12,4},{16,0},{20,28},{24,8},{28,20},{1,17},{... | collective-permute-start | bytes 2752520 | tf_op jit(solution)/shard_map/ppermute | solution.py:80
  242.9 22.9 %collective-permute-start.25 = (bf16[512,896]{1,0:T(8,128)(2,1)S(1)}, bf16[512,896]{1,0:T(8,128)(2,1)S(1)}, u32[]{:S(2)}, u32[]{:S(2)}) collective-permute-start(bf16[512,896]{1,0:T(8,128)(2,1)S(1)} %collective-permute-done.24.refs_1_), channel_id=1, source_target_pairs={{0,8},{4,20},{8,0},{12,28},{16,24},{20,4},{24,16},{28,12},{1,9},{5... | collective-permute-start | bytes 2752520 | tf_op jit(solution)/shard_map/ppermute | solution.py:80
  243.4 22.5 %collective-permute-start.26 = (bf16[512,896]{1,0:T(8,128)(2,1)S(1)}, bf16[512,896]{1,0:T(8,128)(2,1)S(1)}, u32[]{:S(2)}, u32[]{:S(2)}) collective-permute-start(bf16[512,896]{1,0:T(8,128)(2,1)S(1)} %collective-permute-done.22.refs_2_), channel_id=1, source_target_pairs={{0,16},{4,12},{8,24},{12,4},{16,0},{20,28},{24,8},{28,20},{1,17},{... | collective-permute-start | bytes 2752520 | tf_op jit(solution)/shard_map/ppermute | solution.py:80
  265.9 8.9 %collective-permute-start.30 = (bf16[512,896]{1,0:T(8,128)(2,1)S(1)}, bf16[512,896]{1,0:T(8,128)(2,1)S(1)}, u32[]{:S(2)}, u32[]{:S(2)}) collective-permute-start(bf16[512,896]{1,0:T(8,128)(2,1)S(1)} %collective-permute-done.22.refs_2_), channel_id=1, source_target_pairs={{0,4},{4,0},{8,12},{12,8},{16,20},{20,16},{24,28},{28,24},{1,5},{5... | collective-permute-start | bytes 2752520 | tf_op jit(solution)/shard_map/ppermute | solution.py:20
  266.0 8.8 %collective-permute-start.31 = (bf16[512,896]{1,0:T(8,128)(2,1)S(1)}, bf16[512,896]{1,0:T(8,128)(2,1)S(1)}, u32[]{:S(2)}, u32[]{:S(2)}) collective-permute-start(bf16[512,896]{1,0:T(8,128)(2,1)S(1)} %collective-permute-done.25.refs_3_), channel_id=1, source_target_pairs={{0,4},{4,0},{8,12},{12,8},{16,20},{20,16},{24,28},{28,24},{1,5},{5... | collective-permute-start | bytes 2752520 | tf_op jit(solution)/shard_map/ppermute | solution.py:20
  266.4 8.3 %collective-permute-start.32 = (bf16[512,896]{1,0:T(8,128)(2,1)S(1)}, bf16[512,896]{1,0:T(8,128)(2,1)S(1)}, u32[]{:S(2)}, u32[]{:S(2)}) collective-permute-start(bf16[512,896]{1,0:T(8,128)(2,1)S(1)} %collective-permute-done.26.refs_2_), channel_id=1, source_target_pairs={{0,4},{4,0},{8,12},{12,8},{16,20},{20,16},{24,28},{28,24},{1,5},{5... | collective-permute-start | bytes 2752520 | tf_op jit(solution)/shard_map/ppermute | solution.py:20
  (32 other events, 435.0 us)

commit v3 on v2

--- a/solution.py
+++ b/solution.py
@@ -97,31 +97,34 @@
     return lax.all_to_all(blocks, "fsdp", split_axis=0, concat_axis=0, tiled=True)
 
 
-def gather_all(block, rows, short, columns):
+def gather_all(block, rows, short, columns, index_of):
     high = axis_bits(lax.axis_size("fsdp"))
     weights = in_masks(spread(block, high + [1]))
     rows_a, rows_b = line_gather(rows)
     short = everywhere(short)
-    return weights, rows_a, rows_b, short, exchange_columns(columns)
-
-
-def gather_all_rounds(block, rows, short, columns):
+    return weights, rows_a, rows_b, index_of(short), exchange_columns(columns)
+
+
+def gather_all_rounds(block, rows, short, columns, index_of):
     x, y = axis_bits(lax.axis_size("fsdp"))
     a1, b1 = line_step(rows, rows)
     near = [by_core(block, x, y)]
     sibling = swap(block, "fsdp", 1)
-    ((a1, b1, *near, sibling, columns),) = together((a1, b1, *near, sibling, columns))
+    half = columns.shape[1] // 2
+    first, second = exchange_columns(columns[:, :half]), columns[:, half:]
+    ((a1, b1, *near, sibling, first, second),) = together((a1, b1, *near, sibling, first, second))
     near.append(by_core(sibling, x, y))
-    columns = exchange_columns(columns)
+    second = exchange_columns(second)
     a2, b2 = line_step(a1, b1)
-    ((a2, b2, *near, short, columns),) = together((a2, b2, *near, short, columns))
+    ((a2, b2, *near, short, second),) = together((a2, b2, *near, short, second))
     diagonal = by_core(near[0], y, x)
     a3, b3 = line_step(a2, b2)
     far = [swap(part, "fsdp", 1) for part in near]
-    short = everywhere(short)
-    ((a3, b3, diagonal, *far, short, columns),) = together((a3, b3, diagonal, *far, short, columns))
+    columns = jnp.concatenate([first, second], axis=1)
+    index = index_of(everywhere(short))
+    (a3, b3, diagonal, columns), far, index = together((a3, b3, diagonal, columns), far, index)
     weights = in_pairs([block, sibling], near, far, [diagonal, swap(diagonal, "fsdp", 1)])
-    return weights, [a1, a2, a3], [b1, b2, b3], short, columns
+    return weights, [a1, a2, a3], [b1, b2, b3], index, columns
 
 
 def line_copy(own, a, b, k, z, odd, view, spot, sem):
@@ -221,7 +224,7 @@
     )(place, slot, own, *rows_a, *rows_b, *pieces)
 
 
-def attend_kernel(heads, block, place_ref, seg_row, seg_col, cot_ref, in_ref, *refs):
+def attend_kernel(heads, block, abreast, place_ref, seg_row, seg_col, cot_ref, in_ref, *refs):
     out_ref, grad_ref, qkv, bias, dk_sum, dv_sum = refs
     size = HEAD_DIMENSION
     length = qkv.shape[0]
@@ -239,34 +242,57 @@
     values_t = values.T
     dk_sum[...] = jnp.zeros_like(dk_sum)
     dv_sum[...] = jnp.zeros_like(dv_sum)
-    for h in range(heads):
-        q_h = qkv[:, h * size : (h + 1) * size]
-        d_h = cot_ref[:, h * size : (h + 1) * size]
-        q_t = q_h.T
-        d_t = d_h.T
-        for start in range(0, length, block):
-            stop = start + block
-            scores = jnp.dot(keys[:stop], q_t[:, start:stop], preferred_element_type=jnp.float32)
-            scores = scores + bias[:stop, start:stop]
-            top = jnp.max(scores, axis=0, keepdims=True)
-            weights = jnp.exp2((scores - top) * (scale * math.log2(math.e)))
-            probs = weights * (1.0 / jnp.sum(weights, axis=0, keepdims=True))
-            probs_b = probs.astype(jnp.bfloat16)
-            out_t = jnp.dot(values_t[:, :stop], probs_b, preferred_element_type=jnp.float32).astype(
+    starts = list(range(0, length, block))
+    for first in range(0, heads, abreast):
+        items = [
+            (h, start, start + block)
+            for h in range(first, min(first + abreast, heads))
+            for start in starts
+        ]
+        q_t = {h: qkv[:, h * size : (h + 1) * size].T for h, _, _ in items}
+        d_t = {h: cot_ref[:, h * size : (h + 1) * size].T for h, _, _ in items}
+        scores = [
+            jnp.dot(keys[:stop], q_t[h][:, start:stop], preferred_element_type=jnp.float32)
+            + bias[:stop, start:stop]
+            for h, start, stop in items
+        ]
+        dprob = [
+            jnp.dot(values[:stop], d_t[h][:, start:stop], preferred_element_type=jnp.float32)
+            for h, start, stop in items
+        ]
+        top = [jnp.max(x, axis=0, keepdims=True) for x in scores]
+        weights = [
+            jnp.exp2((x - t) * (scale * math.log2(math.e))) for x, t in zip(scores, top)
+        ]
+        probs = [x * (1.0 / jnp.sum(x, axis=0, keepdims=True)) for x in weights]
+        probs_b = [x.astype(jnp.bfloat16) for x in probs]
+        out_t = [
+            jnp.dot(values_t[:, :stop], x, preferred_element_type=jnp.float32).astype(jnp.bfloat16)
+            for (_, _, stop), x in zip(items, probs_b)
+        ]
+        delta = [
+            jnp.sum(
+                d_t[h][:, start:stop].astype(jnp.float32) * x.astype(jnp.float32),
+                axis=0,
+                keepdims=True,
+            )
+            for (h, start, stop), x in zip(items, out_t)
+        ]
+        dscore = [
+            (p * (x - t)).astype(jnp.bfloat16) for p, x, t in zip(probs, dprob, delta)
+        ]
+        dq_t = [
+            (jnp.dot(keys_t[:, :stop], x, preferred_element_type=jnp.float32) * scale).astype(
                 jnp.bfloat16
             )
-            delta = jnp.sum(
-                d_t[:, start:stop].astype(jnp.float32) * out_t.astype(jnp.float32), axis=0, keepdims=True
-            )
-            dprob = jnp.dot(values[:stop], d_t[:, start:stop], preferred_element_type=jnp.float32)
-            dscore = (probs * (dprob - delta)).astype(jnp.bfloat16)
-            dq_t = (
-                jnp.dot(keys_t[:, :stop], dscore, preferred_element_type=jnp.float32) * scale
-            ).astype(jnp.bfloat16)
-            dk_sum[:stop] += jnp.dot(dscore, q_h[start:stop], preferred_element_type=jnp.float32)
-            dv_sum[:stop] += jnp.dot(probs_b, d_h[start:stop], preferred_element_type=jnp.float32)
-            out_ref[start:stop, h * size : (h + 1) * size] = out_t.T
-            grad_ref[start:stop, h * size : (h + 1) * size] = dq_t.T
+            for (_, _, stop), x in zip(items, dscore)
+        ]
+        for (h, start, stop), x, p, o, q in zip(items, dscore, probs_b, out_t, dq_t):
+            columns = slice(h * size, (h + 1) * size)
+            dk_sum[:stop] += jnp.dot(x, qkv[start:stop, columns], preferred_element_type=jnp.float32)
+            dv_sum[:stop] += jnp.dot(p, cot_ref[start:stop, columns], preferred_element_type=jnp.float32)
+            out_ref[start:stop, columns] = o.T
+            grad_ref[start:stop, columns] = q.T
     grad_ref[:, heads * size : (heads + 1) * size] = (dk_sum[...] * scale).astype(jnp.bfloat16)
     grad_ref[:, (heads + 1) * size : (heads + 2) * size] = dv_sum[...].astype(jnp.bfloat16)
 
@@ -276,8 +302,9 @@
     size = HEAD_DIMENSION
     heads = cols // size - 2
     length = cotangent.shape[0]
+    abreast = max(1, 5 * 512 * 512 // (length * length))
     return pl.pallas_call(
-        functools.partial(attend_kernel, heads, 256),
+        functools.partial(attend_kernel, heads, 256, abreast),
         grid=(1,),
         out_shape=[
             jax.ShapeDtypeStruct((length, heads * size), jnp.bfloat16),
@@ -328,8 +355,10 @@
             for g in range(sets):
                 at = k * sets + g
                 pick = (order == slot_ref[at : at + 1, :]).astype(jnp.bfloat16)
+                tok = rows_v.shape[3]
+                pieces = [rows_v[k, i] for i in range(g * span // tok, (g + 1) * span // tok)]
                 moved = lax.dot_general(
-                    rows_v[k, :, g * span : (g + 1) * span],
+                    jnp.concatenate(pieces, axis=1),
                     pick,
                     across,
                     preferred_element_type=jnp.float32,
@@ -346,9 +375,9 @@
 
 def pack_columns(place, slot, spot, own, rows_a, rows_b):
     packs, total = spot.shape
-    cols, count = own.shape
+    n_fsdp, cols, tok = own.shape
     n_seq = len(rows_a) + 1
-    tokens = n_seq * count
+    tokens = n_seq * n_fsdp * tok
     length = tokens // packs
     return pl.pallas_call(
         functools.partial(pack_kernel, n_seq),
@@ -362,7 +391,7 @@
         + [ANY] * (2 * n_seq - 1),
         out_specs=pl.BlockSpec((cols, length), lambda i: (0, i)),
         scratch_shapes=[
-            pltpu.VMEM((n_seq, cols, count), jnp.bfloat16),
+            pltpu.VMEM((n_seq, n_fsdp, cols, tok), jnp.bfloat16),
             pltpu.VMEM((packs, cols, total), jnp.bfloat16),
             pltpu.SemaphoreType.DMA((n_seq,)),
         ],
@@ -416,8 +445,6 @@
         old = [pltpu.make_async_copy(r, a, sem_o.at[i]) for i, (a, r) in enumerate(results(before))]
         for copy in old:
             copy.start()
-        for copy in old:
-            copy.wait()
     for j in range(steps):
         for copy in copies[j]:
             copy.wait()
@@ -425,6 +452,9 @@
             for copy in copies[j + 2]:
                 copy.start()
         part = jnp.dot(packed_v[j], d_v[j], preferred_element_type=jnp.float32)
+        if j == 0 and adds:
+            for copy in old:
+                copy.wait()
         if j == 0 and not adds:
             acc[...] = part
         else:
@@ -500,11 +530,7 @@
     high = axis_bits(n_fsdp)
     rounds = len(high) == 2 and n_seq == 4 and groups == 2
     gather = gather_all_rounds if rounds else gather_all
-    columns = jnp.swapaxes(hidden.reshape(tok_rows, n_fsdp, width // n_fsdp), 0, 1)
-    weights, rows_a, rows_b, dest, columns = gather(block, hidden, destination, columns)
-    columns = columns.reshape(n_fsdp * tok_rows, -1).T
-    mine = lax.dynamic_index_in_dim(dest, f, 0, keepdims=False)
-
+    columns = jnp.transpose(hidden.reshape(tok_rows, n_fsdp, width // n_fsdp), (1, 2, 0))
     each = n_seq * (2 * tok_rows // (n_fsdp * n_seq))
     order = jnp.arange(tok_rows, dtype=jnp.int32)
     earlier = order[:, None] < order[None, :]
@@ -516,21 +542,27 @@
     def from_here(x, axis):
         return lax.dynamic_slice_in_dim(jnp.concatenate([x, x], axis), z, n_seq, axis)
 
-    target = mine // length
-    slot = target * cap + jnp.arange(n_seq, dtype=jnp.int32)[:, None] * each + ranks(target)
-    slot = from_here(slot, 0).reshape(1, length)
-    target = dest // length
-    slots = target * each + ranks(target)
-    numbers = jnp.arange(n_fsdp * each, dtype=jnp.int32)
-    hit = slots[:, :, None, :] == numbers[None, None, :, None]
-    spots = jnp.sum(jnp.where(hit, (dest % length + 1)[:, :, None, :], 0), axis=-1) - 1
-    span = 128 // each
-    within = (jnp.arange(n_fsdp, dtype=jnp.int32) % span)[:, None, None]
-    slots = target * (span * each - each) + within * each + slots
-    spots = spots.reshape(n_fsdp, n_seq, n_fsdp, each)
-    place = lax.dynamic_index_in_dim(spots, f, 2, keepdims=False).reshape(1, n_fsdp * cap)
-    slots = jnp.swapaxes(from_here(slots, 1), 0, 1).reshape(-1, span * tok_rows)
-    spots = jnp.transpose(from_here(spots, 1), (2, 1, 0, 3)).reshape(n_fsdp, -1)
+    def index_of(dest):
+        mine = lax.dynamic_index_in_dim(dest, f, 0, keepdims=False)
+        target = mine // length
+        slot = target * cap + jnp.arange(n_seq, dtype=jnp.int32)[:, None] * each + ranks(target)
+        slot = from_here(slot, 0).reshape(1, length)
+        target = dest // length
+        slots = target * each + ranks(target)
+        numbers = jnp.arange(n_fsdp * each, dtype=jnp.int32)
+        hit = slots[:, :, None, :] == numbers[None, None, :, None]
+        spots = jnp.sum(jnp.where(hit, (dest % length + 1)[:, :, None, :], 0), axis=-1) - 1
+        span = 128 // each
+        within = (jnp.arange(n_fsdp, dtype=jnp.int32) % span)[:, None, None]
+        slots = target * (span * each - each) + within * each + slots
+        spots = spots.reshape(n_fsdp, n_seq, n_fsdp, each)
+        place = lax.dynamic_index_in_dim(spots, f, 2, keepdims=False).reshape(1, n_fsdp * cap)
+        slots = jnp.swapaxes(from_here(slots, 1), 0, 1).reshape(-1, span * tok_rows)
+        spots = jnp.transpose(from_here(spots, 1), (2, 1, 0, 3)).reshape(n_fsdp, -1)
+        return slot, place, slots, spots
+
+    weights, rows_a, rows_b, index, columns = gather(block, hidden, destination, columns, index_of)
+    slot, place, slots, spots = index
 
     def grads_of(packed, parts, group, before, adds=False):
         return gradients(here, packed, parts, group, groups, before, adds)
@@ -573,13 +605,14 @@
     f0 = [swap(n0, "fsdp", 1), swap(m0, "fsdp", 1)]
     e0 = swap(d0, "fsdp", 1)
     grads = grads_of(packed, in_pairs([g0, s0], [n0, m0], f0, [d0, e0]), 0, None)
-    ((m1, d1, n1, *grads),) = together((m1, d1, n1, *grads))
+    attn_out = jnp.concatenate([out0, out1], axis=1)
+    ((m1, d1, n1, attn_out, *grads),) = together((m1, d1, n1, attn_out, *grads))
     f1 = [swap(n1, "fsdp", 1), swap(m1, "fsdp", 1)]
     e1 = swap(d1, "fsdp", 1)
     parts = in_pairs([g1, s1], [n1, m1], f1, [d1, e1])
     grads = grads_of(packed, parts[:2], 1, grads)
     grads = grads_of(packed, parts[2:], 1, grads, True)
-    return (jnp.concatenate([out0, out1], axis=1), *grads)
+    return (attn_out, *grads)
 
 
 def solution(mesh):

time: 291 us -> 285 us (0.979); the launches traced: 285 us -> 283 us
  blocking collectives: 73.1 us -> 28.4 us
  waiting for transfers between devices: 68 us -> 95.8 us
  starting transfers between devices: 30.4 us -> 52.7 us
  Pallas kernels: 90 us -> 81.2 us
    all_to_all x0 -> x2, waiting for transfers between devices: none -> 45.9 us  [the longest x1 28.2 us: exchange_columns(): lax.all_to_all(blocks, 'fsdp', split_axis=0, concat_axis=0, tiled=True)]
    ppermute x6, waiting for transfers between devices: 43.4 us -> 8.07 us  [line_step(): lax.ppermute(a, ('fsdp', 'seq'), pairs(0))]
    all_to_all x1 -> x0, blocking collectives: 32 us -> none  [everywhere(): lax.all_to_all(sent, ('fsdp', 'seq'), split_axis=0, concat_axis=0, tiled=...]
    all_to_all x2, waiting for transfers between devices: 5.78 us -> 21.2 us  [on_device(): lax.all_to_all(x, 'fsdp', split_axis=0, concat_axis=0, tiled=True)]
    all_to_all x1, blocking collectives: 41.1 us -> 28.4 us  [exchange_columns(): lax.all_to_all(blocks, 'fsdp', split_axis=0, concat_axis=0, tiled=True)]
    all_to_all x0 -> x2, starting transfers between devices: none -> 9.22 us  [the longest x1 5.01 us: everywhere(): lax.all_to_all(sent, ('fsdp', 'seq'), split_axis=0, concat_axis=0, tiled=...]
    all_to_all x2, starting transfers between devices: 8.87 us -> 18.1 us  [on_device(): lax.all_to_all(x, 'fsdp', split_axis=0, concat_axis=0, tiled=True)]
    pallas_call x2, Pallas kernels: 23.9 us -> 15.9 us  [attend(): pl.pallas_call(functools.partial(attend_kernel, heads, 256, abreast), gri...]
  transfers between devices with their start and end apart: 35 -> 37, of which waited for: 10 -> 15; matrix products, arithmetic and copies ran while one was open for 5% -> 6% of each run, Pallas kernels for 29% -> 26%
where the time goes in v3:
time: 285 us; the launch traced here: 283 us
  waiting for transfers between devices  95.8 us (34%)
  Pallas kernels  81.2 us (28%)
  starting transfers between devices  52.7 us (18%)
  blocking collectives  28.4 us (10%)
  local copies, waits for them, and re-layouts  16.2 us (6%)
  other arithmetic  6.83 us (2%)
    all_to_all x1, blocking collectives, exchange_columns(): lax.all_to_all(blocks, 'fsdp', split_axis=0, concat_axis=0, tiled=True)  28.4 us
    all_to_all x1, waiting for transfers between devices, exchange_columns(): lax.all_to_all(blocks, 'fsdp', split_axis=0, concat_axis=0, tiled=True)  28.2 us
    pallas_call x3, Pallas kernels, gradients(): pl.pallas_call(functools.partial(grads_kernel, layout, group, adds, befor...  24.8 us
    pallas_call x2, Pallas kernels, project(): pl.pallas_call(functools.partial(project_kernel, n_seq, layout, cap, grou...  22.8 us
    all_to_all x2, waiting for transfers between devices, on_device(): lax.all_to_all(x, 'fsdp', split_axis=0, concat_axis=0, tiled=True)  21.2 us
    all_to_all x2, starting transfers between devices, on_device(): lax.all_to_all(x, 'fsdp', split_axis=0, concat_axis=0, tiled=True)  18.1 us
    all_to_all x1, waiting for transfers between devices, everywhere(): lax.all_to_all(sent, ('fsdp', 'seq'), split_axis=0, concat_axis=0, tiled=...  17.7 us
    pallas_call x1, Pallas kernels, pack_columns(): pl.pallas_call(functools.partial(pack_kernel, n_seq), grid=(packs,), out_...  17.7 us
  transfers between devices with their start and end apart: 37, of which 15 were waited for; matrix products, arithmetic and copies ran while one was open for 6% of the time, Pallas kernels for 26%

profile of v3, /device:TPU:0, one launch (start us, length us, event | category | flops | bytes accessed | tf_op | source)
XLA Modules:
  0.0 282.6 jit_solution(10883061544148233582)
XLA Ops:
  4.2 3.0 %collective-permute-start.2 = (bf16[640,1792]{1,0:T(8,128)(2,1)S(1)}, bf16[640,1792]{1,0:T(8,128)(2,1)}, u32[]{:S(2)}, u32[]{:S(2)}) collective-permute-start(bf16[640,1792]{1,0:T(8,128)(2,1)S(1)} %slice_dynamic-update-slice_fusion.2.refs_7_), channel_id=1, source_target_pairs={{0,8},{4,20},{8,0},{12,28},{16,24},{20,4},{24,16},{28,12},{1,9},{5... | collective-permute-start | bytes 6881288 | tf_op jit(solution)/shard_map/ppermute | solution.py:80
  8.8 2.4 copy.42
  11.3 2.2 fusion.10
  13.5 28.4 %all_to_all.40 = bf16[8,320,128]{2,1,0:T(8,128)(2,1)S(1)} all-to-all(bf16[8,320,128]{2,1,0:T(8,128)(2,1)S(1)} %get-tuple-element.123), channel_id=1, replica_groups=mesh['fsdp'=8,'seq'=4] {'fsdp'}, dimensions={0} | all-to-all | bytes 1310720 | tf_op jit(solution)/shard_map/all_to_all | solution.py:97
  44.8 4.2 %all-to-all-start.1 = ((bf16[8,320,128]{2,1,0:T(8,128)(2,1)}), bf16[8,320,128]{2,1,0:T(8,128)(2,1)}, u32[]{:S(2)}, u32[]{:S(2)}) async-start(bf16[8,320,128]{2,1,0:T(8,128)(2,1)} %get-tuple-element.67), calls=%async_computation.1 | async-start | bytes 1310720 | tf_op jit(solution)/shard_map/all_to_all | solution.py:97
  49.1 28.2 %all-to-all-done.1 = bf16[8,320,128]{2,1,0:T(8,128)(2,1)} async-done(((bf16[8,320,128]{2,1,0:T(8,128)(2,1)}), bf16[8,320,128]{2,1,0:T(8,128)(2,1)}, u32[]{:S(2)}, u32[]{:S(2)}) %all-to-all-start.1) | async-done | bytes 655392 | tf_op jit(solution)/shard_map/all_to_all | solution.py:97
  77.4 1.7 collective-permute-start.9
  79.7 5.0 %all-to-all-start.2 = ((s32[32,1,128]{2,1,0:T(1,128)}), s32[32,1,128]{2,1,0:T(1,128)S(1)}, u32[]{:S(2)}, u32[]{:S(2)}) async-start(s32[32,1,128]{2,1,0:T(1,128)} %broadcast_in_dim.10), calls=%async_computation.2 | async-start | bytes 32768 | tf_op jit(solution)/shard_map/all_to_all | solution.py:74
  84.7 1.8 collective-permute-start.7
  86.5 2.2 pad_maximum_fusion.refs_0_
  88.7 17.7 %all-to-all-done.2 = s32[32,1,128]{2,1,0:T(1,128)S(1)} async-done(((s32[32,1,128]{2,1,0:T(1,128)}), s32[32,1,128]{2,1,0:T(1,128)S(1)}, u32[]{:S(2)}, u32[]{:S(2)}) %all-to-all-start.2) | async-done | bytes 16416 | tf_op jit(solution)/shard_map/all_to_all | solution.py:74
  112.0 3.2 %collective-permute-done.7.refs_3_ = bf16[128,5120]{1,0:T(8,128)(2,1)} collective-permute-done((bf16[128,5120]{1,0:T(8,128)(2,1)}, bf16[128,5120]{1,0:T(8,128)(2,1)}, u32[]{:S(2)}, u32[]{:S(2)}) %collective-permute-start.7) | collective-permute-done | bytes 1310752 | tf_op jit(solution)/shard_map/ppermute | solution.py:59
  116.9 1.7 collective-permute-start.12
  118.6 2.3 collective-permute-done.14.refs_14_
  122.3 11.4 %project.2 = bf16[1024,896]{1,0:T(8,128)(2,1)} custom-call(s32[2]{0:T(128)} %pad_add_fusion.1.me_ref, s32[1,512]{1,0:T(1,128)} %bitcast.47, bf16[128,5120]{1,0:T(8,128)(2,1)} %refs_0_.3, bf16[128,5120]{1,0:T(8,128)(2,1)} %collective-permute-done.refs_1_, bf16[128,5120]{1,0:T(8,128)(2,1)} %collective-permute-done.4.refs_2_, ...), custom_call_target="tpu_custom_call" | custom-call | flops 5637144576 | bytes 16252928 | tf_op jit(solution)/shard_map/project/pallas_call | solution.py:205
  133.7 13.7 %all-to-all-start.3 = ((bf16[8,128,896]{2,1,0:T(8,128)(2,1)}), bf16[8,128,896]{2,1,0:T(8,128)(2,1)S(1)}, u32[]{:S(2)}, u32[]{:S(2)}) async-start(bf16[8,128,896]{2,1,0:T(8,128)(2,1)} %bitcast.41), calls=%async_computation.3 | async-start | bytes 3670016 | tf_op jit(solution)/shard_map/all_to_all | solution.py:570
  148.4 1.8 collective-permute-start.15
  150.2 11.4 %project.3 = bf16[1024,896]{1,0:T(8,128)(2,1)} custom-call(s32[2]{0:T(128)} %pad_add_fusion.1.me_ref, s32[1,512]{1,0:T(1,128)} %bitcast.48, bf16[128,5120]{1,0:T(8,128)(2,1)} %refs_0_.3, bf16[128,5120]{1,0:T(8,128)(2,1)} %collective-permute-done.refs_1_, bf16[128,5120]{1,0:T(8,128)(2,1)} %collective-permute-done.4.refs_2_, ...), custom_call_target="tpu_custom_call" | custom-call | flops 5637144576 | bytes 16252928 | tf_op jit(solution)/shard_map/project/pallas_call | solution.py:205
  161.6 9.6 %all-to-all-done.3 = bf16[8,128,896]{2,1,0:T(8,128)(2,1)S(1)} async-done(((bf16[8,128,896]{2,1,0:T(8,128)(2,1)}), bf16[8,128,896]{2,1,0:T(8,128)(2,1)S(1)}, u32[]{:S(2)}, u32[]{:S(2)}) %all-to-all-start.3) | async-done | bytes 1835040 | tf_op jit(solution)/shard_map/all_to_all | solution.py:570
  171.2 4.3 %all-to-all-start.4 = ((bf16[8,128,896]{2,1,0:T(8,128)(2,1)}), bf16[8,128,896]{2,1,0:T(8,128)(2,1)}, u32[]{:S(2)}, u32[]{:S(2)}) async-start(bf16[8,128,896]{2,1,0:T(8,128)(2,1)} %bitcast.40), calls=%async_computation.4 | async-start | bytes 3670016 | tf_op jit(solution)/shard_map/all_to_all | solution.py:570
  176.4 8.0 %attend.2 = (bf16[512,640]{1,0:T(8,128)(2,1)}, bf16[512,896]{1,0:T(8,128)(2,1)}) custom-call(s32[1,1024]{1,0:T(1,128)} %reshape.234.place_ref, s32[1,512]{1,0:T(1,128)} %seg_row.3, s32[512,1]{1,0:T(8,128)} %copy.47.seg_col, bf16[512,1280]{1,0:T(8,128)(2,1)} %cot_ref.3, bf16[1024,896]{1,0:T(8,128)(2,1)} %bitcast.43), custom_call_target="tpu_custom_call" | custom-call | flops 2952790016 | bytes 4587520 | tf_op jit(solution)/shard_map/attend/pallas_call | solution.py:306
  187.9 11.6 %all-to-all-done.4 = bf16[8,128,896]{2,1,0:T(8,128)(2,1)} async-done(((bf16[8,128,896]{2,1,0:T(8,128)(2,1)}), bf16[8,128,896]{2,1,0:T(8,128)(2,1)}, u32[]{:S(2)}, u32[]{:S(2)}) %all-to-all-start.4) | async-done | bytes 1835040 | tf_op jit(solution)/shard_map/all_to_all | solution.py:570
  199.5 7.9 %attend.3 = (bf16[512,640]{1,0:T(8,128)(2,1)}, bf16[512,896]{1,0:T(8,128)(2,1)}) custom-call(s32[1,1024]{1,0:T(1,128)} %reshape.234.place_ref, s32[1,512]{1,0:T(1,128)} %seg_row.3, s32[512,1]{1,0:T(8,128)} %copy.47.seg_col, bf16[512,1280]{1,0:T(8,128)(2,1)} %cot_ref.3, bf16[1024,896]{1,0:T(8,128)(2,1)} %bitcast.14.in_ref), custom_call_target="tpu_custom_call" | custom-call | flops 2952790016 | bytes 4587520 | tf_op jit(solution)/shard_map/attend/pallas_call | solution.py:306
  208.7 1.7 collective-permute-start.21
  210.4 4.6 %collective-permute-done.17.refs_3_ = bf16[8,640,128]{2,1,0:T(8,128)(2,1)S(1)} collective-permute-done((bf16[8,640,128]{2,1,0:T(8,128)(2,1)S(1)}, bf16[8,640,128]{2,1,0:T(8,128)(2,1)S(1)}, u32[]{:S(2)}, u32[]{:S(2)}) %collective-permute-start.17) | collective-permute-done | bytes 1310752 | tf_op jit(solution)/shard_map/ppermute | solution.py:59
  215.0 1.7 collective-permute-start.23
  216.7 17.7 %pack_columns.1.packed_ref = bf16[640,4096]{1,0:T(8,128)(2,1)} custom-call(s32[2]{0:T(128)} %pad_add_fusion.1.me_ref, s32[8,512]{1,0:T(8,128)} %reshape.235.slot_ref, s32[8,1024]{1,0:T(8,128)} %reshape.236.spot_ref, bf16[8,640,128]{2,1,0:T(8,128)(2,1)} %pad_maximum_fusion.refs_0_, bf16[8,640,128]{2,1,0:T(8,128)(2,1)} %collective-permute-done.12.refs_1_, ...), custom_call_target="tpu_custom_call" | custom-call | flops 10737418240 | bytes 10485760 | tf_op jit(solution)/shard_map/pack_columns/pallas_call | solution.py:382
  234.4 7.4 %collective-permute-done.21.refs_3_ = bf16[512,896]{1,0:T(8,128)(2,1)} collective-permute-done((bf16[512,896]{1,0:T(8,128)(2,1)}, bf16[512,896]{1,0:T(8,128)(2,1)}, u32[]{:S(2)}, u32[]{:S(2)}) %collective-permute-start.21) | collective-permute-done | bytes 917536 | tf_op jit(solution)/shard_map/ppermute | solution.py:80
  248.1 10.1 %gradients.3 = (f32[640,1280]{1,0:T(8,128)}, f32[640,256]{1,0:T(8,128)}, f32[640,256]{1,0:T(8,128)}) custom-call(s32[2]{0:T(128)} %pad_add_fusion.1.me_ref, bf16[640,4096]{1,0:T(8,128)(2,1)} %pack_columns.1.packed_ref, bf16[512,896]{1,0:T(8,128)(2,1)} %get-tuple-element.92.refs_0_, bf16[512,896]{1,0:T(8,128)(2,1)} %collective-permute-done.19.refs_1_, ...), custom_call_target="tpu_custom_call" | custom-call | flops 4697620480 | bytes 14876672 | tf_op jit(solution)/shard_map/gradients/pallas_call | solution.py:485
  258.3 6.8 %collective-permute-done.25.refs_3_ = bf16[512,896]{1,0:T(8,128)(2,1)S(1)} collective-permute-done((bf16[512,896]{1,0:T(8,128)(2,1)S(1)}, bf16[512,896]{1,0:T(8,128)(2,1)S(1)}, u32[]{:S(2)}, u32[]{:S(2)}) %collective-permute-start.25) | collective-permute-done | bytes 917536 | tf_op jit(solution)/shard_map/ppermute | solution.py:80
  266.0 7.0 %gradients.4 = (f32[640,1280]{1,0:T(8,128)}, f32[640,256]{1,0:T(8,128)}, f32[640,256]{1,0:T(8,128)}) custom-call(s32[2]{0:T(128)} %pad_add_fusion.1.me_ref, bf16[640,4096]{1,0:T(8,128)(2,1)} %pack_columns.1.packed_ref, bf16[512,896]{1,0:T(8,128)(2,1)} %get-tuple-element.97.refs_0_, ...), custom_call_target="tpu_custom_call", output_to_operand_aliasing={{0}: (6, {}), {1}: (7, {}), {2}: (8, {})} | custom-call | flops 2348810240 | bytes 8585216 | tf_op jit(solution)/shard_map/gradients/pallas_call | solution.py:485
  274.6 7.6 %gradients.5 = (f32[640,1280]{1,0:T(8,128)}, f32[640,256]{1,0:T(8,128)}, f32[640,256]{1,0:T(8,128)}) custom-call(s32[2]{0:T(128)} %pad_add_fusion.1.me_ref, bf16[640,4096]{1,0:T(8,128)(2,1)} %pack_columns.1.packed_ref, bf16[512,896]{1,0:T(8,128)(2,1)} %copy-done.9, ...), custom_call_target="tpu_custom_call", output_to_operand_aliasing={{0}: (6, {}), {1}: (7, {}), {2}: (8, {})} | custom-call | flops 2348810240 | bytes 8585216 | tf_op jit(solution)/shard_map/gradients/pallas_call | solution.py:485
  (133 shorter events, 32.7 us)
Async XLA Ops:
  4.2 37.6 %collective-permute-start.2 = (bf16[640,1792]{1,0:T(8,128)(2,1)S(1)}, bf16[640,1792]{1,0:T(8,128)(2,1)}, u32[]{:S(2)}, u32[]{:S(2)}) collective-permute-start(bf16[640,1792]{1,0:T(8,128)(2,1)S(1)} %slice_dynamic-update-slice_fusion.2.refs_7_), channel_id=1, source_target_pairs={{0,8},{4,20},{8,0},{12,28},{16,24},{20,4},{24,16},{28,12},{1,9},{5... | collective-permute-start | bytes 6881288 | tf_op jit(solution)/shard_map/ppermute | solution.py:80
  7.2 34.6 %collective-permute-start.3 = (bf16[640,1792]{1,0:T(8,128)(2,1)S(1)}, bf16[640,1792]{1,0:T(8,128)(2,1)}, u32[]{:S(2)}, u32[]{:S(2)}) collective-permute-start(bf16[640,1792]{1,0:T(8,128)(2,1)S(1)} %slice_dynamic-update-slice_fusion.2.refs_7_), channel_id=1, source_target_pairs={{0,4},{4,0},{8,12},{12,8},{16,20},{20,16},{24,28},{28,24},{1,5},{5... | collective-permute-start | bytes 6881288 | tf_op jit(solution)/shard_map/ppermute | solution.py:20
  7.2 34.6 %collective-permute-start = (bf16[128,5120]{1,0:T(8,128)(2,1)}, bf16[128,5120]{1,0:T(8,128)(2,1)}, u32[]{:S(2)}, u32[]{:S(2)}) collective-permute-start(bf16[128,5120]{1,0:T(8,128)(2,1)} %refs_0_.3), channel_id=1, source_target_pairs={{0,1},{1,2},{2,3},{3,7},{4,0},{5,4},{6,5},{7,6},{8,9},{9,10},{10,1... | collective-permute-start | bytes 3932168 | tf_op jit(solution)/shard_map/ppermute | solution.py:59
  8.8 33.1 %collective-permute-start.1 = (bf16[128,5120]{1,0:T(8,128)(2,1)}, bf16[128,5120]{1,0:T(8,128)(2,1)}, u32[]{:S(2)}, u32[]{:S(2)}) collective-permute-start(bf16[128,5120]{1,0:T(8,128)(2,1)} %refs_0_.3), channel_id=1, source_target_pairs={{0,4},{1,0},{2,1},{3,2},{4,5},{5,6},{6,7},{7,3},{8,12},{9,8},{10,9... | collective-permute-start | bytes 3932168 | tf_op jit(solution)/shard_map/ppermute | solution.py:59
  41.9 35.4 %collective-permute-start.6 = (bf16[640,1792]{1,0:T(8,128)(2,1)}, bf16[640,1792]{1,0:T(8,128)(2,1)S(1)}, u32[]{:S(2)}, u32[]{:S(2)}) collective-permute-start(bf16[640,1792]{1,0:T(8,128)(2,1)} %collective-permute-done.3.refs_8_), channel_id=1, source_target_pairs={{0,8},{4,20},{8,0},{12,28},{16,24},{20,4},{24,16},{28,12},{1,9},{5... | collective-permute-start | bytes 6881288 | tf_op jit(solution)/shard_map/ppermute | solution.py:80
  43.3 34.0 %collective-permute-start.4 = (bf16[128,5120]{1,0:T(8,128)(2,1)}, bf16[128,5120]{1,0:T(8,128)(2,1)}, u32[]{:S(2)}, u32[]{:S(2)}) collective-permute-start(bf16[128,5120]{1,0:T(8,128)(2,1)} %collective-permute-done.refs_1_), channel_id=1, source_target_pairs={{0,1},{1,2},{2,3},{3,7},{4,0},{5,4},{6,5},{7,6},{8,9},{9,10},{10,1... | collective-permute-start | bytes 3932168 | tf_op jit(solution)/shard_map/ppermute | solution.py:59
  44.8 32.4 %collective-permute-start.5 = (bf16[128,5120]{1,0:T(8,128)(2,1)}, bf16[128,5120]{1,0:T(8,128)(2,1)}, u32[]{:S(2)}, u32[]{:S(2)}) collective-permute-start(bf16[128,5120]{1,0:T(8,128)(2,1)} %collective-permute-done.1.refs_4_), channel_id=1, source_target_pairs={{0,4},{1,0},{2,1},{3,2},{4,5},{5,6},{6,7},{7,3},{8,12},{9,8},{10,9... | collective-permute-start | bytes 3932168 | tf_op jit(solution)/shard_map/ppermute | solution.py:59
  44.8 32.4 %all-to-all-start.1 = ((bf16[8,320,128]{2,1,0:T(8,128)(2,1)}), bf16[8,320,128]{2,1,0:T(8,128)(2,1)}, u32[]{:S(2)}, u32[]{:S(2)}) async-start(bf16[8,320,128]{2,1,0:T(8,128)(2,1)} %get-tuple-element.67), calls=%async_computation.1 | async-start | bytes 1310720 | tf_op jit(solution)/shard_map/all_to_all | solution.py:97
  77.3 38.9 %collective-permute-start.10 = (bf16[640,1792]{1,0:T(8,128)(2,1)}, bf16[640,1792]{1,0:T(8,128)(2,1)}, u32[]{:S(2)}, u32[]{:S(2)}) collective-permute-start(bf16[640,1792]{1,0:T(8,128)(2,1)} %collective-permute-done.2.refs_9_), channel_id=1, source_target_pairs={{0,4},{4,0},{8,12},{12,8},{16,20},{20,16},{24,28},{28,24},{1,5},{5... | collective-permute-start | bytes 6881288 | tf_op jit(solution)/shard_map/ppermute | solution.py:20
  77.4 38.8 %collective-permute-start.9 = (bf16[640,1792]{1,0:T(8,128)(2,1)}, bf16[640,1792]{1,0:T(8,128)(2,1)}, u32[]{:S(2)}, u32[]{:S(2)}) collective-permute-start(bf16[640,1792]{1,0:T(8,128)(2,1)} %collective-permute-done.2.refs_9_), channel_id=1, source_target_pairs={{0,16},{4,12},{8,24},{12,4},{16,0},{20,28},{24,8},{28,20},{1,17},{... | collective-permute-start | bytes 6881288 | tf_op jit(solution)/shard_map/ppermute | solution.py:80
  79.1 37.1 %collective-permute-start.11 = (bf16[640,1792]{1,0:T(8,128)(2,1)S(1)}, bf16[640,1792]{1,0:T(8,128)(2,1)}, u32[]{:S(2)}, u32[]{:S(2)}) collective-permute-start(bf16[640,1792]{1,0:T(8,128)(2,1)S(1)} %collective-permute-done.6.refs_10_), channel_id=1, source_target_pairs={{0,4},{4,0},{8,12},{12,8},{16,20},{20,16},{24,28},{28,24},{1,5},{5... | collective-permute-start | bytes 6881288 | tf_op jit(solution)/shard_map/ppermute | solution.py:20
  79.7 26.8 %all-to-all-start.2 = ((s32[32,1,128]{2,1,0:T(1,128)}), s32[32,1,128]{2,1,0:T(1,128)S(1)}, u32[]{:S(2)}, u32[]{:S(2)}) async-start(s32[32,1,128]{2,1,0:T(1,128)} %broadcast_in_dim.10), calls=%async_computation.2 | async-start | bytes 32768 | tf_op jit(solution)/shard_map/all_to_all | solution.py:74
  84.7 30.5 %collective-permute-start.7 = (bf16[128,5120]{1,0:T(8,128)(2,1)}, bf16[128,5120]{1,0:T(8,128)(2,1)}, u32[]{:S(2)}, u32[]{:S(2)}) collective-permute-start(bf16[128,5120]{1,0:T(8,128)(2,1)} %collective-permute-done.4.refs_2_), channel_id=1, source_target_pairs={{0,1},{1,2},{2,3},{3,7},{4,0},{5,4},{6,5},{7,6},{8,9},{9,10},{10,1... | collective-permute-start | bytes 3932168 | tf_op jit(solution)/shard_map/ppermute | solution.py:59
  86.5 29.7 %collective-permute-start.8 = (bf16[128,5120]{1,0:T(8,128)(2,1)}, bf16[128,5120]{1,0:T(8,128)(2,1)}, u32[]{:S(2)}, u32[]{:S(2)}) collective-permute-start(bf16[128,5120]{1,0:T(8,128)(2,1)} %collective-permute-done.5.refs_5_), channel_id=1, source_target_pairs={{0,4},{1,0},{2,1},{3,2},{4,5},{5,6},{6,7},{7,3},{8,12},{9,8},{10,9... | collective-permute-start | bytes 3932168 | tf_op jit(solution)/shard_map/ppermute | solution.py:59
  116.9 30.8 %collective-permute-start.12 = (bf16[8,640,128]{2,1,0:T(8,128)(2,1)}, bf16[8,640,128]{2,1,0:T(8,128)(2,1)}, u32[]{:S(2)}, u32[]{:S(2)}) collective-permute-start(bf16[8,640,128]{2,1,0:T(8,128)(2,1)} %pad_maximum_fusion.refs_0_), channel_id=1, source_target_pairs={{0,1},{1,2},{2,3},{3,7},{4,0},{5,4},{6,5},{7,6},{8,9},{9,10},{10,1... | collective-permute-start | bytes 3932168 | tf_op jit(solution)/shard_map/ppermute | solution.py:59
  118.6 29.8 %collective-permute-start.13 = (bf16[8,640,128]{2,1,0:T(8,128)(2,1)}, bf16[8,640,128]{2,1,0:T(8,128)(2,1)}, u32[]{:S(2)}, u32[]{:S(2)}) collective-permute-start(bf16[8,640,128]{2,1,0:T(8,128)(2,1)} %pad_maximum_fusion.refs_0_), channel_id=1, source_target_pairs={{0,4},{1,0},{2,1},{3,2},{4,5},{5,6},{6,7},{7,3},{8,12},{9,8},{10,9... | collective-permute-start | bytes 3932168 | tf_op jit(solution)/shard_map/ppermute | solution.py:59
  133.7 37.5 %all-to-all-start.3 = ((bf16[8,128,896]{2,1,0:T(8,128)(2,1)}), bf16[8,128,896]{2,1,0:T(8,128)(2,1)S(1)}, u32[]{:S(2)}, u32[]{:S(2)}) async-start(bf16[8,128,896]{2,1,0:T(8,128)(2,1)} %bitcast.41), calls=%async_computation.3 | async-start | bytes 3670016 | tf_op jit(solution)/shard_map/all_to_all | solution.py:570
  148.4 36.0 %collective-permute-start.15 = (bf16[8,640,128]{2,1,0:T(8,128)(2,1)}, bf16[8,640,128]{2,1,0:T(8,128)(2,1)S(1)}, u32[]{:S(2)}, u32[]{:S(2)}) collective-permute-start(bf16[8,640,128]{2,1,0:T(8,128)(2,1)} %collective-permute-done.12.refs_1_), channel_id=1, source_target_pairs={{0,1},{1,2},{2,3},{3,7},{4,0},{5,4},{6,5},{7,6},{8,9},{9,10},{10,1... | collective-permute-start | bytes 3932168 | tf_op jit(solution)/shard_map/ppermute | solution.py:59
  150.2 34.3 %collective-permute-start.16 = (bf16[8,640,128]{2,1,0:T(8,128)(2,1)}, bf16[8,640,128]{2,1,0:T(8,128)(2,1)}, u32[]{:S(2)}, u32[]{:S(2)}) collective-permute-start(bf16[8,640,128]{2,1,0:T(8,128)(2,1)} %collective-permute-done.13.refs_4_), channel_id=1, source_target_pairs={{0,4},{1,0},{2,1},{3,2},{4,5},{5,6},{6,7},{7,3},{8,12},{9,8},{10,9... | collective-permute-start | bytes 3932168 | tf_op jit(solution)/shard_map/ppermute | solution.py:59
  171.2 28.3 %all-to-all-start.4 = ((bf16[8,128,896]{2,1,0:T(8,128)(2,1)}), bf16[8,128,896]{2,1,0:T(8,128)(2,1)}, u32[]{:S(2)}, u32[]{:S(2)}) async-start(bf16[8,128,896]{2,1,0:T(8,128)(2,1)} %bitcast.40), calls=%async_computation.4 | async-start | bytes 3670016 | tf_op jit(solution)/shard_map/all_to_all | solution.py:570
  184.4 30.5 %collective-permute-start.17 = (bf16[8,640,128]{2,1,0:T(8,128)(2,1)S(1)}, bf16[8,640,128]{2,1,0:T(8,128)(2,1)S(1)}, u32[]{:S(2)}, u32[]{:S(2)}) collective-permute-start(bf16[8,640,128]{2,1,0:T(8,128)(2,1)S(1)} %collective-permute-done.15.refs_2_), channel_id=1, source_target_pairs={{0,1},{1,2},{2,3},{3,7},{4,0},{5,4},{6,5},{7,6},{8,9},{9,10},{10,1... | collective-permute-start | bytes 3932168 | tf_op jit(solution)/shard_map/ppermute | solution.py:59
  186.0 30.7 %collective-permute-start.18 = (bf16[8,640,128]{2,1,0:T(8,128)(2,1)}, bf16[8,640,128]{2,1,0:T(8,128)(2,1)}, u32[]{:S(2)}, u32[]{:S(2)}) collective-permute-start(bf16[8,640,128]{2,1,0:T(8,128)(2,1)} %collective-permute-done.16.refs_5_), channel_id=1, source_target_pairs={{0,4},{1,0},{2,1},{3,2},{4,5},{5,6},{6,7},{7,3},{8,12},{9,8},{10,9... | collective-permute-start | bytes 3932168 | tf_op jit(solution)/shard_map/ppermute | solution.py:59
  186.0 21.4 %collective-permute-start.19 = (bf16[512,896]{1,0:T(8,128)(2,1)}, bf16[512,896]{1,0:T(8,128)(2,1)}, u32[]{:S(2)}, u32[]{:S(2)}) collective-permute-start(bf16[512,896]{1,0:T(8,128)(2,1)} %get-tuple-element.92.refs_0_), channel_id=1, source_target_pairs={{0,4},{4,0},{8,12},{12,8},{16,20},{20,16},{24,28},{28,24},{1,5},{5... | collective-permute-start | bytes 2752520 | tf_op jit(solution)/shard_map/ppermute | solution.py:20
  186.3 22.1 %collective-permute-start.20 = (bf16[512,896]{1,0:T(8,128)(2,1)}, bf16[512,896]{1,0:T(8,128)(2,1)}, u32[]{:S(2)}, u32[]{:S(2)}) collective-permute-start(bf16[512,896]{1,0:T(8,128)(2,1)} %get-tuple-element.92.refs_0_), channel_id=1, source_target_pairs={{0,8},{4,20},{8,0},{12,28},{16,24},{20,4},{24,16},{28,12},{1,9},{5... | collective-permute-start | bytes 2752520 | tf_op jit(solution)/shard_map/ppermute | solution.py:80
  208.4 33.4 %collective-permute-start.22 = (bf16[512,896]{1,0:T(8,128)(2,1)}, bf16[512,896]{1,0:T(8,128)(2,1)S(1)}, u32[]{:S(2)}, u32[]{:S(2)}) collective-permute-start(bf16[512,896]{1,0:T(8,128)(2,1)} %get-tuple-element.97.refs_0_), channel_id=1, source_target_pairs={{0,8},{4,20},{8,0},{12,28},{16,24},{20,4},{24,16},{28,12},{1,9},{5... | collective-permute-start | bytes 2752520 | tf_op jit(solution)/shard_map/ppermute | solution.py:80
  208.7 33.0 %collective-permute-start.24 = (bf16[512,896]{1,0:T(8,128)(2,1)}, bf16[512,896]{1,0:T(8,128)(2,1)S(1)}, u32[]{:S(2)}, u32[]{:S(2)}) collective-permute-start(bf16[512,896]{1,0:T(8,128)(2,1)} %get-tuple-element.97.refs_0_), channel_id=1, source_target_pairs={{0,4},{4,0},{8,12},{12,8},{16,20},{20,16},{24,28},{28,24},{1,5},{5... | collective-permute-start | bytes 2752520 | tf_op jit(solution)/shard_map/ppermute | solution.py:20
  208.7 33.0 %collective-permute-start.21 = (bf16[512,896]{1,0:T(8,128)(2,1)}, bf16[512,896]{1,0:T(8,128)(2,1)}, u32[]{:S(2)}, u32[]{:S(2)}) collective-permute-start(bf16[512,896]{1,0:T(8,128)(2,1)} %collective-permute-done.19.refs_1_), channel_id=1, source_target_pairs={{0,8},{4,20},{8,0},{12,28},{16,24},{20,4},{24,16},{28,12},{1,9},{5... | collective-permute-start | bytes 2752520 | tf_op jit(solution)/shard_map/ppermute | solution.py:80
  215.0 26.8 %collective-permute-start.23 = (bf16[512,896]{1,0:T(8,128)(2,1)}, bf16[512,896]{1,0:T(8,128)(2,1)S(1)}, u32[]{:S(2)}, u32[]{:S(2)}) collective-permute-start(bf16[512,896]{1,0:T(8,128)(2,1)} %collective-permute-done.20.refs_2_), channel_id=1, source_target_pairs={{0,16},{4,12},{8,24},{12,4},{16,0},{20,28},{24,8},{28,20},{1,17},{... | collective-permute-start | bytes 2752520 | tf_op jit(solution)/shard_map/ppermute | solution.py:80
  242.4 22.6 %collective-permute-start.25 = (bf16[512,896]{1,0:T(8,128)(2,1)S(1)}, bf16[512,896]{1,0:T(8,128)(2,1)S(1)}, u32[]{:S(2)}, u32[]{:S(2)}) collective-permute-start(bf16[512,896]{1,0:T(8,128)(2,1)S(1)} %collective-permute-done.24.refs_1_), channel_id=1, source_target_pairs={{0,8},{4,20},{8,0},{12,28},{16,24},{20,4},{24,16},{28,12},{1,9},{5... | collective-permute-start | bytes 2752520 | tf_op jit(solution)/shard_map/ppermute | solution.py:80
  242.8 22.3 %collective-permute-start.26 = (bf16[512,896]{1,0:T(8,128)(2,1)S(1)}, bf16[512,896]{1,0:T(8,128)(2,1)S(1)}, u32[]{:S(2)}, u32[]{:S(2)}) collective-permute-start(bf16[512,896]{1,0:T(8,128)(2,1)S(1)} %collective-permute-done.22.refs_2_), channel_id=1, source_target_pairs={{0,16},{4,12},{8,24},{12,4},{16,0},{20,28},{24,8},{28,20},{1,17},{... | collective-permute-start | bytes 2752520 | tf_op jit(solution)/shard_map/ppermute | solution.py:80
  265.1 7.9 %collective-permute-start.30 = (bf16[512,896]{1,0:T(8,128)(2,1)S(1)}, bf16[512,896]{1,0:T(8,128)(2,1)S(1)}, u32[]{:S(2)}, u32[]{:S(2)}) collective-permute-start(bf16[512,896]{1,0:T(8,128)(2,1)S(1)} %collective-permute-done.22.refs_2_), channel_id=1, source_target_pairs={{0,4},{4,0},{8,12},{12,8},{16,20},{20,16},{24,28},{28,24},{1,5},{5... | collective-permute-start | bytes 2752520 | tf_op jit(solution)/shard_map/ppermute | solution.py:20
  265.5 7.6 %collective-permute-start.31 = (bf16[512,896]{1,0:T(8,128)(2,1)S(1)}, bf16[512,896]{1,0:T(8,128)(2,1)S(1)}, u32[]{:S(2)}, u32[]{:S(2)}) collective-permute-start(bf16[512,896]{1,0:T(8,128)(2,1)S(1)} %collective-permute-done.25.refs_3_), channel_id=1, source_target_pairs={{0,4},{4,0},{8,12},{12,8},{16,20},{20,16},{24,28},{28,24},{1,5},{5... | collective-permute-start | bytes 2752520 | tf_op jit(solution)/shard_map/ppermute | solution.py:20
  (28 other events, 334.9 us)

commit v4 on v3

--- a/solution.py
+++ b/solution.py
@@ -110,19 +110,17 @@
     a1, b1 = line_step(rows, rows)
     near = [by_core(block, x, y)]
     sibling = swap(block, "fsdp", 1)
-    half = columns.shape[1] // 2
-    first, second = exchange_columns(columns[:, :half]), columns[:, half:]
-    ((a1, b1, *near, sibling, first, second),) = together((a1, b1, *near, sibling, first, second))
+    short = everywhere(short)
+    ((a1, b1, *near, sibling, columns, short),) = together((a1, b1, *near, sibling, columns, short))
     near.append(by_core(sibling, x, y))
-    second = exchange_columns(second)
+    columns = exchange_columns(columns)
     a2, b2 = line_step(a1, b1)
-    ((a2, b2, *near, short, second),) = together((a2, b2, *near, short, second))
+    index = index_of(short)
+    (a2, b2, columns), near, index = together((a2, b2, columns), near, index)
     diagonal = by_core(near[0], y, x)
     a3, b3 = line_step(a2, b2)
     far = [swap(part, "fsdp", 1) for part in near]
-    columns = jnp.concatenate([first, second], axis=1)
-    index = index_of(everywhere(short))
-    (a3, b3, diagonal, columns), far, index = together((a3, b3, diagonal, columns), far, index)
+    (a3, b3, diagonal, columns), far = together((a3, b3, diagonal, columns), far)
     weights = in_pairs([block, sibling], near, far, [diagonal, swap(diagonal, "fsdp", 1)])
     return weights, [a1, a2, a3], [b1, b2, b3], index, columns
 
@@ -598,9 +596,9 @@
     out1, g1 = attend(place, segment_ids[0], cotangent, 1, after(arrived1, g0))
     ((s0, n0, g1),) = together((s0, n0, g1))
     m0, n1, d0 = by_core(s0, x, y), by_core(g1, x, y), by_core(n0, y, x)
+    packed = pack_columns(here, slots, spots, columns, [a1, a2, a3], [b1, b2, b3])
+    ((packed, m0, n0, n1, d0, g1),) = together((packed, m0, n0, n1, d0, g1))
     s1 = swap(g1, "fsdp", 1)
-    packed = pack_columns(here, slots, spots, columns, [a1, a2, a3], [b1, b2, b3])
-    ((packed, m0, n0, n1, d0, s1),) = together((packed, m0, n0, n1, d0, s1))
     m1, d1 = by_core(s1, x, y), by_core(n1, y, x)
     f0 = [swap(n0, "fsdp", 1), swap(m0, "fsdp", 1)]
     e0 = swap(d0, "fsdp", 1)

time: 285 us -> 276 us (0.968)
  waiting for transfers between devices: 95.8 us -> 134 us
  blocking collectives: 28.4 us -> 0 us
  starting transfers between devices: 52.7 us -> 40 us
    ppermute x6, waiting for transfers between devices: 8.07 us -> 50.8 us  [line_step(): lax.ppermute(a, ('fsdp', 'seq'), pairs(0))]
    all_to_all x1 -> x0, blocking collectives: 28.4 us -> none  [exchange_columns(): lax.all_to_all(blocks, 'fsdp', split_axis=0, concat_axis=0, tiled=True)]
    all_to_all x2, waiting for transfers between devices: 21.2 us -> 8.42 us  [on_device(): lax.all_to_all(x, 'fsdp', split_axis=0, concat_axis=0, tiled=True)]
    all_to_all x2, starting transfers between devices: 18.1 us -> 8.12 us  [on_device(): lax.all_to_all(x, 'fsdp', split_axis=0, concat_axis=0, tiled=True)]
    all_to_all x1, waiting for transfers between devices: 17.7 us -> 24.6 us  [everywhere(): lax.all_to_all(sent, ('fsdp', 'seq'), split_axis=0, concat_axis=0, tiled=...]
    ppermute x9, waiting for transfers between devices: 15.2 us -> 12 us  [by_core(): lax.ppermute(x, 'fsdp', [(i, i ^ (odd if i & 1 else even)) for i in range...]
    unnamed x52 -> x60, local copies, waits for them, and re-layouts: 9.72 us -> 9.95 us
  transfers between devices with their start and end apart: 37 -> 37, of which waited for: 15 -> 19; matrix products, arithmetic and copies ran while one was open for 6% -> 4% of each run, Pallas kernels for 26% -> 27%
where the time goes in v4:
time: 276 us; the launch traced here: 275 us
  waiting for transfers between devices  134 us (49%)
  Pallas kernels  80.7 us (29%)
  starting transfers between devices  40 us (14%)
  local copies, waits for them, and re-layouts  14.2 us (5%)
  other arithmetic  5.13 us (2%)
    ppermute x6, waiting for transfers between devices, line_step(): lax.ppermute(a, ('fsdp', 'seq'), pairs(0))  50.8 us
    all_to_all x1, waiting for transfers between devices, exchange_columns(): lax.all_to_all(blocks, 'fsdp', split_axis=0, concat_axis=0, tiled=True)  30.7 us
    pallas_call x3, Pallas kernels, gradients(): pl.pallas_call(functools.partial(grads_kernel, layout, group, adds, befor...  24.8 us
    all_to_all x1, waiting for transfers between devices, everywhere(): lax.all_to_all(sent, ('fsdp', 'seq'), split_axis=0, concat_axis=0, tiled=...  24.6 us
    pallas_call x2, Pallas kernels, project(): pl.pallas_call(functools.partial(project_kernel, n_seq, layout, cap, grou...  22.9 us
    pallas_call x1, Pallas kernels, pack_columns(): pl.pallas_call(functools.partial(pack_kernel, n_seq), grid=(packs,), out_...  17.2 us
    pallas_call x2, Pallas kernels, attend(): pl.pallas_call(functools.partial(attend_kernel, heads, 256, abreast), gri...  15.8 us
    ppermute x9, waiting for transfers between devices, by_core(): lax.ppermute(x, 'fsdp', [(i, i ^ (odd if i & 1 else even)) for i in range...  12 us
  transfers between devices with their start and end apart: 37, of which 19 were waited for; matrix products, arithmetic and copies ran while one was open for 4% of the time, Pallas kernels for 27%

profile of v4, /device:TPU:0, one launch (start us, length us, event | category | flops | bytes accessed | tf_op | source)
XLA Modules:
  0.0 275.4 jit_solution(17863504616856229127)
XLA Ops:
  4.2 3.0 %collective-permute-start.2 = (bf16[640,1792]{1,0:T(8,128)(2,1)S(1)}, bf16[640,1792]{1,0:T(8,128)(2,1)}, u32[]{:S(2)}, u32[]{:S(2)}) collective-permute-start(bf16[640,1792]{1,0:T(8,128)(2,1)S(1)} %slice_dynamic-update-slice_fusion.2.refs_7_), channel_id=1, source_target_pairs={{0,8},{4,20},{8,0},{12,28},{16,24},{20,4},{24,16},{28,12},{1,9},{5... | collective-permute-start | bytes 6881288 | tf_op jit(solution)/shard_map/ppermute | solution.py:80
  7.2 1.6 collective-permute-start
  9.4 5.4 %all-to-all-start = ((s32[32,1,128]{2,1,0:T(1,128)}), s32[32,1,128]{2,1,0:T(1,128)S(1)}, u32[]{:S(2)}, u32[]{:S(2)}) async-start(s32[32,1,128]{2,1,0:T(1,128)} %broadcast_in_dim.10), calls=%async_computation | async-start | bytes 32768 | tf_op jit(solution)/shard_map/all_to_all | solution.py:74
  14.8 2.4 copy.42
  17.2 24.6 %all-to-all-done = s32[32,1,128]{2,1,0:T(1,128)S(1)} async-done(((s32[32,1,128]{2,1,0:T(1,128)}), s32[32,1,128]{2,1,0:T(1,128)S(1)}, u32[]{:S(2)}, u32[]{:S(2)}) %all-to-all-start) | async-done | bytes 16416 | tf_op jit(solution)/shard_map/all_to_all | solution.py:74
  41.9 1.5 collective-permute-start.6
  44.0 4.3 %all-to-all-start.1 = ((bf16[8,640,128]{2,1,0:T(8,128)(2,1)}), bf16[8,640,128]{2,1,0:T(8,128)(2,1)}, u32[]{:S(2)}, u32[]{:S(2)}) async-start(bf16[8,640,128]{2,1,0:T(8,128)(2,1)} %bitcast.42), calls=%async_computation.1 | async-start | bytes 2621440 | tf_op jit(solution)/shard_map/all_to_all | solution.py:97
  49.1 1.6 select_reduce_fusion
  53.8 30.7 %all-to-all-done.1.refs_0_ = bf16[8,640,128]{2,1,0:T(8,128)(2,1)} async-done(((bf16[8,640,128]{2,1,0:T(8,128)(2,1)}), bf16[8,640,128]{2,1,0:T(8,128)(2,1)}, u32[]{:S(2)}, u32[]{:S(2)}) %all-to-all-start.1) | async-done | bytes 1310752 | tf_op jit(solution)/shard_map/all_to_all | solution.py:97
  87.0 29.3 %collective-permute-done.7.refs_3_ = bf16[128,5120]{1,0:T(8,128)(2,1)S(1)} collective-permute-done((bf16[128,5120]{1,0:T(8,128)(2,1)}, bf16[128,5120]{1,0:T(8,128)(2,1)S(1)}, u32[]{:S(2)}, u32[]{:S(2)}) %collective-permute-start.7) | collective-permute-done | bytes 1310752 | tf_op jit(solution)/shard_map/ppermute | solution.py:59
  119.4 1.5 collective-permute-start.12
  120.9 2.0 collective-permute-done.14.refs_14_
  122.9 11.4 %project.2 = bf16[1024,896]{1,0:T(8,128)(2,1)} custom-call(s32[2]{0:T(128)} %pad_add_fusion.1.me_ref, s32[1,512]{1,0:T(1,128)} %bitcast.47, bf16[128,5120]{1,0:T(8,128)(2,1)} %refs_0_.3, bf16[128,5120]{1,0:T(8,128)(2,1)} %collective-permute-done.refs_1_, bf16[128,5120]{1,0:T(8,128)(2,1)} %collective-permute-done.4.refs_2_, bf16[128,5120]{1,0:T(8,128)(2,1)} %copy-done.4, ...), custom_call_target="tpu_custom_call" | custom-call | flops 5637144576 | bytes 16252928 | tf_op jit(solution)/shard_map/project/pallas_call | solution.py:203
  134.3 3.8 %all-to-all-start.2 = ((bf16[8,128,896]{2,1,0:T(8,128)(2,1)}), bf16[8,128,896]{2,1,0:T(8,128)(2,1)S(1)}, u32[]{:S(2)}, u32[]{:S(2)}) async-start(bf16[8,128,896]{2,1,0:T(8,128)(2,1)} %bitcast.41), calls=%async_computation.2 | async-start | bytes 3670016 | tf_op jit(solution)/shard_map/all_to_all | solution.py:568
  138.1 11.8 %collective-permute-done.12.refs_1_ = bf16[8,640,128]{2,1,0:T(8,128)(2,1)} collective-permute-done((bf16[8,640,128]{2,1,0:T(8,128)(2,1)}, bf16[8,640,128]{2,1,0:T(8,128)(2,1)}, u32[]{:S(2)}, u32[]{:S(2)}) %collective-permute-start.12) | collective-permute-done | bytes 1310752 | tf_op jit(solution)/shard_map/ppermute | solution.py:59
  150.7 1.8 collective-permute-start.15
  152.4 11.4 %project.3 = bf16[1024,896]{1,0:T(8,128)(2,1)} custom-call(s32[2]{0:T(128)} %pad_add_fusion.1.me_ref, s32[1,512]{1,0:T(1,128)} %bitcast.48, bf16[128,5120]{1,0:T(8,128)(2,1)} %refs_0_.3, bf16[128,5120]{1,0:T(8,128)(2,1)} %collective-permute-done.refs_1_, bf16[128,5120]{1,0:T(8,128)(2,1)} %collective-permute-done.4.refs_2_, bf16[128,5120]{1,0:T(8,128)(2,1)} %copy-done.4, ...), custom_call_target="tpu_custom_call" | custom-call | flops 5637144576 | bytes 16252928 | tf_op jit(solution)/shard_map/project/pallas_call | solution.py:203
  163.9 4.3 %all-to-all-start.3 = ((bf16[8,128,896]{2,1,0:T(8,128)(2,1)}), bf16[8,128,896]{2,1,0:T(8,128)(2,1)}, u32[]{:S(2)}, u32[]{:S(2)}) async-start(bf16[8,128,896]{2,1,0:T(8,128)(2,1)} %bitcast.40), calls=%async_computation.3 | async-start | bytes 3670016 | tf_op jit(solution)/shard_map/all_to_all | solution.py:568
  169.1 7.9 %attend.2 = (bf16[512,640]{1,0:T(8,128)(2,1)}, bf16[512,896]{1,0:T(8,128)(2,1)}) custom-call(s32[1,1024]{1,0:T(1,128)} %reshape.143.place_ref, s32[1,512]{1,0:T(1,128)} %seg_row.3, s32[512,1]{1,0:T(8,128)} %copy.47.seg_col, bf16[512,1280]{1,0:T(8,128)(2,1)} %cot_ref.3, bf16[1024,896]{1,0:T(8,128)(2,1)} %bitcast.43), custom_call_target="tpu_custom_call" | custom-call | flops 2952790016 | bytes 4587520 | tf_op jit(solution)/shard_map/attend/pallas_call | solution.py:304
  177.0 3.6 %collective-permute-done.15.refs_2_ = bf16[8,640,128]{2,1,0:T(8,128)(2,1)S(1)} collective-permute-done((bf16[8,640,128]{2,1,0:T(8,128)(2,1)}, bf16[8,640,128]{2,1,0:T(8,128)(2,1)S(1)}, u32[]{:S(2)}, u32[]{:S(2)}) %collective-permute-start.15) | collective-permute-done | bytes 1310752 | tf_op jit(solution)/shard_map/ppermute | solution.py:59
  181.4 1.7 collective-permute-start.17
  183.8 8.4 %all-to-all-done.3 = bf16[8,128,896]{2,1,0:T(8,128)(2,1)} async-done(((bf16[8,128,896]{2,1,0:T(8,128)(2,1)}), bf16[8,128,896]{2,1,0:T(8,128)(2,1)}, u32[]{:S(2)}, u32[]{:S(2)}) %all-to-all-start.3) | async-done | bytes 1835040 | tf_op jit(solution)/shard_map/all_to_all | solution.py:568
  192.2 7.9 %attend.3 = (bf16[512,640]{1,0:T(8,128)(2,1)}, bf16[512,896]{1,0:T(8,128)(2,1)}) custom-call(s32[1,1024]{1,0:T(1,128)} %reshape.143.place_ref, s32[1,512]{1,0:T(1,128)} %seg_row.3, s32[512,1]{1,0:T(8,128)} %copy.47.seg_col, bf16[512,1280]{1,0:T(8,128)(2,1)} %cot_ref.3, bf16[1024,896]{1,0:T(8,128)(2,1)} %bitcast.13.in_ref), custom_call_target="tpu_custom_call" | custom-call | flops 2952790016 | bytes 4587520 | tf_op jit(solution)/shard_map/attend/pallas_call | solution.py:304
  201.4 1.7 collective-permute-start.22
  203.1 1.5 collective-permute-start.23
  204.6 6.0 %collective-permute-done.17.refs_3_ = bf16[8,640,128]{2,1,0:T(8,128)(2,1)S(1)} collective-permute-done((bf16[8,640,128]{2,1,0:T(8,128)(2,1)S(1)}, bf16[8,640,128]{2,1,0:T(8,128)(2,1)S(1)}, u32[]{:S(2)}, u32[]{:S(2)}) %collective-permute-start.17) | collective-permute-done | bytes 1310752 | tf_op jit(solution)/shard_map/ppermute | solution.py:59
  211.6 17.2 %pack_columns.1.packed_ref = bf16[640,4096]{1,0:T(8,128)(2,1)} custom-call(s32[2]{0:T(128)} %pad_add_fusion.1.me_ref, s32[8,512]{1,0:T(8,128)} %reshape.144.slot_ref, s32[8,1024]{1,0:T(8,128)} %reshape.145.spot_ref, bf16[8,640,128]{2,1,0:T(8,128)(2,1)} %all-to-all-done.1.refs_0_, bf16[8,640,128]{2,1,0:T(8,128)(2,1)} %collective-permute-done.12.refs_1_, ...), custom_call_target="tpu_custom_call" | custom-call | flops 10737418240 | bytes 10485760 | tf_op jit(solution)/shard_map/pack_columns/pallas_call | solution.py:380
  228.9 5.4 %collective-permute-done.22.refs_2_ = bf16[512,896]{1,0:T(8,128)(2,1)S(1)} collective-permute-done((bf16[512,896]{1,0:T(8,128)(2,1)}, bf16[512,896]{1,0:T(8,128)(2,1)S(1)}, u32[]{:S(2)}, u32[]{:S(2)}) %collective-permute-start.22) | collective-permute-done | bytes 917536 | tf_op jit(solution)/shard_map/ppermute | solution.py:80
  242.0 10.1 %gradients.3 = (f32[640,1280]{1,0:T(8,128)}, f32[640,256]{1,0:T(8,128)}, f32[640,256]{1,0:T(8,128)}) custom-call(s32[2]{0:T(128)} %pad_add_fusion.1.me_ref, bf16[640,4096]{1,0:T(8,128)(2,1)} %pack_columns.1.packed_ref, bf16[512,896]{1,0:T(8,128)(2,1)} %get-tuple-element.90.refs_0_, bf16[512,896]{1,0:T(8,128)(2,1)} %collective-permute-done.19.refs_1_, ...), custom_call_target="tpu_custom_call" | custom-call | flops 4697620480 | bytes 14876672 | tf_op jit(solution)/shard_map/gradients/pallas_call | solution.py:483
  252.1 5.4 %collective-permute-done.26.refs_2_ = bf16[512,896]{1,0:T(8,128)(2,1)S(1)} collective-permute-done((bf16[512,896]{1,0:T(8,128)(2,1)S(1)}, bf16[512,896]{1,0:T(8,128)(2,1)S(1)}, u32[]{:S(2)}, u32[]{:S(2)}) %collective-permute-start.26) | collective-permute-done | bytes 917536 | tf_op jit(solution)/shard_map/ppermute | solution.py:80
  259.0 7.0 %gradients.4 = (f32[640,1280]{1,0:T(8,128)}, f32[640,256]{1,0:T(8,128)}, f32[640,256]{1,0:T(8,128)}) custom-call(s32[2]{0:T(128)} %pad_add_fusion.1.me_ref, bf16[640,4096]{1,0:T(8,128)(2,1)} %pack_columns.1.packed_ref, bf16[512,896]{1,0:T(8,128)(2,1)} %get-tuple-element.96.refs_0_, ...), custom_call_target="tpu_custom_call", output_to_operand_aliasing={{0}: (6, {}), {1}: (7, {}), {2}: (8, {})} | custom-call | flops 2348810240 | bytes 8585216 | tf_op jit(solution)/shard_map/gradients/pallas_call | solution.py:483
  267.6 7.6 %gradients.5 = (f32[640,1280]{1,0:T(8,128)}, f32[640,256]{1,0:T(8,128)}, f32[640,256]{1,0:T(8,128)}) custom-call(s32[2]{0:T(128)} %pad_add_fusion.1.me_ref, bf16[640,4096]{1,0:T(8,128)(2,1)} %pack_columns.1.packed_ref, bf16[512,896]{1,0:T(8,128)(2,1)} %copy-done.13, ...), custom_call_target="tpu_custom_call", output_to_operand_aliasing={{0}: (6, {}), {1}: (7, {}), {2}: (8, {})} | custom-call | flops 2348810240 | bytes 8585216 | tf_op jit(solution)/shard_map/gradients/pallas_call | solution.py:483
  (138 shorter events, 30.2 us)
Async XLA Ops:
  4.2 37.6 %collective-permute-start.2 = (bf16[640,1792]{1,0:T(8,128)(2,1)S(1)}, bf16[640,1792]{1,0:T(8,128)(2,1)}, u32[]{:S(2)}, u32[]{:S(2)}) collective-permute-start(bf16[640,1792]{1,0:T(8,128)(2,1)S(1)} %slice_dynamic-update-slice_fusion.2.refs_7_), channel_id=1, source_target_pairs={{0,8},{4,20},{8,0},{12,28},{16,24},{20,4},{24,16},{28,12},{1,9},{5... | collective-permute-start | bytes 6881288 | tf_op jit(solution)/shard_map/ppermute | solution.py:80
  7.2 34.6 %collective-permute-start.3 = (bf16[640,1792]{1,0:T(8,128)(2,1)S(1)}, bf16[640,1792]{1,0:T(8,128)(2,1)}, u32[]{:S(2)}, u32[]{:S(2)}) collective-permute-start(bf16[640,1792]{1,0:T(8,128)(2,1)S(1)} %slice_dynamic-update-slice_fusion.2.refs_7_), channel_id=1, source_target_pairs={{0,4},{4,0},{8,12},{12,8},{16,20},{20,16},{24,28},{28,24},{1,5},{5... | collective-permute-start | bytes 6881288 | tf_op jit(solution)/shard_map/ppermute | solution.py:20
  7.2 34.6 %collective-permute-start = (bf16[128,5120]{1,0:T(8,128)(2,1)}, bf16[128,5120]{1,0:T(8,128)(2,1)}, u32[]{:S(2)}, u32[]{:S(2)}) collective-permute-start(bf16[128,5120]{1,0:T(8,128)(2,1)} %refs_0_.3), channel_id=1, source_target_pairs={{0,1},{1,2},{2,3},{3,7},{4,0},{5,4},{6,5},{7,6},{8,9},{9,10},{10,1... | collective-permute-start | bytes 3932168 | tf_op jit(solution)/shard_map/ppermute | solution.py:59
  8.8 33.0 %collective-permute-start.1 = (bf16[128,5120]{1,0:T(8,128)(2,1)}, bf16[128,5120]{1,0:T(8,128)(2,1)}, u32[]{:S(2)}, u32[]{:S(2)}) collective-permute-start(bf16[128,5120]{1,0:T(8,128)(2,1)} %refs_0_.3), channel_id=1, source_target_pairs={{0,4},{1,0},{2,1},{3,2},{4,5},{5,6},{6,7},{7,3},{8,12},{9,8},{10,9... | collective-permute-start | bytes 3932168 | tf_op jit(solution)/shard_map/ppermute | solution.py:59
  9.4 32.4 %all-to-all-start = ((s32[32,1,128]{2,1,0:T(1,128)}), s32[32,1,128]{2,1,0:T(1,128)S(1)}, u32[]{:S(2)}, u32[]{:S(2)}) async-start(s32[32,1,128]{2,1,0:T(1,128)} %broadcast_in_dim.10), calls=%async_computation | async-start | bytes 32768 | tf_op jit(solution)/shard_map/all_to_all | solution.py:74
  41.9 42.6 %collective-permute-start.6 = (bf16[640,1792]{1,0:T(8,128)(2,1)}, bf16[640,1792]{1,0:T(8,128)(2,1)}, u32[]{:S(2)}, u32[]{:S(2)}) collective-permute-start(bf16[640,1792]{1,0:T(8,128)(2,1)} %collective-permute-done.3.refs_8_), channel_id=1, source_target_pairs={{0,8},{4,20},{8,0},{12,28},{16,24},{20,4},{24,16},{28,12},{1,9},{5... | collective-permute-start | bytes 6881288 | tf_op jit(solution)/shard_map/ppermute | solution.py:80
  43.4 41.0 %collective-permute-start.4 = (bf16[128,5120]{1,0:T(8,128)(2,1)}, bf16[128,5120]{1,0:T(8,128)(2,1)}, u32[]{:S(2)}, u32[]{:S(2)}) collective-permute-start(bf16[128,5120]{1,0:T(8,128)(2,1)} %collective-permute-done.refs_1_), channel_id=1, source_target_pairs={{0,1},{1,2},{2,3},{3,7},{4,0},{5,4},{6,5},{7,6},{8,9},{9,10},{10,1... | collective-permute-start | bytes 3932168 | tf_op jit(solution)/shard_map/ppermute | solution.py:59
  43.9 40.5 %collective-permute-start.5 = (bf16[128,5120]{1,0:T(8,128)(2,1)}, bf16[128,5120]{1,0:T(8,128)(2,1)}, u32[]{:S(2)}, u32[]{:S(2)}) collective-permute-start(bf16[128,5120]{1,0:T(8,128)(2,1)} %collective-permute-done.1.refs_4_), channel_id=1, source_target_pairs={{0,4},{1,0},{2,1},{3,2},{4,5},{5,6},{6,7},{7,3},{8,12},{9,8},{10,9... | collective-permute-start | bytes 3932168 | tf_op jit(solution)/shard_map/ppermute | solution.py:59
  44.0 40.5 %all-to-all-start.1 = ((bf16[8,640,128]{2,1,0:T(8,128)(2,1)}), bf16[8,640,128]{2,1,0:T(8,128)(2,1)}, u32[]{:S(2)}, u32[]{:S(2)}) async-start(bf16[8,640,128]{2,1,0:T(8,128)(2,1)} %bitcast.42), calls=%async_computation.1 | async-start | bytes 2621440 | tf_op jit(solution)/shard_map/all_to_all | solution.py:97
  84.5 32.8 %collective-permute-start.10 = (bf16[640,1792]{1,0:T(8,128)(2,1)}, bf16[640,1792]{1,0:T(8,128)(2,1)S(1)}, u32[]{:S(2)}, u32[]{:S(2)}) collective-permute-start(bf16[640,1792]{1,0:T(8,128)(2,1)} %collective-permute-done.2.refs_9_), channel_id=1, source_target_pairs={{0,4},{4,0},{8,12},{12,8},{16,20},{20,16},{24,28},{28,24},{1,5},{5... | collective-permute-start | bytes 6881288 | tf_op jit(solution)/shard_map/ppermute | solution.py:20
  84.6 32.7 %collective-permute-start.11 = (bf16[640,1792]{1,0:T(8,128)(2,1)}, bf16[640,1792]{1,0:T(8,128)(2,1)S(1)}, u32[]{:S(2)}, u32[]{:S(2)}) collective-permute-start(bf16[640,1792]{1,0:T(8,128)(2,1)} %collective-permute-done.6.refs_10_), channel_id=1, source_target_pairs={{0,4},{4,0},{8,12},{12,8},{16,20},{20,16},{24,28},{28,24},{1,5},{5... | collective-permute-start | bytes 6881288 | tf_op jit(solution)/shard_map/ppermute | solution.py:20
  85.1 32.2 %collective-permute-start.9 = (bf16[640,1792]{1,0:T(8,128)(2,1)}, bf16[640,1792]{1,0:T(8,128)(2,1)S(1)}, u32[]{:S(2)}, u32[]{:S(2)}) collective-permute-start(bf16[640,1792]{1,0:T(8,128)(2,1)} %collective-permute-done.2.refs_9_), channel_id=1, source_target_pairs={{0,16},{4,12},{8,24},{12,4},{16,0},{20,28},{24,8},{28,20},{1,17},{... | collective-permute-start | bytes 6881288 | tf_op jit(solution)/shard_map/ppermute | solution.py:80
  86.5 29.8 %collective-permute-start.7 = (bf16[128,5120]{1,0:T(8,128)(2,1)}, bf16[128,5120]{1,0:T(8,128)(2,1)S(1)}, u32[]{:S(2)}, u32[]{:S(2)}) collective-permute-start(bf16[128,5120]{1,0:T(8,128)(2,1)} %collective-permute-done.4.refs_2_), channel_id=1, source_target_pairs={{0,1},{1,2},{2,3},{3,7},{4,0},{5,4},{6,5},{7,6},{8,9},{9,10},{10,1... | collective-permute-start | bytes 3932168 | tf_op jit(solution)/shard_map/ppermute | solution.py:59
  87.0 30.3 %collective-permute-start.8 = (bf16[128,5120]{1,0:T(8,128)(2,1)}, bf16[128,5120]{1,0:T(8,128)(2,1)S(1)}, u32[]{:S(2)}, u32[]{:S(2)}) collective-permute-start(bf16[128,5120]{1,0:T(8,128)(2,1)} %collective-permute-done.5.refs_5_), channel_id=1, source_target_pairs={{0,4},{1,0},{2,1},{3,2},{4,5},{5,6},{6,7},{7,3},{8,12},{9,8},{10,9... | collective-permute-start | bytes 3932168 | tf_op jit(solution)/shard_map/ppermute | solution.py:59
  119.4 30.6 %collective-permute-start.12 = (bf16[8,640,128]{2,1,0:T(8,128)(2,1)}, bf16[8,640,128]{2,1,0:T(8,128)(2,1)}, u32[]{:S(2)}, u32[]{:S(2)}) collective-permute-start(bf16[8,640,128]{2,1,0:T(8,128)(2,1)} %all-to-all-done.1.refs_0_), channel_id=1, source_target_pairs={{0,1},{1,2},{2,3},{3,7},{4,0},{5,4},{6,5},{7,6},{8,9},{9,10},{10,1... | collective-permute-start | bytes 3932168 | tf_op jit(solution)/shard_map/ppermute | solution.py:59
  120.9 29.8 %collective-permute-start.13 = (bf16[8,640,128]{2,1,0:T(8,128)(2,1)}, bf16[8,640,128]{2,1,0:T(8,128)(2,1)}, u32[]{:S(2)}, u32[]{:S(2)}) collective-permute-start(bf16[8,640,128]{2,1,0:T(8,128)(2,1)} %all-to-all-done.1.refs_0_), channel_id=1, source_target_pairs={{0,4},{1,0},{2,1},{3,2},{4,5},{5,6},{6,7},{7,3},{8,12},{9,8},{10,9... | collective-permute-start | bytes 3932168 | tf_op jit(solution)/shard_map/ppermute | solution.py:59
  134.3 29.5 %all-to-all-start.2 = ((bf16[8,128,896]{2,1,0:T(8,128)(2,1)}), bf16[8,128,896]{2,1,0:T(8,128)(2,1)S(1)}, u32[]{:S(2)}, u32[]{:S(2)}) async-start(bf16[8,128,896]{2,1,0:T(8,128)(2,1)} %bitcast.41), calls=%async_computation.2 | async-start | bytes 3670016 | tf_op jit(solution)/shard_map/all_to_all | solution.py:568
  150.7 30.0 %collective-permute-start.15 = (bf16[8,640,128]{2,1,0:T(8,128)(2,1)}, bf16[8,640,128]{2,1,0:T(8,128)(2,1)S(1)}, u32[]{:S(2)}, u32[]{:S(2)}) collective-permute-start(bf16[8,640,128]{2,1,0:T(8,128)(2,1)} %collective-permute-done.12.refs_1_), channel_id=1, source_target_pairs={{0,1},{1,2},{2,3},{3,7},{4,0},{5,4},{6,5},{7,6},{8,9},{9,10},{10,1... | collective-permute-start | bytes 3932168 | tf_op jit(solution)/shard_map/ppermute | solution.py:59
  152.4 29.0 %collective-permute-start.16 = (bf16[8,640,128]{2,1,0:T(8,128)(2,1)}, bf16[8,640,128]{2,1,0:T(8,128)(2,1)}, u32[]{:S(2)}, u32[]{:S(2)}) collective-permute-start(bf16[8,640,128]{2,1,0:T(8,128)(2,1)} %collective-permute-done.13.refs_4_), channel_id=1, source_target_pairs={{0,4},{1,0},{2,1},{3,2},{4,5},{5,6},{6,7},{7,3},{8,12},{9,8},{10,9... | collective-permute-start | bytes 3932168 | tf_op jit(solution)/shard_map/ppermute | solution.py:59
  163.9 28.3 %all-to-all-start.3 = ((bf16[8,128,896]{2,1,0:T(8,128)(2,1)}), bf16[8,128,896]{2,1,0:T(8,128)(2,1)}, u32[]{:S(2)}, u32[]{:S(2)}) async-start(bf16[8,128,896]{2,1,0:T(8,128)(2,1)} %bitcast.40), calls=%async_computation.3 | async-start | bytes 3670016 | tf_op jit(solution)/shard_map/all_to_all | solution.py:568
  181.4 29.2 %collective-permute-start.17 = (bf16[8,640,128]{2,1,0:T(8,128)(2,1)S(1)}, bf16[8,640,128]{2,1,0:T(8,128)(2,1)S(1)}, u32[]{:S(2)}, u32[]{:S(2)}) collective-permute-start(bf16[8,640,128]{2,1,0:T(8,128)(2,1)S(1)} %collective-permute-done.15.refs_2_), channel_id=1, source_target_pairs={{0,1},{1,2},{2,3},{3,7},{4,0},{5,4},{6,5},{7,6},{8,9},{9,10},{10,1... | collective-permute-start | bytes 3932168 | tf_op jit(solution)/shard_map/ppermute | solution.py:59
  183.1 28.1 %collective-permute-start.18 = (bf16[8,640,128]{2,1,0:T(8,128)(2,1)}, bf16[8,640,128]{2,1,0:T(8,128)(2,1)}, u32[]{:S(2)}, u32[]{:S(2)}) collective-permute-start(bf16[8,640,128]{2,1,0:T(8,128)(2,1)} %collective-permute-done.16.refs_5_), channel_id=1, source_target_pairs={{0,4},{1,0},{2,1},{3,2},{4,5},{5,6},{6,7},{7,3},{8,12},{9,8},{10,9... | collective-permute-start | bytes 3932168 | tf_op jit(solution)/shard_map/ppermute | solution.py:59
  183.1 17.0 %collective-permute-start.19 = (bf16[512,896]{1,0:T(8,128)(2,1)}, bf16[512,896]{1,0:T(8,128)(2,1)}, u32[]{:S(2)}, u32[]{:S(2)}) collective-permute-start(bf16[512,896]{1,0:T(8,128)(2,1)} %get-tuple-element.90.refs_0_), channel_id=1, source_target_pairs={{0,4},{4,0},{8,12},{12,8},{16,20},{20,16},{24,28},{28,24},{1,5},{5... | collective-permute-start | bytes 2752520 | tf_op jit(solution)/shard_map/ppermute | solution.py:20
  183.1 17.9 %collective-permute-start.20 = (bf16[512,896]{1,0:T(8,128)(2,1)}, bf16[512,896]{1,0:T(8,128)(2,1)}, u32[]{:S(2)}, u32[]{:S(2)}) collective-permute-start(bf16[512,896]{1,0:T(8,128)(2,1)} %get-tuple-element.90.refs_0_), channel_id=1, source_target_pairs={{0,8},{4,20},{8,0},{12,28},{16,24},{20,4},{24,16},{28,12},{1,9},{5... | collective-permute-start | bytes 2752520 | tf_op jit(solution)/shard_map/ppermute | solution.py:80
  201.0 27.9 %collective-permute-start.21 = (bf16[512,896]{1,0:T(8,128)(2,1)}, bf16[512,896]{1,0:T(8,128)(2,1)}, u32[]{:S(2)}, u32[]{:S(2)}) collective-permute-start(bf16[512,896]{1,0:T(8,128)(2,1)} %collective-permute-done.19.refs_1_), channel_id=1, source_target_pairs={{0,8},{4,20},{8,0},{12,28},{16,24},{20,4},{24,16},{28,12},{1,9},{5... | collective-permute-start | bytes 2752520 | tf_op jit(solution)/shard_map/ppermute | solution.py:80
  201.4 32.9 %collective-permute-start.22 = (bf16[512,896]{1,0:T(8,128)(2,1)}, bf16[512,896]{1,0:T(8,128)(2,1)S(1)}, u32[]{:S(2)}, u32[]{:S(2)}) collective-permute-start(bf16[512,896]{1,0:T(8,128)(2,1)} %get-tuple-element.96.refs_0_), channel_id=1, source_target_pairs={{0,8},{4,20},{8,0},{12,28},{16,24},{20,4},{24,16},{28,12},{1,9},{5... | collective-permute-start | bytes 2752520 | tf_op jit(solution)/shard_map/ppermute | solution.py:80
  203.1 31.2 %collective-permute-start.23 = (bf16[512,896]{1,0:T(8,128)(2,1)}, bf16[512,896]{1,0:T(8,128)(2,1)}, u32[]{:S(2)}, u32[]{:S(2)}) collective-permute-start(bf16[512,896]{1,0:T(8,128)(2,1)} %collective-permute-done.20.refs_2_), channel_id=1, source_target_pairs={{0,16},{4,12},{8,24},{12,4},{16,0},{20,28},{24,8},{28,20},{1,17},{... | collective-permute-start | bytes 2752520 | tf_op jit(solution)/shard_map/ppermute | solution.py:80
  235.4 22.1 %collective-permute-start.26 = (bf16[512,896]{1,0:T(8,128)(2,1)S(1)}, bf16[512,896]{1,0:T(8,128)(2,1)S(1)}, u32[]{:S(2)}, u32[]{:S(2)}) collective-permute-start(bf16[512,896]{1,0:T(8,128)(2,1)S(1)} %collective-permute-done.22.refs_2_), channel_id=1, source_target_pairs={{0,16},{4,12},{8,24},{12,4},{16,0},{20,28},{24,8},{28,20},{1,17},{... | collective-permute-start | bytes 2752520 | tf_op jit(solution)/shard_map/ppermute | solution.py:80
  237.4 20.4 %collective-permute-start.25 = (bf16[512,896]{1,0:T(8,128)(2,1)S(1)}, bf16[512,896]{1,0:T(8,128)(2,1)S(1)}, u32[]{:S(2)}, u32[]{:S(2)}) collective-permute-start(bf16[512,896]{1,0:T(8,128)(2,1)S(1)} %collective-permute-done.24.refs_1_), channel_id=1, source_target_pairs={{0,8},{4,20},{8,0},{12,28},{16,24},{20,4},{24,16},{28,12},{1,9},{5... | collective-permute-start | bytes 2752520 | tf_op jit(solution)/shard_map/ppermute | solution.py:80
  257.7 8.3 %collective-permute-start.30 = (bf16[512,896]{1,0:T(8,128)(2,1)S(1)}, bf16[512,896]{1,0:T(8,128)(2,1)S(1)}, u32[]{:S(2)}, u32[]{:S(2)}) collective-permute-start(bf16[512,896]{1,0:T(8,128)(2,1)S(1)} %collective-permute-done.22.refs_2_), channel_id=1, source_target_pairs={{0,4},{4,0},{8,12},{12,8},{16,20},{20,16},{24,28},{28,24},{1,5},{5... | collective-permute-start | bytes 2752520 | tf_op jit(solution)/shard_map/ppermute | solution.py:20
  258.5 7.6 %collective-permute-start.31 = (bf16[512,896]{1,0:T(8,128)(2,1)S(1)}, bf16[512,896]{1,0:T(8,128)(2,1)S(1)}, u32[]{:S(2)}, u32[]{:S(2)}) collective-permute-start(bf16[512,896]{1,0:T(8,128)(2,1)S(1)} %collective-permute-done.25.refs_3_), channel_id=1, source_target_pairs={{0,4},{4,0},{8,12},{12,8},{16,20},{20,16},{24,28},{28,24},{1,5},{5... | collective-permute-start | bytes 2752520 | tf_op jit(solution)/shard_map/ppermute | solution.py:20
  258.5 7.5 %collective-permute-start.32 = (bf16[512,896]{1,0:T(8,128)(2,1)S(1)}, bf16[512,896]{1,0:T(8,128)(2,1)S(1)}, u32[]{:S(2)}, u32[]{:S(2)}) collective-permute-start(bf16[512,896]{1,0:T(8,128)(2,1)S(1)} %collective-permute-done.26.refs_2_), channel_id=1, source_target_pairs={{0,4},{4,0},{8,12},{12,8},{16,20},{20,16},{24,28},{28,24},{1,5},{5... | collective-permute-start | bytes 2752520 | tf_op jit(solution)/shard_map/ppermute | solution.py:20
  (32 other events, 297.1 us)
